TPU v7x, 256 devices: a whole 4x4x8 slice. The times are simulated.
256 devices in a mesh: width: 8 (over y, core), hidden: 32 (over x, z).
Axes of the slice: x: 4, y: 4, z: 8, core: 2. Of those that a mesh axis runs over, the one named last changes fastest.
Arguments:
- start_latent: float32 [512, 6144], P(None, 'width'), may hold values from -6 to 6
- target_one: float32 [512, 6144], P(None, 'width'), may hold values from -6 to 6
- target_two: float32 [512, 6144], P(None, 'width'), may hold values from -6 to 6
- w_up: bfloat16 [6144, 24576], P('width', 'hidden'), may hold values from -0.078125 to 0.078125
- w_down: bfloat16 [24576, 6144], P('hidden', 'width'), may hold values from -0.0390625 to 0.0390625
Outputs:
- grad_start: float32 [512, 6144], P('hidden', 'width')
- grad_up: float32 [6144, 24576], P('width', 'hidden')
- grad_down: float32 [24576, 6144], P('hidden', 'width')
All inputs are finite; a program needn't handle non-finite values.
Results may differ from a plain program's by a relative error of at most 0.018.
Values may be sent and summed in bfloat16 or wider, within the bound.
No kernel may reach another device: no remote copies, remote signals or barrier semaphores. Data moves between devices by JAX's collectives and lax.ppermute only.
A program may use at most 64 MiB of HBM per device.

v0:
```python
import math

import jax
import jax.numpy as jnp
from jax import lax
from jax.sharding import PartitionSpec as P

gelu_scale = math.sqrt(2.0 / math.pi)
cubic_coef = 0.044715


def gelu_parts(preact):
    inner = gelu_scale * (preact + cubic_coef * preact * preact * preact)
    tangent = jnp.tanh(inner)
    value_out = 0.5 * preact * (1.0 + tangent)
    slope_out = 0.5 * (1.0 + tangent) + 0.5 * preact * (1.0 - tangent * tangent) * gelu_scale * (
        1.0 + 3.0 * cubic_coef * preact * preact
    )
    return (value_out, slope_out)


def width_reduce(left_mat, project):
    own_share = lax.psum_scatter(
        project(left_mat).astype(jnp.bfloat16), "width", scatter_dimension=0, tiled=True
    )
    return lax.all_gather(own_share, "width", axis=0, tiled=True)


def across_hidden(partial_sum, added_term):
    share_rows = partial_sum.shape[0] // lax.axis_size("hidden")
    own_first = lax.axis_index("hidden") * share_rows
    summed = added_term + lax.psum(partial_sum, "hidden")
    return (summed.astype(jnp.bfloat16), lax.dynamic_slice_in_dim(summed, own_first, share_rows, 0))


def shards(start_latent, target_one, target_two, w_up, w_down):

    def up_project(piece_rows):
        return jnp.dot(piece_rows, w_up, preferred_element_type=jnp.float32)

    def down_back(piece_rows):
        return jnp.einsum("rd,hd->rh", piece_rows, w_down, preferred_element_type=jnp.float32)

    input_zero = start_latent.astype(jnp.bfloat16)
    pre_zero = width_reduce(input_zero, up_project)
    gelu_zero, slope_zero = gelu_parts(pre_zero.astype(jnp.float32))
    act_zero = gelu_zero.astype(jnp.bfloat16)
    down_zero = jnp.dot(act_zero, w_down, preferred_element_type=jnp.float32)
    input_one, unused_rows = across_hidden(down_zero, start_latent)
    pre_one = width_reduce(input_one, up_project)
    gelu_one, slope_one = gelu_parts(pre_one.astype(jnp.float32))
    act_one = gelu_one.astype(jnp.bfloat16)
    error_two = target_two.astype(jnp.bfloat16)
    back_one = width_reduce(error_two, down_back)
    inner_one = (back_one.astype(jnp.float32) * slope_one).astype(jnp.bfloat16)
    spread_one = jnp.einsum("rh,dh->rd", inner_one, w_up, preferred_element_type=jnp.float32)
    error_one, grad_one_rows = across_hidden(spread_one, target_one + target_two)
    back_zero = width_reduce(error_one, down_back)
    inner_zero = (back_zero.astype(jnp.float32) * slope_zero).astype(jnp.bfloat16)
    spread_zero = jnp.einsum("rh,dh->rd", inner_zero, w_up, preferred_element_type=jnp.float32)
    grad_start = grad_one_rows + lax.psum_scatter(
        spread_zero, "hidden", scatter_dimension=0, tiled=True
    )
    grad_up = jnp.einsum("rd,rh->dh", input_zero, inner_zero, preferred_element_type=jnp.float32)
    grad_up = grad_up + jnp.einsum(
        "rd,rh->dh", input_one, inner_one, preferred_element_type=jnp.float32
    )
    grad_down = jnp.einsum("rh,rd->hd", act_zero, error_one, preferred_element_type=jnp.float32)
    grad_down = grad_down + jnp.einsum(
        "rh,rd->hd", act_one, error_two, preferred_element_type=jnp.float32
    )
    return (grad_start, grad_up, grad_down)


def solution(mesh):
    return jax.shard_map(
        shards,
        mesh=mesh,
        in_specs=(
            P(None, "width"),
            P(None, "width"),
            P(None, "width"),
            P("width", "hidden"),
            P("hidden", "width"),
        ),
        out_specs=(P("hidden", "width"), P("width", "hidden"), P("hidden", "width")),
        check_vma=False,
    )
```

profile of v0, /device:TPU:1, one launch (start us, length us, event | category | flops | bytes accessed | tf_op | source)
XLA Modules:
  0.0 731.7 jit_solution(3406488193409347981)
XLA Ops:
  7.2 0.0 copy-start
  7.2 0.0 reduce-scatter.8.cloned.1.call-start
  7.2 1.2 copy-done
  8.4 3.1 convolution_convert_fusion.2
  11.5 0.0 reduce-scatter.8.cloned.1.call-update
  11.5 0.0 all-reduce.3.cloned.1.call-start
  11.6 35.4 %reduce-scatter.8.cloned.1.call-done = bf16[64,768]{1,0:T(8,128)(2,1)} async-done(((bf16[512,768]{1,0:T(8,128)(2,1)}), bf16[64,768]{1,0:T(8,128)(2,1)}) %reduce-scatter.8.cloned.1.call-update) | async-done | bytes 98320 | tf_op jit(solution)/shard_map/reduce_scatter | solution.py:23
  47.0 16.6 %all_gather.13 = bf16[512,768]{1,0:T(8,128)(2,1)S(1)} all-gather(bf16[64,768]{1,0:T(8,128)(2,1)} %reduce-scatter.8.cloned.1.call-done), channel_id=1, replica_groups=mesh['width'=8,'hidden'=32] {'width'}, dimensions={0}, use_global_device_ids=true | all-gather | bytes 884736 | tf_op jit(solution)/shard_map/all_gather | solution.py:26
  63.6 0.9 copy-done.4
  64.5 3.5 fusion.40
  68.0 0.0 all-reduce.3.cloned.1.call-update
  68.0 0.0 reduce-scatter.6.cloned.1.call-start
  68.1 1.3 copy-done.1
  69.4 3.0 convolution_convert_fusion.3
  72.4 0.0 reduce-scatter.6.cloned.1.call-update
  72.4 0.0 reduce-scatter.10.cloned.1.call-start
  72.4 142.5 %all-reduce.3.cloned.1.call-done = f32[512,768]{1,0:T(8,128)} async-done(((f32[512,768]{1,0:T(8,128)}), f32[512,768]{1,0:T(8,128)}) %all-reduce.3.cloned.1.call-update) | async-done | bytes 1572880 | tf_op jit(solution)/shard_map/psum | solution.py:32
  214.9 2.0 add_convert_fusion
  217.0 0.9 copy-done.9
  217.8 1.7 convolution_convert_fusion.1
  219.5 0.0 reduce-scatter.10.cloned.1.call-update
  219.5 0.0 all-reduce.5.cloned.1.call-start
  219.6 30.5 %reduce-scatter.6.cloned.1.call-done = bf16[64,768]{1,0:T(8,128)(2,1)} async-done(((bf16[512,768]{1,0:T(8,128)(2,1)}), bf16[64,768]{1,0:T(8,128)(2,1)}) %reduce-scatter.6.cloned.1.call-update) | async-done | bytes 98320 | tf_op jit(solution)/shard_map/reduce_scatter | solution.py:23
  250.1 17.6 %all_gather.12 = bf16[512,768]{1,0:T(8,128)(2,1)} all-gather(bf16[64,768]{1,0:T(8,128)(2,1)} %reduce-scatter.6.cloned.1.call-done), channel_id=1, replica_groups=mesh['width'=8,'hidden'=32] {'width'}, dimensions={0}, use_global_device_ids=true | all-gather | bytes 884736 | tf_op jit(solution)/shard_map/all_gather | solution.py:26
  267.7 18.3 %reduce-scatter.10.cloned.1.call-done = bf16[64,768]{1,0:T(8,128)(2,1)} async-done(((bf16[512,768]{1,0:T(8,128)(2,1)}), bf16[64,768]{1,0:T(8,128)(2,1)}) %reduce-scatter.10.cloned.1.call-update) | async-done | bytes 98320 | tf_op jit(solution)/shard_map/reduce_scatter | solution.py:23
  286.0 16.6 %all_gather.14 = bf16[512,768]{1,0:T(8,128)(2,1)S(1)} all-gather(bf16[64,768]{1,0:T(8,128)(2,1)} %reduce-scatter.10.cloned.1.call-done), channel_id=1, replica_groups=mesh['width'=8,'hidden'=32] {'width'}, dimensions={0}, use_global_device_ids=true | all-gather | bytes 884736 | tf_op jit(solution)/shard_map/all_gather | solution.py:26
  302.6 4.0 fusion.46
  306.6 0.0 all-reduce.5.cloned.1.call-update
  306.6 0.0 reduce-scatter.12.cloned.1.call-start
  306.6 146.8 %all-reduce.5.cloned.1.call-done = f32[512,768]{1,0:T(8,128)} async-done(((f32[512,768]{1,0:T(8,128)}), f32[512,768]{1,0:T(8,128)}) %all-reduce.5.cloned.1.call-update) | async-done | bytes 1572880 | tf_op jit(solution)/shard_map/psum | solution.py:32
  453.4 2.3 add_add_fusion
  455.7 1.1 copy-done.2
  456.8 1.7 convolution_convert_fusion
  458.5 0.0 reduce-scatter.12.cloned.1.call-update
  458.6 0.0 reduce-scatter.14.cloned.1.call-start
  458.6 32.7 %reduce-scatter.12.cloned.1.call-done = bf16[64,768]{1,0:T(8,128)(2,1)} async-done(((bf16[512,768]{1,0:T(8,128)(2,1)}), bf16[64,768]{1,0:T(8,128)(2,1)}) %reduce-scatter.12.cloned.1.call-update) | async-done | bytes 98320 | tf_op jit(solution)/shard_map/reduce_scatter | solution.py:23
  491.3 16.7 %all_gather.15 = bf16[512,768]{1,0:T(8,128)(2,1)S(1)} all-gather(bf16[64,768]{1,0:T(8,128)(2,1)} %reduce-scatter.12.cloned.1.call-done), channel_id=1, replica_groups=mesh['width'=8,'hidden'=32] {'width'}, dimensions={0}, use_global_device_ids=true | all-gather | bytes 884736 | tf_op jit(solution)/shard_map/all_gather | solution.py:26
  508.1 0.9 copy-done.7
  509.0 4.0 fusion.43
  513.0 0.0 reduce-scatter.14.cloned.1.call-update
  513.0 2.8 fusion.27
  515.8 0.0 copy-start.5
  515.8 2.6 convolution_add_fusion
  518.4 1.7 fusion.30
  520.1 3.1 bitcast_add_fusion
  523.1 3.0 copy.9
  526.2 197.2 %reduce-scatter.14.cloned.1.call-done = f32[16,768]{1,0:T(8,128)} async-done(((f32[512,768]{1,0:T(8,128)}), f32[16,768]{1,0:T(8,128)}) %reduce-scatter.14.cloned.1.call-update) | async-done | bytes 49168 | tf_op jit(solution)/shard_map/reduce_scatter | solution.py:61
  723.4 1.4 dynamic-slice_add_fusion
  (16 shorter events, 0.0 us)
Async XLA Ops:
  7.2 1.3 copy-start
  7.2 39.9 %reduce-scatter.8.cloned.1.call-start = ((), (), s32[]{:S(2)}) async-start(), calls=%async_computation.6 | async-start | bytes 884736 | tf_op jit(solution)/shard_map/reduce_scatter | solution.py:23
  11.5 203.4 %all-reduce.3.cloned.1.call-start = ((), (), s32[]{:S(2)}) async-start(), calls=%async_computation.7 | async-start | bytes 3145728 | tf_op jit(solution)/shard_map/psum | solution.py:32
  63.6 0.9 copy-start.4
  68.0 1.4 copy-start.1
  68.0 182.1 %reduce-scatter.6.cloned.1.call-start = ((), (), s32[]{:S(2)}) async-start(), calls=%async_computation.5 | async-start | bytes 884736 | tf_op jit(solution)/shard_map/reduce_scatter | solution.py:23
  72.4 213.6 %reduce-scatter.10.cloned.1.call-start = ((), (), s32[]{:S(2)}) async-start(), calls=%async_computation.8 | async-start | bytes 884736 | tf_op jit(solution)/shard_map/reduce_scatter | solution.py:23
  217.0 0.9 copy-start.9
  219.5 233.9 %all-reduce.5.cloned.1.call-start = ((), (), s32[]{:S(2)}) async-start(), calls=%async_computation.9 | async-start | bytes 3145728 | tf_op jit(solution)/shard_map/psum | solution.py:32
  306.6 184.7 %reduce-scatter.12.cloned.1.call-start = ((), (), s32[]{:S(2)}) async-start(), calls=%async_computation.10 | async-start | bytes 884736 | tf_op jit(solution)/shard_map/reduce_scatter | solution.py:23
  453.4 3.4 copy-start.11
  455.7 1.1 copy-start.2
  458.6 264.8 %reduce-scatter.14.cloned.1.call-start = ((), (), s32[]{:S(2)}) async-start(), calls=%async_computation.11 | async-start | bytes 1622016 | tf_op jit(solution)/shard_map/reduce_scatter | solution.py:61
  508.1 0.9 copy-start.7
  515.8 2.6 copy-start.3
  515.8 2.6 copy-start.5
  515.8 2.6 copy-start.8
  518.4 1.7 copy-start.6
  518.4 1.7 copy-start.10
Sparse Core Ops, SparseCore 0:
  11.7 35.3 reduce-scatter.7
  68.1 146.7 all-reduce.2
  217.5 32.5 reduce-scatter.5
  253.2 32.7 reduce-scatter.9
  306.7 146.6 all-reduce.4
  458.7 32.6 reduce-scatter.11
  513.1 210.2 reduce-scatter.13
where the time goes:
time: 736 us; the launch traced here: 732 us
  waiting for transfers between devices  604 us (82%)
  blocking collectives  67.5 us (9%)
  matrix products  31 us (4%)
  between operations  14.2 us (2%)
  local copies, waits for them, and re-layouts  9.39 us (1%)
    psum x2, waiting for transfers between devices, across_hidden(): summed = added_term + lax.psum(partial_sum, 'hidden')  289 us
    reduce_scatter x1, waiting for transfers between devices, shards(): lax.psum_scatter(spread_zero, 'hidden', scatter_dimension=0, tiled=True)  197 us
    reduce_scatter x4, waiting for transfers between devices, width_reduce(): lax.psum_scatter(project(left_mat).astype(jnp.bfloat16), 'width', scatter...  117 us
    all_gather x4, blocking collectives, width_reduce(): return lax.all_gather(own_share, 'width', axis=0, tiled=True)  67.5 us
  transfers between devices with their start and end apart: 7, of which 7 were waited for; matrix products, arithmetic and copies ran while one was open for 3% of the time, Pallas kernels for 0%

commit v1 on v0

v1 whole, which is shorter than its diff:
```python
import math

import jax
import jax.numpy as jnp
from jax import lax
from jax.sharding import Mesh, PartitionSpec as P

gelu_scale = math.sqrt(2.0 / math.pi)
cubic_coef = 0.044715
f32 = jnp.float32
bf16 = jnp.bfloat16
SIZES = {"y": 4, "core": 2, "x": 4, "z": 8}
HIDDEN = ("x", "z")


def gelu_parts(preact):
    inner = gelu_scale * (preact + cubic_coef * preact * preact * preact)
    tangent = jnp.tanh(inner)
    value_out = 0.5 * preact * (1.0 + tangent)
    slope_out = 0.5 * (1.0 + tangent) + 0.5 * preact * (1.0 - tangent * tangent) * gelu_scale * (
        1.0 + 3.0 * cubic_coef * preact * preact
    )
    return (value_out, slope_out)


def swap(block):
    return lax.ppermute(block, "core", [(0, 1), (1, 0)])


def scatter_sum(parts, axes):
    landed = lax.all_to_all(parts, axes, 0, 0, tiled=True)
    return jnp.sum(landed.astype(f32), axis=0)


def spread(block, axes, count):
    copies = jnp.broadcast_to(block[None], (count,) + block.shape)
    return lax.all_to_all(copies, axes, 0, 0, tiled=True)


def dot(a, b):
    return jnp.dot(a, b, preferred_element_type=f32)


def dot_t(a, b):
    return lax.dot_general(a, b, (((1,), (1,)), ((), ())), preferred_element_type=f32)


def t_dot(a, b):
    return lax.dot_general(a, b, (((0,), (0,)), ((), ())), preferred_element_type=f32)


def shards(start_latent, target_one, target_two, w_up, w_down):
    n_y = SIZES["y"]
    n_h = SIZES["x"] * SIZES["z"]
    rows, wide = start_latent.shape
    deep = w_up.shape[1]
    eight = rows // (2 * n_h)
    half = rows // 2
    core = lax.axis_index("core")
    place = lax.axis_index("x") * SIZES["z"] + lax.axis_index("z")

    def halves(full):
        cut = full.reshape(n_h, 2, eight, wide)
        own = lax.dynamic_index_in_dim(cut, core, 1, keepdims=False)
        other = lax.dynamic_index_in_dim(cut, 1 - core, 1, keepdims=False)
        return own, other

    def own_rows(full):
        own, other = halves(full)
        mine = lax.dynamic_index_in_dim(own, place, 0, keepdims=False)
        theirs = lax.dynamic_index_in_dim(other, place, 0, keepdims=False)
        return jnp.concatenate([mine, swap(theirs)], axis=1)

    start_own, start_other = halves(start_latent)
    start_own = start_own.astype(bf16).reshape(half, wide)
    start_other = start_other.astype(bf16).reshape(half, wide)
    pre_other = dot(start_other, w_up).astype(bf16)
    pre_own = dot(start_own, w_up)
    pre_part = (pre_own + swap(pre_other).astype(f32)).astype(bf16)
    pre_zero = scatter_sum(pre_part.reshape(n_y, half // n_y, deep), "y").astype(bf16)
    gelu_zero, slope_zero = gelu_parts(pre_zero.astype(f32))
    act_zero = spread(gelu_zero.astype(bf16), "y", n_y).reshape(half, deep)

    up_wide = jnp.concatenate([w_up, swap(w_up)], axis=0)
    down_wide = jnp.concatenate([w_down, swap(w_down)], axis=1)

    down_part = dot(act_zero, down_wide).astype(bf16)
    latent_one = own_rows(start_latent) + scatter_sum(down_part.reshape(n_h, eight, 2 * wide), HIDDEN)
    input_one = spread(latent_one.astype(bf16), HIDDEN, n_h).reshape(half, 2 * wide)

    two_own, two_other = halves(target_two)
    two_own = two_own.astype(bf16).reshape(half, wide)
    two_other = two_other.astype(bf16).reshape(half, wide)
    back_other = dot_t(two_other, w_down).astype(bf16)
    back_own = dot_t(two_own, w_down)
    back_part = (back_own + swap(back_other).astype(f32)).astype(bf16)

    pre_part = dot(input_one, up_wide).astype(bf16)
    both = jnp.concatenate(
        [pre_part.reshape(n_y, half // n_y, deep), back_part.reshape(n_y, half // n_y, deep)], axis=2
    )
    both = scatter_sum(both, "y")
    pre_one = both[:, :deep].astype(bf16)
    back_one = both[:, deep:].astype(bf16)
    gelu_one, slope_one = gelu_parts(pre_one.astype(f32))
    act_one_part = gelu_one.astype(bf16)
    inner_one = (back_one.astype(f32) * slope_one).astype(bf16)
    inner_one = spread(inner_one, "y", n_y).reshape(half, deep)

    spread_part = dot_t(inner_one, up_wide).astype(bf16)
    targets = own_rows(target_one + target_two)
    grad_one = targets + scatter_sum(spread_part.reshape(n_h, eight, 2 * wide), HIDDEN)
    error_one = spread(grad_one.astype(bf16), HIDDEN, n_h).reshape(half, 2 * wide)
    grad_one_other = swap(grad_one[:, wide:])

    back_part = dot_t(error_one, down_wide).astype(bf16)
    back_zero = scatter_sum(back_part.reshape(n_y, half // n_y, deep), "y").astype(bf16)
    inner_zero = (back_zero.astype(f32) * slope_zero).astype(bf16)
    inner_zero = spread(inner_zero, "y", n_y).reshape(half, deep)
    inner_zero_other = swap(inner_zero)

    part_own = dot_t(inner_zero, w_up).astype(bf16).reshape(n_h, eight, wide)
    part_other = dot_t(inner_zero_other, w_up).astype(bf16).reshape(n_h, eight, wide)
    summed = scatter_sum(jnp.concatenate([part_own, part_other], axis=1), HIDDEN)
    grad_start = summed + jnp.concatenate([grad_one[:, :wide], grad_one_other], axis=0)
    grad_start = jnp.where(core == 0, grad_start, jnp.roll(grad_start, eight, axis=0))

    act_zero_other = swap(act_zero)
    act_one = lax.all_gather(act_one_part, "y", axis=0, tiled=True)
    act_one_other = swap(act_one)
    inner_one_other = swap(inner_one)
    input_one_other = swap(input_one[:, wide:])
    error_one_other = swap(error_one[:, wide:])

    grad_up = t_dot(
        jnp.concatenate([start_own, start_other, input_one[:, :wide], input_one_other], axis=0),
        jnp.concatenate([inner_zero, inner_zero_other, inner_one, inner_one_other], axis=0),
    )
    grad_down = t_dot(
        jnp.concatenate([act_zero, act_zero_other, act_one, act_one_other], axis=0),
        jnp.concatenate([error_one[:, :wide], error_one_other, two_own, two_other], axis=0),
    )
    return (grad_start, grad_up, grad_down)


def solution(mesh):
    fine = Mesh(
        mesh.devices.reshape(tuple(SIZES.values())), tuple(SIZES)
    )
    width, hidden = ("y", "core"), HIDDEN
    return jax.shard_map(
        shards,
        mesh=fine,
        in_specs=(
            P(None, width),
            P(None, width),
            P(None, width),
            P(width, hidden),
            P(hidden, width),
        ),
        out_specs=(P(hidden, width), P(width, hidden), P(hidden, width)),
        check_vma=False,
    )
```

time: 736 us -> 226 us (0.31)
  waiting for transfers between devices: 604 us -> 30 us
  starting transfers between devices: 0.29 us -> 70.2 us
  between operations: 14.2 us -> 1.04 us
  blocking collectives: 67.5 us -> 80.5 us
  matrix products: 31 us -> 23.6 us
    reduce_scatter x5 -> x0, waiting for transfers between devices: 314 us -> none  [the longest x1 197 us: shards(): lax.psum_scatter(spread_zero, 'hidden', scatter_dimension=0, tiled=True)]
    psum x2 -> x0, waiting for transfers between devices: 289 us -> none  [across_hidden(): summed = added_term + lax.psum(partial_sum, 'hidden')]
    all_to_all x0 -> x6, blocking collectives: none -> 70.2 us  [the longest x3 40.8 us: spread(): return lax.all_to_all(copies, axes, 0, 0, tiled=True)]
    all_gather x4 -> x1, blocking collectives: 67.5 us -> 10.2 us  [shards(): act_one = lax.all_gather(act_one_part, 'y', axis=0, tiled=True)]
    all_to_all x0 -> x5, starting transfers between devices: none -> 35.3 us  [the longest x3 23.2 us: scatter_sum(): landed = lax.all_to_all(parts, axes, 0, 0, tiled=True)]
    ppermute x0 -> x13, starting transfers between devices: none -> 34.9 us  [swap(): return lax.ppermute(block, 'core', [(0, 1), (1, 0)])]
    all_to_all x0 -> x5, waiting for transfers between devices: none -> 26.9 us  [the longest x3 18.2 us: scatter_sum(): landed = lax.all_to_all(parts, axes, 0, 0, tiled=True)]
    dot_general x11 -> x12, matrix products: 31 us -> 23.6 us  [the longest x6 8.91 us: dot_t(): lax.dot_general(a, b, (((1,), (1,)), ((), ())), preferred_element_type=f32)]
  transfers between devices with their start and end apart: 7 -> 18, of which waited for: 7 -> 8; matrix products, arithmetic and copies ran while one was open for 3% -> 11% of each run, Pallas kernels for 0% -> 0%
where the time goes in v1:
time: 226 us; the launch traced here: 225 us
  blocking collectives  80.5 us (36%)
  starting transfers between devices  70.2 us (31%)
  waiting for transfers between devices  30 us (13%)
  matrix products  23.6 us (10%)
  local copies, waits for them, and re-layouts  13.2 us (6%)
  other arithmetic  6.64 us (3%)
    all_to_all x3, blocking collectives, spread(): return lax.all_to_all(copies, axes, 0, 0, tiled=True)  40.8 us
    ppermute x13, starting transfers between devices, swap(): return lax.ppermute(block, 'core', [(0, 1), (1, 0)])  34.9 us
    all_to_all x3, blocking collectives, scatter_sum(): landed = lax.all_to_all(parts, axes, 0, 0, tiled=True)  29.4 us
    all_to_all x3, starting transfers between devices, scatter_sum(): landed = lax.all_to_all(parts, axes, 0, 0, tiled=True)  23.2 us
    all_to_all x3, waiting for transfers between devices, scatter_sum(): landed = lax.all_to_all(parts, axes, 0, 0, tiled=True)  18.2 us
    all_to_all x2, starting transfers between devices, spread(): return lax.all_to_all(copies, axes, 0, 0, tiled=True)  12 us
    all_gather x1, blocking collectives, shards(): act_one = lax.all_gather(act_one_part, 'y', axis=0, tiled=True)  10.2 us
    dot_general x6, matrix products, dot_t(): lax.dot_general(a, b, (((1,), (1,)), ((), ())), preferred_element_type=f32)  8.91 us
  transfers between devices with their start and end apart: 18, of which 8 were waited for; matrix products, arithmetic and copies ran while one was open for 11% of the time, Pallas kernels for 0%

profile of v1, /device:TPU:1, one launch (start us, length us, event | category | flops | bytes accessed | tf_op | source)
XLA Modules:
  0.0 225.2 jit_solution(12718045867899873616)
XLA Ops:
  0.7 1.6 fusion.35
  2.9 3.3 %collective-permute-start.2 = (bf16[256,768]{1,0:T(8,128)(2,1)S(1)}, bf16[256,768]{1,0:T(8,128)(2,1)S(1)}, u32[]{:S(2)}, u32[]{:S(2)}) collective-permute-start(bf16[256,768]{1,0:T(8,128)(2,1)S(1)} %convolution_convert_fusion.7), channel_id=1, source_target_pairs={{0,32},{32,0},{1,33},{33,1},{2,34},{34,2},{3,35},{35,3},{4,36},{36... | collective-permute-start | bytes 1179656 | tf_op jit(solution)/shard_map/ppermute | solution.py:27
  6.3 1.2 collective-permute-done.2
  8.0 10.1 %all_to_all.55 = bf16[4,64,768]{2,1,0:T(8,128)(2,1)S(1)} all-to-all(bf16[4,64,768]{2,1,0:T(8,128)(2,1)S(1)} %bitcast.63), channel_id=1, replica_groups=mesh['y'=4,'core'=2,'x'=4,'z'=8] {'y'}, dimensions={0} | all-to-all | bytes 786432 | tf_op jit(solution)/shard_map/all_to_all | solution.py:31
  18.3 0.8 broadcast_in_dim.10
  19.0 3.5 %all-to-all-start.1 = ((bf16[4,64,768]{2,1,0:T(8,128)(2,1)}), bf16[4,64,768]{2,1,0:T(8,128)(2,1)S(1)}, u32[]{:S(2)}, u32[]{:S(2)}) async-start(bf16[4,64,768]{2,1,0:T(8,128)(2,1)} %broadcast_in_dim.10), calls=%async_computation.1 | async-start | bytes 786432 | tf_op jit(solution)/shard_map/all_to_all | solution.py:37
  22.5 1.1 constant_dynamic-update-slice_fusion.1
  23.6 2.4 %constant_dynamic-update-slice_fusion = bf16[768,1536]{1,0:T(8,128)(2,1)} fusion(bf16[768,1536]{1,0:T(8,128)(2,1)} %constant_dynamic-update-slice_fusion.1, bf16[768,768]{1,0:T(8,128)(2,1)} %collective-permute-done.3), kind=kLoop, calls=%fused_computation.102 | loop fusion | bytes 2359296 | tf_op jit(solution)/shard_map/concatenate | solution.py:85
  25.9 3.0 %all-to-all-done.1 = bf16[4,64,768]{2,1,0:T(8,128)(2,1)S(1)} async-done(((bf16[4,64,768]{2,1,0:T(8,128)(2,1)}), bf16[4,64,768]{2,1,0:T(8,128)(2,1)S(1)}, u32[]{:S(2)}, u32[]{:S(2)}) %all-to-all-start.1) | async-done | bytes 393248 | tf_op jit(solution)/shard_map/all_to_all | solution.py:37
  28.9 3.5 %fusion = bf16[32,8,1536]{2,1,0:T(8,128)(2,1)} fusion(bf16[256,768]{1,0:T(8,128)(2,1)S(1)} %bitcast.69, bf16[768,1536]{1,0:T(8,128)(2,1)} %constant_dynamic-update-slice_fusion), kind=kOutput, calls=%fused_computation.2 | convolution fusion | flops 604372992 | bytes 3538944 | tf_op jit(solution)/shard_map/dot_general | solution.py:41
  32.4 10.2 %all-to-all-start.2 = ((bf16[32,8,1536]{2,1,0:T(8,128)(2,1)}), bf16[32,8,1536]{2,1,0:T(8,128)(2,1)S(1)}, u32[]{:S(2)}, u32[]{:S(2)}) async-start(bf16[32,8,1536]{2,1,0:T(8,128)(2,1)} %fusion), calls=%async_computation.2 | async-start | bytes 1572864 | tf_op jit(solution)/shard_map/all_to_all | solution.py:31
  42.6 0.8 dynamic-slice_bitcast_fusion.1
  43.4 3.2 %collective-permute-start.1 = (f32[8,768]{1,0:T(8,128)S(1)}, f32[8,768]{1,0:T(8,128)S(1)}, u32[]{:S(2)}, u32[]{:S(2)}) collective-permute-start(f32[8,768]{1,0:T(8,128)S(1)} %get-tuple-element.8), channel_id=1, source_target_pairs={{0,32},{32,0},{1,33},{33,1},{2,34},{34,2},{3,35},{35,3},{4,36},{36... | collective-permute-start | bytes 73736 | tf_op jit(solution)/shard_map/ppermute | solution.py:27
  46.6 12.5 %all-to-all-done.2 = bf16[32,8,1536]{2,1,0:T(8,128)(2,1)S(1)} async-done(((bf16[32,8,1536]{2,1,0:T(8,128)(2,1)}), bf16[32,8,1536]{2,1,0:T(8,128)(2,1)S(1)}, u32[]{:S(2)}, u32[]{:S(2)}) %all-to-all-start.2) | async-done | bytes 786464 | tf_op jit(solution)/shard_map/all_to_all | solution.py:31
  59.3 1.0 broadcast_in_dim.11
  60.2 8.6 %all-to-all-start.3 = ((bf16[32,8,1536]{2,1,0:T(8,128)(2,1)}), bf16[32,8,1536]{2,1,0:T(8,128)(2,1)S(1)}, u32[]{:S(2)}, u32[]{:S(2)}) async-start(bf16[32,8,1536]{2,1,0:T(8,128)(2,1)} %broadcast_in_dim.11), calls=%async_computation.3 | async-start | bytes 1572864 | tf_op jit(solution)/shard_map/all_to_all | solution.py:37
  68.8 4.0 %collective-permute-start.4 = (bf16[768,768]{1,0:T(8,128)(2,1)S(1)}, bf16[768,768]{1,0:T(8,128)(2,1)S(1)}, u32[]{:S(2)}, u32[]{:S(2)}) collective-permute-start(bf16[768,768]{1,0:T(8,128)(2,1)S(1)} %copy-done), channel_id=1, source_target_pairs={{0,32},{32,0},{1,33},{33,1},{2,34},{34,2},{3,35},{35,3},{4,36},{36... | collective-permute-start | bytes 3538952 | tf_op jit(solution)/shard_map/ppermute | solution.py:27
  72.9 1.4 fusion.37
  74.3 0.7 copy-done.9
  75.7 1.1 constant_dynamic-update-slice_fusion.3
  77.9 1.1 constant_dynamic-update-slice_fusion.2
  79.0 5.8 %all-to-all-done.3 = bf16[32,8,1536]{2,1,0:T(8,128)(2,1)S(1)} async-done(((bf16[32,8,1536]{2,1,0:T(8,128)(2,1)}), bf16[32,8,1536]{2,1,0:T(8,128)(2,1)S(1)}, u32[]{:S(2)}, u32[]{:S(2)}) %all-to-all-start.3) | async-done | bytes 786464 | tf_op jit(solution)/shard_map/all_to_all | solution.py:37
  84.8 2.4 %convolution_convert_fusion.6 = bf16[256,768]{1,0:T(8,128)(2,1)S(1)} fusion(bf16[1536,768]{1,0:T(8,128)(2,1)} %constant_dynamic-update-slice_fusion.2, bf16[32,8,1536]{2,1,0:T(8,128)(2,1)S(1)} %all-to-all-done.3), kind=kOutput, calls=%fused_computation.41 | convolution fusion | flops 604176384 | bytes 3538944 | tf_op jit(solution)/shard_map/dot_general | solution.py:41
  87.3 10.7 %all_to_all.56 = bf16[4,64,1536]{2,1,0:T(8,128)(2,1)S(1)} all-to-all(bf16[4,64,1536]{2,1,0:T(8,128)(2,1)S(1)} %pad_maximum_fusion), channel_id=1, replica_groups=mesh['y'=4,'core'=2,'x'=4,'z'=8] {'y'}, dimensions={0} | all-to-all | bytes 1572864 | tf_op jit(solution)/shard_map/all_to_all | solution.py:31
  98.1 0.8 fusion.47
  99.0 9.6 %all_to_all.57 = bf16[4,64,768]{2,1,0:T(8,128)(2,1)S(1)} all-to-all(bf16[4,64,768]{2,1,0:T(8,128)(2,1)S(1)} %broadcast_in_dim.12), channel_id=1, replica_groups=mesh['y'=4,'core'=2,'x'=4,'z'=8] {'y'}, dimensions={0} | all-to-all | bytes 786432 | tf_op jit(solution)/shard_map/all_to_all | solution.py:37
  108.6 0.7 copy-done.15
  109.4 3.4 %fusion.1 = bf16[32,8,1536]{2,1,0:T(8,128)(2,1)} fusion(bf16[256,768]{1,0:T(8,128)(2,1)S(1)} %bitcast.72, bf16[1536,768]{1,0:T(8,128)(2,1)} %constant_dynamic-update-slice_fusion.2), kind=kOutput, calls=%fused_computation.3 | convolution fusion | flops 604372992 | bytes 3538944 | tf_op jit(solution)/shard_map/dot_general | solution.py:45
  112.8 7.6 %all-to-all-start.6 = ((bf16[32,8,1536]{2,1,0:T(8,128)(2,1)}), bf16[32,8,1536]{2,1,0:T(8,128)(2,1)}, u32[]{:S(2)}, u32[]{:S(2)}) async-start(bf16[32,8,1536]{2,1,0:T(8,128)(2,1)} %fusion.1), calls=%async_computation.6 | async-start | bytes 1572864 | tf_op jit(solution)/shard_map/all_to_all | solution.py:31
  120.4 1.6 add.114
  122.0 7.5 %collective-permute-start = (f32[8,768]{1,0:T(8,128)S(1)}, f32[8,768]{1,0:T(8,128)S(1)}, u32[]{:S(2)}, u32[]{:S(2)}) collective-permute-start(f32[8,768]{1,0:T(8,128)S(1)} %get-tuple-element.6), channel_id=1, source_target_pairs={{0,32},{32,0},{1,33},{33,1},{2,34},{34,2},{3,35},{35,3},{4,36},{36... | collective-permute-start | bytes 73736 | tf_op jit(solution)/shard_map/ppermute | solution.py:27
  129.5 5.7 %all-to-all-done.6 = bf16[32,8,1536]{2,1,0:T(8,128)(2,1)} async-done(((bf16[32,8,1536]{2,1,0:T(8,128)(2,1)}), bf16[32,8,1536]{2,1,0:T(8,128)(2,1)}, u32[]{:S(2)}, u32[]{:S(2)}) %all-to-all-start.6) | async-done | bytes 786464 | tf_op jit(solution)/shard_map/all_to_all | solution.py:31
  135.2 1.3 convert_reduce_fusion.1
  136.5 0.6 fusion.65
  137.1 21.5 %all_to_all.58 = bf16[32,8,1536]{2,1,0:T(8,128)(2,1)S(1)} all-to-all(bf16[32,8,1536]{2,1,0:T(8,128)(2,1)S(1)} %broadcast_in_dim.13), channel_id=1, replica_groups=mesh['y'=4,'core'=2,'x'=4,'z'=8] {'x','z'}, dimensions={0} | all-to-all | bytes 1572864 | tf_op jit(solution)/shard_map/all_to_all | solution.py:37
  158.7 2.5 %convolution_convert_fusion.4 = bf16[256,768]{1,0:T(8,128)(2,1)S(1)} fusion(bf16[768,1536]{1,0:T(8,128)(2,1)} %constant_dynamic-update-slice_fusion, bf16[32,8,1536]{2,1,0:T(8,128)(2,1)S(1)} %all_to_all.58), kind=kOutput, calls=%fused_computation.39 | convolution fusion | flops 604176384 | bytes 3538944 | tf_op jit(solution)/shard_map/dot_general | solution.py:45
  161.2 8.6 %all_to_all.59 = bf16[4,64,768]{2,1,0:T(8,128)(2,1)S(1)} all-to-all(bf16[4,64,768]{2,1,0:T(8,128)(2,1)S(1)} %bitcast.75), channel_id=1, replica_groups=mesh['y'=4,'core'=2,'x'=4,'z'=8] {'y'}, dimensions={0} | all-to-all | bytes 786432 | tf_op jit(solution)/shard_map/all_to_all | solution.py:31
  170.1 9.6 %all_to_all.60 = bf16[4,64,768]{2,1,0:T(8,128)(2,1)S(1)} all-to-all(bf16[4,64,768]{2,1,0:T(8,128)(2,1)S(1)} %broadcast_in_dim.14), channel_id=1, replica_groups=mesh['y'=4,'core'=2,'x'=4,'z'=8] {'y'}, dimensions={0} | all-to-all | bytes 786432 | tf_op jit(solution)/shard_map/all_to_all | solution.py:37
  179.7 11.8 %collective-permute-start.6 = (bf16[256,768]{1,0:T(8,128)(2,1)S(1)}, bf16[256,768]{1,0:T(8,128)(2,1)}, u32[]{:S(2)}, u32[]{:S(2)}) collective-permute-start(bf16[256,768]{1,0:T(8,128)(2,1)S(1)} %bitcast.64), channel_id=1, source_target_pairs={{0,32},{32,0},{1,33},{33,1},{2,34},{34,2},{3,35},{35,3},{4,36},{36... | collective-permute-start | bytes 1179656 | tf_op jit(solution)/shard_map/ppermute | solution.py:27
  192.1 1.0 collective-permute-done.6
  193.0 1.5 fusion.33
  194.6 1.0 pad_maximum_fusion.1
  195.5 5.4 %all-to-all-start.10 = ((bf16[32,16,768]{2,1,0:T(8,128)(2,1)}), bf16[32,16,768]{2,1,0:T(8,128)(2,1)S(1)}, u32[]{:S(2)}, u32[]{:S(2)}) async-start(bf16[32,16,768]{2,1,0:T(8,128)(2,1)} %pad_maximum_fusion.1), calls=%async_computation.10 | async-start | bytes 1572864 | tf_op jit(solution)/shard_map/all_to_all | solution.py:31
  200.9 10.2 %all_gather.3 = bf16[256,768]{1,0:T(8,128)(2,1)S(1)} all-gather(bf16[64,768]{1,0:T(8,128)(2,1)S(1)} %copy-done.17), channel_id=1, replica_groups=mesh['y'=4,'core'=2,'x'=4,'z'=8] {'y'}, dimensions={0}, use_global_device_ids=true | all-gather | bytes 491520 | tf_op jit(solution)/shard_map/all_gather | solution.py:129
  211.2 3.5 %collective-permute-start.11 = (bf16[256,768]{1,0:T(8,128)(2,1)S(1)}, bf16[256,768]{1,0:T(8,128)(2,1)S(1)}, u32[]{:S(2)}, u32[]{:S(2)}) collective-permute-start(bf16[256,768]{1,0:T(8,128)(2,1)S(1)} %all_gather.3), channel_id=1, source_target_pairs={{0,32},{32,0},{1,33},{33,1},{2,34},{34,2},{3,35},{35,3},{4,36},{36... | collective-permute-start | bytes 1179656 | tf_op jit(solution)/shard_map/ppermute | solution.py:27
  216.5 3.9 %fusion.17 = f32[768,768]{1,0:T(8,128)} fusion(bf16[256,768]{1,0:T(8,128)(2,1)S(1)} %collective-permute-done.11, bf16[256,768]{1,0:T(8,128)(2,1)S(1)} %all_gather.3, bf16[256,768]{1,0:T(8,128)(2,1)} %collective-permute-done.10, bf16[256,768]{1,0:T(8,128)(2,1)S(1)} %bitcast.71, bf16[256,768]{1,0:T(8,128)(2,1)S(1)} %copy-done.10, ...), kind=kOutput, calls=%fused_computation.19 | convolution fusion | flops 1220542464 | bytes 5505024 | tf_op jit(solution)/shard_map/dot_general | solution.py:49
  220.5 3.9 %fusion.2 = f32[768,768]{1,0:T(8,128)} fusion(bf16[256,768]{1,0:T(8,128)(2,1)S(1)} %collective-permute-done.8, bf16[256,768]{1,0:T(8,128)(2,1)S(1)} %get-tuple-element.15, bf16[256,768]{1,0:T(8,128)(2,1)S(1)} %copy-done.8, bf16[256,768]{1,0:T(8,128)(2,1)S(1)} %copy-done.4, bf16[256,768]{1,0:T(8,128)(2,1)S(1)} %collective-permute-done.9, ...), kind=kOutput, calls=%fused_computation.4 | convolution fusion | flops 1220542464 | bytes 5505024 | tf_op jit(solution)/shard_map/dot_general | solution.py:49
  224.5 0.6 maximum_select_fusion
  (78 shorter events, 6.2 us)
Async XLA Ops:
  0.6 1.7 copy-start
  0.6 5.5 %copy-start.1 = (bf16[768,768]{1,0:T(8,128)(2,1)S(1)}, bf16[768,768]{1,0:T(8,128)(2,1)}, u32[]{:S(2)}) copy-start(bf16[768,768]{1,0:T(8,128)(2,1)} %param.9) | copy-start | bytes 3538948
  2.3 5.8 %copy-start.3 = (bf16[256,768]{1,0:T(8,128)(2,1)}, bf16[256,768]{1,0:T(8,128)(2,1)S(1)}, u32[]{:S(2)}) copy-start(bf16[256,768]{1,0:T(8,128)(2,1)S(1)} %get-tuple-element.12) | copy-start | bytes 1179652
  2.3 5.8 %copy-start.7 = (bf16[256,768]{1,0:T(8,128)(2,1)}, bf16[256,768]{1,0:T(8,128)(2,1)S(1)}, u32[]{:S(2)}) copy-start(bf16[256,768]{1,0:T(8,128)(2,1)S(1)} %get-tuple-element.11) | copy-start | bytes 1179652
  2.9 4.7 %collective-permute-start.2 = (bf16[256,768]{1,0:T(8,128)(2,1)S(1)}, bf16[256,768]{1,0:T(8,128)(2,1)S(1)}, u32[]{:S(2)}, u32[]{:S(2)}) collective-permute-start(bf16[256,768]{1,0:T(8,128)(2,1)S(1)} %convolution_convert_fusion.7), channel_id=1, source_target_pairs={{0,32},{32,0},{1,33},{33,1},{2,34},{34,2},{3,35},{35,3},{4,36},{36... | collective-permute-start | bytes 1179656 | tf_op jit(solution)/shard_map/ppermute | solution.py:27
  6.2 17.4 %collective-permute-start.3 = (bf16[768,768]{1,0:T(8,128)(2,1)S(1)}, bf16[768,768]{1,0:T(8,128)(2,1)}, u32[]{:S(2)}, u32[]{:S(2)}) collective-permute-start(bf16[768,768]{1,0:T(8,128)(2,1)S(1)} %copy-done.1), channel_id=1, source_target_pairs={{0,32},{32,0},{1,33},{33,1},{2,34},{34,2},{3,35},{35,3},{4,36},{36... | collective-permute-start | bytes 3538952 | tf_op jit(solution)/shard_map/ppermute | solution.py:27
  18.2 5.4 %copy-start.11 = (bf16[64,768]{1,0:T(8,128)(2,1)}, bf16[64,768]{1,0:T(8,128)(2,1)S(1)}, u32[]{:S(2)}) copy-start(bf16[64,768]{1,0:T(8,128)(2,1)S(1)} %reduce_sum.60) | copy-start | bytes 294916
  19.0 9.9 %all-to-all-start.1 = ((bf16[4,64,768]{2,1,0:T(8,128)(2,1)}), bf16[4,64,768]{2,1,0:T(8,128)(2,1)S(1)}, u32[]{:S(2)}, u32[]{:S(2)}) async-start(bf16[4,64,768]{2,1,0:T(8,128)(2,1)} %broadcast_in_dim.10), calls=%async_computation.1 | async-start | bytes 786432 | tf_op jit(solution)/shard_map/all_to_all | solution.py:37
  28.9 3.5 %copy-start.13 = (bf16[4,64,768]{2,1,0:T(8,128)(2,1)}, bf16[4,64,768]{2,1,0:T(8,128)(2,1)S(1)}, u32[]{:S(2)}) copy-start(bf16[4,64,768]{2,1,0:T(8,128)(2,1)S(1)} %all-to-all-done.1) | copy-start | bytes 1179652
  32.4 26.8 %all-to-all-start.2 = ((bf16[32,8,1536]{2,1,0:T(8,128)(2,1)}), bf16[32,8,1536]{2,1,0:T(8,128)(2,1)S(1)}, u32[]{:S(2)}, u32[]{:S(2)}) async-start(bf16[32,8,1536]{2,1,0:T(8,128)(2,1)} %fusion), calls=%async_computation.2 | async-start | bytes 1572864 | tf_op jit(solution)/shard_map/all_to_all | solution.py:31
  43.4 15.9 %collective-permute-start.1 = (f32[8,768]{1,0:T(8,128)S(1)}, f32[8,768]{1,0:T(8,128)S(1)}, u32[]{:S(2)}, u32[]{:S(2)}) collective-permute-start(f32[8,768]{1,0:T(8,128)S(1)} %get-tuple-element.8), channel_id=1, source_target_pairs={{0,32},{32,0},{1,33},{33,1},{2,34},{34,2},{3,35},{35,3},{4,36},{36... | collective-permute-start | bytes 73736 | tf_op jit(solution)/shard_map/ppermute | solution.py:27
  60.2 24.5 %all-to-all-start.3 = ((bf16[32,8,1536]{2,1,0:T(8,128)(2,1)}), bf16[32,8,1536]{2,1,0:T(8,128)(2,1)S(1)}, u32[]{:S(2)}, u32[]{:S(2)}) async-start(bf16[32,8,1536]{2,1,0:T(8,128)(2,1)} %broadcast_in_dim.11), calls=%async_computation.3 | async-start | bytes 1572864 | tf_op jit(solution)/shard_map/all_to_all | solution.py:37
  68.8 9.1 %collective-permute-start.4 = (bf16[768,768]{1,0:T(8,128)(2,1)S(1)}, bf16[768,768]{1,0:T(8,128)(2,1)S(1)}, u32[]{:S(2)}, u32[]{:S(2)}) collective-permute-start(bf16[768,768]{1,0:T(8,128)(2,1)S(1)} %copy-done), channel_id=1, source_target_pairs={{0,32},{32,0},{1,33},{33,1},{2,34},{34,2},{3,35},{35,3},{4,36},{36... | collective-permute-start | bytes 3538952 | tf_op jit(solution)/shard_map/ppermute | solution.py:27
  74.3 0.8 copy-start.9
  74.3 3.1 %copy-start.5 = (bf16[256,768]{1,0:T(8,128)(2,1)}, bf16[256,768]{1,0:T(8,128)(2,1)S(1)}, u32[]{:S(2)}) copy-start(bf16[256,768]{1,0:T(8,128)(2,1)S(1)} %get-tuple-element.10) | copy-start | bytes 1179652
  75.6 1.8 collective-permute-start.5
  108.6 0.7 copy-start.15
  112.8 7.6 %copy-start.2 = (f32[512,768]{1,0:T(8,128)S(1)}, f32[512,768]{1,0:T(8,128)}, u32[]{:S(2)}) copy-start(f32[512,768]{1,0:T(8,128)} %param.7) | copy-start | bytes 4718596
  112.8 22.4 %all-to-all-start.6 = ((bf16[32,8,1536]{2,1,0:T(8,128)(2,1)}), bf16[32,8,1536]{2,1,0:T(8,128)(2,1)}, u32[]{:S(2)}, u32[]{:S(2)}) async-start(bf16[32,8,1536]{2,1,0:T(8,128)(2,1)} %fusion.1), calls=%async_computation.6 | async-start | bytes 1572864 | tf_op jit(solution)/shard_map/all_to_all | solution.py:31
  122.0 14.4 %collective-permute-start = (f32[8,768]{1,0:T(8,128)S(1)}, f32[8,768]{1,0:T(8,128)S(1)}, u32[]{:S(2)}, u32[]{:S(2)}) collective-permute-start(f32[8,768]{1,0:T(8,128)S(1)} %get-tuple-element.6), channel_id=1, source_target_pairs={{0,32},{32,0},{1,33},{33,1},{2,34},{34,2},{3,35},{35,3},{4,36},{36... | collective-permute-start | bytes 73736 | tf_op jit(solution)/shard_map/ppermute | solution.py:27
  158.7 11.2 %copy-start.12 = (bf16[64,768]{1,0:T(8,128)(2,1)S(1)}, bf16[64,768]{1,0:T(8,128)(2,1)}, u32[]{:S(2)}) copy-start(bf16[64,768]{1,0:T(8,128)(2,1)} %copy-done.11) | copy-start | bytes 294916
  169.9 21.7 %copy-start.14 = (bf16[4,64,768]{2,1,0:T(8,128)(2,1)S(1)}, bf16[4,64,768]{2,1,0:T(8,128)(2,1)}, u32[]{:S(2)}) copy-start(bf16[4,64,768]{2,1,0:T(8,128)(2,1)} %copy-done.13) | copy-start | bytes 1179652
  179.7 13.3 %collective-permute-start.6 = (bf16[256,768]{1,0:T(8,128)(2,1)S(1)}, bf16[256,768]{1,0:T(8,128)(2,1)}, u32[]{:S(2)}, u32[]{:S(2)}) collective-permute-start(bf16[256,768]{1,0:T(8,128)(2,1)S(1)} %bitcast.64), channel_id=1, source_target_pairs={{0,32},{32,0},{1,33},{33,1},{2,34},{34,2},{3,35},{35,3},{4,36},{36... | collective-permute-start | bytes 1179656 | tf_op jit(solution)/shard_map/ppermute | solution.py:27
  191.6 24.1 %collective-permute-start.10 = (bf16[256,768]{1,0:T(8,128)(2,1)S(1)}, bf16[256,768]{1,0:T(8,128)(2,1)}, u32[]{:S(2)}, u32[]{:S(2)}) collective-permute-start(bf16[256,768]{1,0:T(8,128)(2,1)S(1)} %bitcast.70), channel_id=1, source_target_pairs={{0,32},{32,0},{1,33},{33,1},{2,34},{34,2},{3,35},{35,3},{4,36},{36... | collective-permute-start | bytes 1179656 | tf_op jit(solution)/shard_map/ppermute | solution.py:27
  194.6 6.4 %copy-start.17 = (bf16[64,768]{1,0:T(8,128)(2,1)S(1)}, bf16[64,768]{1,0:T(8,128)(2,1)}, u32[]{:S(2)}) copy-start(bf16[64,768]{1,0:T(8,128)(2,1)} %get-tuple-element.17) | copy-start | bytes 294916
  195.5 28.8 %all-to-all-start.10 = ((bf16[32,16,768]{2,1,0:T(8,128)(2,1)}), bf16[32,16,768]{2,1,0:T(8,128)(2,1)S(1)}, u32[]{:S(2)}, u32[]{:S(2)}) async-start(bf16[32,16,768]{2,1,0:T(8,128)(2,1)} %pad_maximum_fusion.1), calls=%async_computation.10 | async-start | bytes 1572864 | tf_op jit(solution)/shard_map/all_to_all | solution.py:31
  211.2 5.1 %collective-permute-start.11 = (bf16[256,768]{1,0:T(8,128)(2,1)S(1)}, bf16[256,768]{1,0:T(8,128)(2,1)S(1)}, u32[]{:S(2)}, u32[]{:S(2)}) collective-permute-start(bf16[256,768]{1,0:T(8,128)(2,1)S(1)} %all_gather.3), channel_id=1, source_target_pairs={{0,32},{32,0},{1,33},{33,1},{2,34},{34,2},{3,35},{35,3},{4,36},{36... | collective-permute-start | bytes 1179656 | tf_op jit(solution)/shard_map/ppermute | solution.py:27
  214.6 1.0 copy-start.16
  214.6 1.0 copy-start.18
  214.6 1.9 copy-start.6
  214.6 1.9 copy-start.10
  214.7 1.8 collective-permute-start.12
  214.8 5.6 %collective-permute-start.8 = (bf16[256,768]{1,0:T(8,128)(2,1)S(1)}, bf16[256,768]{1,0:T(8,128)(2,1)S(1)}, u32[]{:S(2)}, u32[]{:S(2)}) collective-permute-start(bf16[256,768]{1,0:T(8,128)(2,1)S(1)} %get-tuple-element.16), channel_id=1, source_target_pairs={{0,32},{32,0},{1,33},{33,1},{2,34},{34,2},{3,35},{35,3},{4,36},{36... | collective-permute-start | bytes 1179656 | tf_op jit(solution)/shard_map/ppermute | solution.py:27
  215.6 4.9 %collective-permute-start.9 = (bf16[256,768]{1,0:T(8,128)(2,1)S(1)}, bf16[256,768]{1,0:T(8,128)(2,1)S(1)}, u32[]{:S(2)}, u32[]{:S(2)}) collective-permute-start(bf16[256,768]{1,0:T(8,128)(2,1)S(1)} %bitcast.73), channel_id=1, source_target_pairs={{0,32},{32,0},{1,33},{33,1},{2,34},{34,2},{3,35},{35,3},{4,36},{36... | collective-permute-start | bytes 1179656 | tf_op jit(solution)/shard_map/ppermute | solution.py:27
  215.6 8.9 %collective-permute-start.7 = (f32[8,768]{1,0:T(8,128)S(1)}, f32[8,768]{1,0:T(8,128)S(1)}, u32[]{:S(2)}, u32[]{:S(2)}) collective-permute-start(f32[8,768]{1,0:T(8,128)S(1)} %get-tuple-element.22), channel_id=1, source_target_pairs={{0,32},{32,0},{1,33},{33,1},{2,34},{34,2},{3,35},{35,3},{4,36},{36... | collective-permute-start | bytes 73736 | tf_op jit(solution)/shard_map/ppermute | solution.py:27
  216.5 4.0 %copy-start.4 = (bf16[256,768]{1,0:T(8,128)(2,1)S(1)}, bf16[256,768]{1,0:T(8,128)(2,1)}, u32[]{:S(2)}) copy-start(bf16[256,768]{1,0:T(8,128)(2,1)} %copy-done.3) | copy-start | bytes 1179652
  216.5 4.0 %copy-start.8 = (bf16[256,768]{1,0:T(8,128)(2,1)S(1)}, bf16[256,768]{1,0:T(8,128)(2,1)}, u32[]{:S(2)}) copy-start(bf16[256,768]{1,0:T(8,128)(2,1)} %copy-done.7) | copy-start | bytes 1179652

commit v2 on v1

v2 whole, which is shorter than its diff:
```python
import functools
import math

import jax
import jax.numpy as jnp
from jax import lax
from jax.experimental import pallas as pl
from jax.experimental.pallas import tpu as pltpu
from jax.sharding import Mesh, PartitionSpec as P

gelu_scale = math.sqrt(2.0 / math.pi)
cubic_coef = 0.044715
f32 = jnp.float32
bf16 = jnp.bfloat16
SIZES = {"y": 4, "core": 2, "x": 4, "z": 8}
HIDDEN = ("x", "z")
STRIP = 64


def gelu_parts(preact):
    inner = gelu_scale * (preact + cubic_coef * preact * preact * preact)
    tangent = jnp.tanh(inner)
    value_out = 0.5 * preact * (1.0 + tangent)
    slope_out = 0.5 * (1.0 + tangent) + 0.5 * preact * (1.0 - tangent * tangent) * gelu_scale * (
        1.0 + 3.0 * cubic_coef * preact * preact
    )
    return (value_out, slope_out)


def dot(a, b):
    return jnp.dot(a, b, preferred_element_type=f32)


def dot_t(a, b):
    return lax.dot_general(a, b, (((1,), (1,)), ((), ())), preferred_element_type=f32)


def t_dot(a, b):
    return lax.dot_general(a, b, (((0,), (0,)), ((), ())), preferred_element_type=f32)


def call(body, outs, *operands, flops=0):
    size = sum(math.prod(o.shape) * o.dtype.itemsize for o in operands)
    size += sum(math.prod(s) * jnp.dtype(t).itemsize for s, t in outs)
    got = pl.pallas_call(
        body,
        out_shape=[jax.ShapeDtypeStruct(s, t) for s, t in outs],
        in_specs=[pl.BlockSpec(memory_space=pltpu.VMEM)] * len(operands),
        out_specs=[pl.BlockSpec(memory_space=pltpu.VMEM)] * len(outs),
        cost_estimate=pl.CostEstimate(flops=flops, bytes_accessed=size, transcendentals=0),
        compiler_params=pltpu.CompilerParams(vmem_limit_bytes=24 * 2**20),
    )(*operands)
    return got[0] if len(outs) == 1 else got


def widen(product, rows_deep, own_block, other_block):
    rows, wide = rows_deep.shape[0], rows_deep.shape[1]

    def body(x_ref, a_ref, b_ref, o_ref):
        o_ref[:, :wide] = product(x_ref[...], a_ref[...]).astype(bf16)
        o_ref[:, wide:] = product(x_ref[...], b_ref[...]).astype(bf16)

    return call(
        body, [((rows, 2 * wide), bf16)], rows_deep, own_block, other_block, flops=4 * rows * wide * wide
    )


def narrow(product, rows_wide, own_block, other_block):
    rows, wide = rows_wide.shape[0], rows_wide.shape[1] // 2

    def body(x_ref, a_ref, b_ref, o_ref):
        total = product(x_ref[:, :wide], a_ref[...]) + product(x_ref[:, wide:], b_ref[...])
        o_ref[...] = total.astype(bf16)

    return call(
        body, [((rows, wide), bf16)], rows_wide, own_block, other_block, flops=4 * rows * wide * wide
    )


def add_up(ref, columns):
    total = ref[0, :, columns].astype(f32)
    for k in range(1, ref.shape[0]):
        total = total + ref[k, :, columns].astype(f32)
    return total


def strips(width, step):
    return [slice(first, first + step) for first in range(0, width, step)]


def sum_and_copy(landed, added):
    count, eight, wide = landed.shape

    def body(l_ref, a_ref, s_ref, c_ref):
        for cols in strips(wide, 256):
            total = a_ref[:, cols] + add_up(l_ref, cols)
            s_ref[:, cols] = total
            rounded = total.astype(bf16)
            for k in range(count):
                c_ref[k, :, cols] = rounded

    return call(body, [((eight, wide), f32), ((count, eight, wide), bf16)], landed, added)


def sum_last(landed, added):
    count, eight, wide = landed.shape
    half = wide // 2

    def body(l_ref, a_ref, m_ref, t_ref):
        for cols in strips(half, 256):
            m_ref[:, cols] = a_ref[:, cols] + add_up(l_ref, cols)
            far = slice(cols.start + half, cols.stop + half)
            t_ref[:, cols] = a_ref[:, far] + add_up(l_ref, far)

    return call(body, [((eight, half), f32)] * 2, landed, added)


def activate(landed):
    count, rows, deep = landed.shape

    def body(l_ref, p_ref, c_ref):
        for cols in strips(deep, 128):
            pre = add_up(l_ref, cols).astype(bf16)
            p_ref[:, cols] = pre
            value = gelu_parts(pre.astype(f32))[0].astype(bf16)
            for k in range(count):
                c_ref[k, :, cols] = value

    return call(body, [((rows, deep), bf16), ((count, rows, deep), bf16)], landed)


def activate_and_back(landed):
    count, rows, deep = landed.shape[0], landed.shape[1], landed.shape[2] // 2

    def body(l_ref, v_ref, c_ref):
        for cols in strips(deep, 128):
            pre = add_up(l_ref, cols).astype(bf16)
            value, slope = gelu_parts(pre.astype(f32))
            v_ref[:, cols] = value.astype(bf16)
            back = add_up(l_ref, slice(cols.start + deep, cols.stop + deep)).astype(bf16)
            inner = (back.astype(f32) * slope).astype(bf16)
            for k in range(count):
                c_ref[k, :, cols] = inner

    return call(body, [((rows, deep), bf16), ((count, rows, deep), bf16)], landed)


def back_through(landed, pre):
    count, rows, deep = landed.shape

    def body(l_ref, p_ref, c_ref):
        for cols in strips(deep, 128):
            slope = gelu_parts(p_ref[:, cols].astype(f32))[1]
            back = add_up(l_ref, cols).astype(bf16)
            inner = (back.astype(f32) * slope).astype(bf16)
            for k in range(count):
                c_ref[k, :, cols] = inner

    return call(body, [((count, rows, deep), bf16)], landed, pre)


def swap(block):
    return lax.ppermute(block, "core", [(0, 1), (1, 0)])


def exchange(parts, axes):
    return lax.all_to_all(parts, axes, 0, 0, tiled=True)


def shards(start_latent, target_one, target_two, w_up, w_down):
    n_y = SIZES["y"]
    n_h = SIZES["x"] * SIZES["z"]
    rows, wide = start_latent.shape
    deep = w_up.shape[1]
    eight = rows // (2 * n_h)
    half = rows // 2
    quarter = half // n_y
    core = lax.axis_index("core")
    place = lax.axis_index("x") * SIZES["z"] + lax.axis_index("z")

    def halves(full):
        cut = full.reshape(n_h, 2, eight, wide)
        own = lax.dynamic_index_in_dim(cut, core, 1, keepdims=False)
        other = lax.dynamic_index_in_dim(cut, 1 - core, 1, keepdims=False)
        return own, other

    def own_rows(full):
        own, other = halves(full)
        mine = lax.dynamic_index_in_dim(own, place, 0, keepdims=False)
        theirs = lax.dynamic_index_in_dim(other, place, 0, keepdims=False)
        return jnp.concatenate([mine, swap(theirs)], axis=1)

    def rounded_halves(full):
        own, other = halves(full)
        return own.astype(bf16).reshape(half, wide), other.astype(bf16).reshape(half, wide)

    def both_cores(own, other_part):
        return (own + swap(other_part.astype(bf16)).astype(f32)).astype(bf16)

    up_other = swap(w_up)
    down_other = swap(w_down)

    start_own, start_other = rounded_halves(start_latent)
    pre_part = both_cores(dot(start_own, w_up), dot(start_other, w_up))
    pre_zero, act_zero = activate(exchange(pre_part.reshape(n_y, quarter, deep), "y"))
    act_zero = exchange(act_zero, "y").reshape(half, deep)

    part = widen(dot, act_zero, w_down, down_other)
    latent_one, input_one = sum_and_copy(
        exchange(part.reshape(n_h, eight, 2 * wide), HIDDEN), own_rows(start_latent)
    )
    input_one = exchange(input_one, HIDDEN).reshape(half, 2 * wide)

    two_own, two_other = rounded_halves(target_two)
    back_part = both_cores(dot_t(two_own, w_down), dot_t(two_other, w_down))

    pre_part = narrow(dot, input_one, w_up, up_other)
    both = jnp.concatenate([pre_part.reshape(n_y, quarter, deep), back_part.reshape(n_y, quarter, deep)], axis=2)
    act_one, inner_one = activate_and_back(exchange(both, "y"))
    inner_one = exchange(inner_one, "y").reshape(half, deep)

    part = widen(dot_t, inner_one, w_up, up_other)
    grad_one, error_one = sum_and_copy(
        exchange(part.reshape(n_h, eight, 2 * wide), HIDDEN), own_rows(target_one + target_two)
    )
    error_one = exchange(error_one, HIDDEN).reshape(half, 2 * wide)

    back_part = narrow(dot_t, error_one, w_down, down_other)
    inner_zero = back_through(exchange(back_part.reshape(n_y, quarter, deep), "y"), pre_zero)
    inner_zero = exchange(inner_zero, "y").reshape(half, deep)

    part = widen(dot_t, inner_zero, w_up, up_other)
    landed = exchange(part.reshape(n_h, eight, 2 * wide), HIDDEN)

    act_one = lax.all_gather(act_one, "y", axis=0, tiled=True)
    grad_down = t_dot(
        jnp.concatenate([act_zero, swap(act_zero), act_one, swap(act_one)], axis=0),
        jnp.concatenate([error_one[:, :wide], swap(error_one[:, wide:]), two_own, two_other], axis=0),
    )
    grad_up = t_dot(
        jnp.concatenate([start_own, start_other, input_one[:, :wide], swap(input_one[:, wide:])], axis=0),
        jnp.concatenate([inner_zero, swap(inner_zero), inner_one, swap(inner_one)], axis=0),
    )
    landed, grad_up, grad_down = lax.optimization_barrier((landed, grad_up, grad_down))

    mine, theirs = sum_last(landed, grad_one)
    theirs = swap(theirs)
    grad_start = jnp.where(
        core == 0, jnp.concatenate([mine, theirs], axis=0), jnp.concatenate([theirs, mine], axis=0)
    )
    return (grad_start, grad_up, grad_down)


def solution(mesh):
    fine = Mesh(mesh.devices.reshape(tuple(SIZES.values())), tuple(SIZES))
    width, hidden = ("y", "core"), HIDDEN
    return jax.shard_map(
        shards,
        mesh=fine,
        in_specs=(
            P(None, width),
            P(None, width),
            P(None, width),
            P(width, hidden),
            P(hidden, width),
        ),
        out_specs=(P(hidden, width), P(width, hidden), P(hidden, width)),
        check_vma=False,
    )
```

time: 226 us -> 219 us (0.969)
  matrix products: 23.6 us -> 9.52 us
  Pallas kernels: 0 us -> 10.5 us
  starting transfers between devices: 70.2 us -> 77.4 us
  local copies, waits for them, and re-layouts: 13.2 us -> 9.59 us
  other arithmetic: 6.64 us -> 3.38 us
  waiting for transfers between devices: 30 us -> 27.3 us
    pallas_call x0 -> x11, Pallas kernels: none -> 10.5 us  [call(): pl.pallas_call(body, out_shape=[jax.ShapeDtypeStruct(s, t) for s, t in ou...]
    ppermute x13, starting transfers between devices: 34.9 us -> 42.8 us  [swap(): return lax.ppermute(block, 'core', [(0, 1), (1, 0)])]
    dot_general x6 -> x2, matrix products: 8.91 us -> 1.77 us  [dot_t(): lax.dot_general(a, b, (((1,), (1,)), ((), ())), preferred_element_type=f32)]
    dot_general x4 -> x2, matrix products: 6.85 us -> 0.95 us  [dot(): return jnp.dot(a, b, preferred_element_type=f32)]
    all_to_all x5, waiting for transfers between devices: 26.9 us -> 21.5 us  [exchange(): return lax.all_to_all(parts, axes, 0, 0, tiled=True)]
    concatenate x4 -> x0, local copies, waits for them, and re-layouts: 4.24 us -> none  [the longest x1 2.36 us: shards(): down_wide = jnp.concatenate([w_down, swap(w_down)], axis=1)]
    ppermute x13, waiting for transfers between devices: 3.14 us -> 5.75 us  [swap(): return lax.ppermute(block, 'core', [(0, 1), (1, 0)])]
    unnamed x40 -> x62, local copies, waits for them, and re-layouts: 4 us -> 4.54 us
  transfers between devices with their start and end apart: 18 -> 18, of which waited for: 8 -> 8; matrix products, arithmetic and copies ran while one was open for 11% -> 7% of each run, Pallas kernels for 0% -> 1%
where the time goes in v2:
time: 219 us; the launch traced here: 218 us
  blocking collectives  79.6 us (36%)
  starting transfers between devices  77.4 us (35%)
  waiting for transfers between devices  27.3 us (12%)
  Pallas kernels  10.5 us (5%)
  local copies, waits for them, and re-layouts  9.59 us (4%)
  matrix products  9.52 us (4%)
  other arithmetic  3.38 us (2%)
    all_to_all x6, blocking collectives, exchange(): return lax.all_to_all(parts, axes, 0, 0, tiled=True)  69.5 us
    ppermute x13, starting transfers between devices, swap(): return lax.ppermute(block, 'core', [(0, 1), (1, 0)])  42.8 us
    all_to_all x5, starting transfers between devices, exchange(): return lax.all_to_all(parts, axes, 0, 0, tiled=True)  34.6 us
    all_to_all x5, waiting for transfers between devices, exchange(): return lax.all_to_all(parts, axes, 0, 0, tiled=True)  21.5 us
    pallas_call x11, Pallas kernels, call(): pl.pallas_call(body, out_shape=[jax.ShapeDtypeStruct(s, t) for s, t in ou...  10.5 us
    all_gather x1, blocking collectives, shards(): act_one = lax.all_gather(act_one, 'y', axis=0, tiled=True)  10.2 us
    dot_general x2, matrix products, t_dot(): lax.dot_general(a, b, (((0,), (0,)), ((), ())), preferred_element_type=f32)  6.8 us
    ppermute x13, waiting for transfers between devices, swap(): return lax.ppermute(block, 'core', [(0, 1), (1, 0)])  5.75 us
  transfers between devices with their start and end apart: 18, of which 8 were waited for; matrix products, arithmetic and copies ran while one was open for 7% of the time, Pallas kernels for 1%

profile of v2, /device:TPU:1, one launch (start us, length us, event | category | flops | bytes accessed | tf_op | source)
XLA Modules:
  0.0 218.4 jit_solution(17260521450329850392)
XLA Ops:
  0.7 1.6 fusion.31
  2.9 3.3 %collective-permute-start = (bf16[256,768]{1,0:T(8,128)(2,1)S(1)}, bf16[256,768]{1,0:T(8,128)(2,1)S(1)}, u32[]{:S(2)}, u32[]{:S(2)}) collective-permute-start(bf16[256,768]{1,0:T(8,128)(2,1)S(1)} %convolution_convert_fusion.1), channel_id=1, source_target_pairs={{0,32},{32,0},{1,33},{33,1},{2,34},{34,2},{3,35},{35,3},{4,36},{36... | collective-permute-start | bytes 1179656 | tf_op jit(solution)/shard_map/ppermute | solution.py:163
  6.3 1.2 collective-permute-done
  8.0 10.1 %all_to_all.55.l_ref = bf16[4,64,768]{2,1,0:T(8,128)(2,1)S(1)} all-to-all(bf16[4,64,768]{2,1,0:T(8,128)(2,1)S(1)} %bitcast.72), channel_id=1, replica_groups=mesh['y'=4,'core'=2,'x'=4,'z'=8] {'y'}, dimensions={0} | all-to-all | bytes 786432 | tf_op jit(solution)/shard_map/all_to_all | solution.py:167
  18.2 8.8 %all_to_all.56 = bf16[4,64,768]{2,1,0:T(8,128)(2,1)S(1)} all-to-all(bf16[4,64,768]{2,1,0:T(8,128)(2,1)S(1)} %get-tuple-element.15), channel_id=1, replica_groups=mesh['y'=4,'core'=2,'x'=4,'z'=8] {'y'}, dimensions={0} | all-to-all | bytes 786432 | tf_op jit(solution)/shard_map/all_to_all | solution.py:167
  27.1 1.7 shard_map.77
  28.8 10.2 %all-to-all-start.2 = ((bf16[32,8,1536]{2,1,0:T(8,128)(2,1)}), bf16[32,8,1536]{2,1,0:T(8,128)(2,1)S(1)}, u32[]{:S(2)}, u32[]{:S(2)}) async-start(bf16[32,8,1536]{2,1,0:T(8,128)(2,1)} %bitcast.5), calls=%async_computation.2 | async-start | bytes 1572864 | tf_op jit(solution)/shard_map/all_to_all | solution.py:167
  39.0 0.8 dynamic-slice_bitcast_fusion.3
  39.8 3.2 %collective-permute-start.2 = (f32[8,768]{1,0:T(8,128)S(1)}, f32[8,768]{1,0:T(8,128)S(1)}, u32[]{:S(2)}, u32[]{:S(2)}) collective-permute-start(f32[8,768]{1,0:T(8,128)S(1)} %get-tuple-element.30), channel_id=1, source_target_pairs={{0,32},{32,0},{1,33},{33,1},{2,34},{34,2},{3,35},{35,3},{4,36},{36... | collective-permute-start | bytes 73736 | tf_op jit(solution)/shard_map/ppermute | solution.py:163
  43.0 0.8 collective-permute-done.2
  43.9 11.6 %all-to-all-done.2.l_ref = bf16[32,8,1536]{2,1,0:T(8,128)(2,1)S(1)} async-done(((bf16[32,8,1536]{2,1,0:T(8,128)(2,1)}), bf16[32,8,1536]{2,1,0:T(8,128)(2,1)S(1)}, u32[]{:S(2)}, u32[]{:S(2)}) %all-to-all-start.2) | async-done | bytes 786464 | tf_op jit(solution)/shard_map/all_to_all | solution.py:167
  55.5 0.7 shard_map.78
  56.3 0.9 copy-done.14
  57.2 8.7 %all-to-all-start.3 = ((bf16[32,8,1536]{2,1,0:T(8,128)(2,1)}), bf16[32,8,1536]{2,1,0:T(8,128)(2,1)}, u32[]{:S(2)}, u32[]{:S(2)}) async-start(bf16[32,8,1536]{2,1,0:T(8,128)(2,1)} %copy-done.14), calls=%async_computation.3 | async-start | bytes 1572864 | tf_op jit(solution)/shard_map/all_to_all | solution.py:167
  65.9 4.0 %collective-permute-start.3 = (bf16[768,768]{1,0:T(8,128)(2,1)S(1)}, bf16[768,768]{1,0:T(8,128)(2,1)S(1)}, u32[]{:S(2)}, u32[]{:S(2)}) collective-permute-start(bf16[768,768]{1,0:T(8,128)(2,1)S(1)} %copy-done), channel_id=1, source_target_pairs={{0,32},{32,0},{1,33},{33,1},{2,34},{34,2},{3,35},{35,3},{4,36},{36... | collective-permute-start | bytes 3538952 | tf_op jit(solution)/shard_map/ppermute | solution.py:163
  69.9 1.4 fusion.33
  72.0 1.7 collective-permute-done.4
  73.7 1.3 add_convert_fusion
  75.0 6.8 %all-to-all-done.3 = bf16[32,8,1536]{2,1,0:T(8,128)(2,1)} async-done(((bf16[32,8,1536]{2,1,0:T(8,128)(2,1)}), bf16[32,8,1536]{2,1,0:T(8,128)(2,1)}, u32[]{:S(2)}, u32[]{:S(2)}) %all-to-all-start.3) | async-done | bytes 786464 | tf_op jit(solution)/shard_map/all_to_all | solution.py:167
  81.8 2.0 shard_map.79
  83.8 10.7 %all_to_all.57.l_ref = bf16[4,64,1536]{2,1,0:T(8,128)(2,1)S(1)} all-to-all(bf16[4,64,1536]{2,1,0:T(8,128)(2,1)S(1)} %pad_maximum_fusion), channel_id=1, replica_groups=mesh['y'=4,'core'=2,'x'=4,'z'=8] {'y'}, dimensions={0} | all-to-all | bytes 1572864 | tf_op jit(solution)/shard_map/all_to_all | solution.py:167
  94.9 10.3 %all_to_all.58 = bf16[4,64,768]{2,1,0:T(8,128)(2,1)S(1)} all-to-all(bf16[4,64,768]{2,1,0:T(8,128)(2,1)S(1)} %get-tuple-element.17), channel_id=1, replica_groups=mesh['y'=4,'core'=2,'x'=4,'z'=8] {'y'}, dimensions={0} | all-to-all | bytes 786432 | tf_op jit(solution)/shard_map/all_to_all | solution.py:167
  105.2 0.8 shard_map.81
  106.0 0.9 copy-done.6
  106.9 6.8 %all-to-all-start.6 = ((bf16[32,8,1536]{2,1,0:T(8,128)(2,1)}), bf16[32,8,1536]{2,1,0:T(8,128)(2,1)}, u32[]{:S(2)}, u32[]{:S(2)}) async-start(bf16[32,8,1536]{2,1,0:T(8,128)(2,1)} %bitcast.57), calls=%async_computation.6 | async-start | bytes 1572864 | tf_op jit(solution)/shard_map/all_to_all | solution.py:167
  113.7 2.1 add.55
  115.8 8.2 %collective-permute-start.5 = (f32[8,768]{1,0:T(8,128)S(1)}, f32[8,768]{1,0:T(8,128)S(1)}, u32[]{:S(2)}, u32[]{:S(2)}) collective-permute-start(f32[8,768]{1,0:T(8,128)S(1)} %get-tuple-element.28), channel_id=1, source_target_pairs={{0,32},{32,0},{1,33},{33,1},{2,34},{34,2},{3,35},{35,3},{4,36},{36... | collective-permute-start | bytes 73736 | tf_op jit(solution)/shard_map/ppermute | solution.py:163
  124.0 0.8 collective-permute-done.5
  125.4 3.0 %all-to-all-done.6.l_ref = bf16[32,8,1536]{2,1,0:T(8,128)(2,1)} async-done(((bf16[32,8,1536]{2,1,0:T(8,128)(2,1)}), bf16[32,8,1536]{2,1,0:T(8,128)(2,1)}, u32[]{:S(2)}, u32[]{:S(2)}) %all-to-all-start.6) | async-done | bytes 786464 | tf_op jit(solution)/shard_map/all_to_all | solution.py:167
  128.5 0.8 copy-done.15
  129.3 1.4 shard_map.82
  130.7 20.9 %all_to_all.59 = bf16[32,8,1536]{2,1,0:T(8,128)(2,1)S(1)} all-to-all(bf16[32,8,1536]{2,1,0:T(8,128)(2,1)S(1)} %get-tuple-element.18), channel_id=1, replica_groups=mesh['y'=4,'core'=2,'x'=4,'z'=8] {'x','z'}, dimensions={0} | all-to-all | bytes 1572864 | tf_op jit(solution)/shard_map/all_to_all | solution.py:167
  151.5 0.8 shard_map.83
  152.4 8.6 %all_to_all.60.l_ref = bf16[4,64,768]{2,1,0:T(8,128)(2,1)S(1)} all-to-all(bf16[4,64,768]{2,1,0:T(8,128)(2,1)S(1)} %bitcast.68), channel_id=1, replica_groups=mesh['y'=4,'core'=2,'x'=4,'z'=8] {'y'}, dimensions={0} | all-to-all | bytes 786432 | tf_op jit(solution)/shard_map/all_to_all | solution.py:167
  161.0 0.9 shard_map.84
  162.0 3.5 %all-to-all-start.9 = ((bf16[4,64,768]{2,1,0:T(8,128)(2,1)}), bf16[4,64,768]{2,1,0:T(8,128)(2,1)S(1)}, u32[]{:S(2)}, u32[]{:S(2)}) async-start(bf16[4,64,768]{2,1,0:T(8,128)(2,1)} %shard_map.84), calls=%async_computation.9 | async-start | bytes 786432 | tf_op jit(solution)/shard_map/all_to_all | solution.py:167
  165.4 12.7 %collective-permute-start.9 = (bf16[256,768]{1,0:T(8,128)(2,1)}, bf16[256,768]{1,0:T(8,128)(2,1)}, u32[]{:S(2)}, u32[]{:S(2)}) collective-permute-start(bf16[256,768]{1,0:T(8,128)(2,1)} %bitcast.59), channel_id=1, source_target_pairs={{0,32},{32,0},{1,33},{33,1},{2,34},{34,2},{3,35},{35,3},{4,36},{36... | collective-permute-start | bytes 1179656 | tf_op jit(solution)/shard_map/ppermute | solution.py:163
  178.1 0.7 copy-done.11
  178.9 1.0 copy-done.12
  179.9 1.7 shard_map.85
  181.6 5.4 %all-to-all-start.10 = ((bf16[32,8,1536]{2,1,0:T(8,128)(2,1)}), bf16[32,8,1536]{2,1,0:T(8,128)(2,1)S(1)}, u32[]{:S(2)}, u32[]{:S(2)}) async-start(bf16[32,8,1536]{2,1,0:T(8,128)(2,1)} %bitcast.22), calls=%async_computation.10 | async-start | bytes 1572864 | tf_op jit(solution)/shard_map/all_to_all | solution.py:167
  187.0 10.2 %all_gather.3 = bf16[256,768]{1,0:T(8,128)(2,1)S(1)} all-gather(bf16[64,768]{1,0:T(8,128)(2,1)S(1)} %copy-done.19), channel_id=1, replica_groups=mesh['y'=4,'core'=2,'x'=4,'z'=8] {'y'}, dimensions={0}, use_global_device_ids=true | all-gather | bytes 491520 | tf_op jit(solution)/shard_map/all_gather | solution.py:235
  197.2 9.8 %collective-permute-start.10 = (bf16[256,768]{1,0:T(8,128)(2,1)S(1)}, bf16[256,768]{1,0:T(8,128)(2,1)S(1)}, u32[]{:S(2)}, u32[]{:S(2)}) collective-permute-start(bf16[256,768]{1,0:T(8,128)(2,1)S(1)} %all_gather.3), channel_id=1, source_target_pairs={{0,32},{32,0},{1,33},{33,1},{2,34},{34,2},{3,35},{35,3},{4,36},{36... | collective-permute-start | bytes 1179656 | tf_op jit(solution)/shard_map/ppermute | solution.py:163
  207.2 1.2 fusion.37
  209.5 3.9 %fusion.15 = f32[768,768]{1,0:T(8,128)} fusion(bf16[256,768]{1,0:T(8,128)(2,1)S(1)} %collective-permute-done.10, bf16[256,768]{1,0:T(8,128)(2,1)S(1)} %all_gather.3, bf16[256,768]{1,0:T(8,128)(2,1)} %collective-permute-done.9, bf16[256,768]{1,0:T(8,128)(2,1)S(1)} %bitcast.60, bf16[256,768]{1,0:T(8,128)(2,1)S(1)} %copy-done.30, ...), kind=kOutput, calls=%fused_computation.15 | convolution fusion | flops 1220542464 | bytes 5505024 | tf_op jit(solution)/shard_map/dot_general | solution.py:39
  213.5 2.9 %fusion = f32[768,768]{1,0:T(8,128)} fusion(bf16[256,768]{1,0:T(8,128)(2,1)S(1)} %collective-permute-done.6, bf16[256,768]{1,0:T(8,128)(2,1)S(1)} %get-tuple-element.37, bf16[256,768]{1,0:T(8,128)(2,1)S(1)} %copy-done.28, bf16[256,768]{1,0:T(8,128)(2,1)S(1)} %copy-done.23, bf16[256,768]{1,0:T(8,128)(2,1)S(1)} %collective-permute-done.8, ...), kind=kOutput, calls=%fused_computation | convolution fusion | flops 1220542464 | bytes 5505024 | tf_op jit(solution)/shard_map/dot_general | solution.py:39
  216.6 1.1 collective-permute-done.12
  217.7 0.6 maximum_select_fusion
  (85 shorter events, 4.6 us)
Async XLA Ops:
  0.6 1.7 copy-start
  0.6 5.5 %copy-start.1 = (bf16[768,768]{1,0:T(8,128)(2,1)S(1)}, bf16[768,768]{1,0:T(8,128)(2,1)}, u32[]{:S(2)}) copy-start(bf16[768,768]{1,0:T(8,128)(2,1)} %a_ref.8) | copy-start | bytes 3538948
  2.3 5.8 %copy-start.22 = (bf16[256,768]{1,0:T(8,128)(2,1)}, bf16[256,768]{1,0:T(8,128)(2,1)S(1)}, u32[]{:S(2)}) copy-start(bf16[256,768]{1,0:T(8,128)(2,1)S(1)} %get-tuple-element.32) | copy-start | bytes 1179652
  2.3 5.8 %copy-start.27 = (bf16[256,768]{1,0:T(8,128)(2,1)}, bf16[256,768]{1,0:T(8,128)(2,1)S(1)}, u32[]{:S(2)}) copy-start(bf16[256,768]{1,0:T(8,128)(2,1)S(1)} %get-tuple-element.31) | copy-start | bytes 1179652
  2.9 4.7 %collective-permute-start = (bf16[256,768]{1,0:T(8,128)(2,1)S(1)}, bf16[256,768]{1,0:T(8,128)(2,1)S(1)}, u32[]{:S(2)}, u32[]{:S(2)}) collective-permute-start(bf16[256,768]{1,0:T(8,128)(2,1)S(1)} %convolution_convert_fusion.1), channel_id=1, source_target_pairs={{0,32},{32,0},{1,33},{33,1},{2,34},{34,2},{3,35},{35,3},{4,36},{36... | collective-permute-start | bytes 1179656 | tf_op jit(solution)/shard_map/ppermute | solution.py:163
  6.2 20.9 %collective-permute-start.1 = (bf16[768,768]{1,0:T(8,128)(2,1)S(1)}, bf16[768,768]{1,0:T(8,128)(2,1)S(1)}, u32[]{:S(2)}, u32[]{:S(2)}) collective-permute-start(bf16[768,768]{1,0:T(8,128)(2,1)S(1)} %copy-done.1), channel_id=1, source_target_pairs={{0,32},{32,0},{1,33},{33,1},{2,34},{34,2},{3,35},{35,3},{4,36},{36... | collective-permute-start | bytes 3538952 | tf_op jit(solution)/shard_map/ppermute | solution.py:163
  18.2 8.9 %copy-start.16 = (bf16[64,768]{1,0:T(8,128)(2,1)}, bf16[64,768]{1,0:T(8,128)(2,1)S(1)}, u32[]{:S(2)}) copy-start(bf16[64,768]{1,0:T(8,128)(2,1)S(1)} %get-tuple-element.19.p_ref) | copy-start | bytes 294916
  27.1 1.7 copy-start.7
  27.1 1.7 copy-start.4
  28.8 26.8 %all-to-all-start.2 = ((bf16[32,8,1536]{2,1,0:T(8,128)(2,1)}), bf16[32,8,1536]{2,1,0:T(8,128)(2,1)S(1)}, u32[]{:S(2)}, u32[]{:S(2)}) async-start(bf16[32,8,1536]{2,1,0:T(8,128)(2,1)} %bitcast.5), calls=%async_computation.2 | async-start | bytes 1572864 | tf_op jit(solution)/shard_map/all_to_all | solution.py:167
  39.8 4.1 %collective-permute-start.2 = (f32[8,768]{1,0:T(8,128)S(1)}, f32[8,768]{1,0:T(8,128)S(1)}, u32[]{:S(2)}, u32[]{:S(2)}) collective-permute-start(f32[8,768]{1,0:T(8,128)S(1)} %get-tuple-element.30), channel_id=1, source_target_pairs={{0,32},{32,0},{1,33},{33,1},{2,34},{34,2},{3,35},{35,3},{4,36},{36... | collective-permute-start | bytes 73736 | tf_op jit(solution)/shard_map/ppermute | solution.py:163
  56.3 0.9 copy-start.14
  57.2 24.6 %all-to-all-start.3 = ((bf16[32,8,1536]{2,1,0:T(8,128)(2,1)}), bf16[32,8,1536]{2,1,0:T(8,128)(2,1)}, u32[]{:S(2)}, u32[]{:S(2)}) async-start(bf16[32,8,1536]{2,1,0:T(8,128)(2,1)} %copy-done.14), calls=%async_computation.3 | async-start | bytes 1572864 | tf_op jit(solution)/shard_map/all_to_all | solution.py:167
  65.9 9.1 %collective-permute-start.3 = (bf16[768,768]{1,0:T(8,128)(2,1)S(1)}, bf16[768,768]{1,0:T(8,128)(2,1)S(1)}, u32[]{:S(2)}, u32[]{:S(2)}) collective-permute-start(bf16[768,768]{1,0:T(8,128)(2,1)S(1)} %copy-done), channel_id=1, source_target_pairs={{0,32},{32,0},{1,33},{33,1},{2,34},{34,2},{3,35},{35,3},{4,36},{36... | collective-permute-start | bytes 3538952 | tf_op jit(solution)/shard_map/ppermute | solution.py:163
  71.4 3.6 %copy-start.24 = (bf16[256,768]{1,0:T(8,128)(2,1)}, bf16[256,768]{1,0:T(8,128)(2,1)S(1)}, u32[]{:S(2)}) copy-start(bf16[256,768]{1,0:T(8,128)(2,1)S(1)} %get-tuple-element.34) | copy-start | bytes 1179652
  71.4 3.6 %copy-start.29 = (bf16[256,768]{1,0:T(8,128)(2,1)}, bf16[256,768]{1,0:T(8,128)(2,1)S(1)}, u32[]{:S(2)}) copy-start(bf16[256,768]{1,0:T(8,128)(2,1)S(1)} %get-tuple-element.33) | copy-start | bytes 1179652
  71.9 1.8 collective-permute-start.4
  81.8 2.0 copy-start.26
  94.8 11.1 %copy-start.18 = (bf16[64,768]{1,0:T(8,128)(2,1)}, bf16[64,768]{1,0:T(8,128)(2,1)S(1)}, u32[]{:S(2)}) copy-start(bf16[64,768]{1,0:T(8,128)(2,1)S(1)} %get-tuple-element.20) | copy-start | bytes 294916
  105.2 0.8 copy-start.9
  106.0 0.9 copy-start.6
  106.9 21.6 %all-to-all-start.6 = ((bf16[32,8,1536]{2,1,0:T(8,128)(2,1)}), bf16[32,8,1536]{2,1,0:T(8,128)(2,1)}, u32[]{:S(2)}, u32[]{:S(2)}) async-start(bf16[32,8,1536]{2,1,0:T(8,128)(2,1)} %bitcast.57), calls=%async_computation.6 | async-start | bytes 1572864 | tf_op jit(solution)/shard_map/all_to_all | solution.py:167
  115.8 9.0 %collective-permute-start.5 = (f32[8,768]{1,0:T(8,128)S(1)}, f32[8,768]{1,0:T(8,128)S(1)}, u32[]{:S(2)}, u32[]{:S(2)}) collective-permute-start(f32[8,768]{1,0:T(8,128)S(1)} %get-tuple-element.28), channel_id=1, source_target_pairs={{0,32},{32,0},{1,33},{33,1},{2,34},{34,2},{3,35},{35,3},{4,36},{36... | collective-permute-start | bytes 73736 | tf_op jit(solution)/shard_map/ppermute | solution.py:163
  128.5 0.8 copy-start.15
  129.3 22.3 %copy-start.5 = (bf16[768,768]{1,0:T(8,128)(2,1)S(1)}, bf16[768,768]{1,0:T(8,128)(2,1)}, u32[]{:S(2)}) copy-start(bf16[768,768]{1,0:T(8,128)(2,1)} %copy-done.4) | copy-start | bytes 3538948
  130.7 21.7 %copy-start.20 = (f32[8,1536]{1,0:T(8,128)}, f32[8,1536]{1,0:T(8,128)S(1)}, u32[]{:S(2)}) copy-start(f32[8,1536]{1,0:T(8,128)S(1)} %get-tuple-element.22.a_ref) | copy-start | bytes 147460
  151.5 0.9 copy-start.2
  151.5 9.5 %copy-start.17 = (bf16[64,768]{1,0:T(8,128)(2,1)S(1)}, bf16[64,768]{1,0:T(8,128)(2,1)}, u32[]{:S(2)}) copy-start(bf16[64,768]{1,0:T(8,128)(2,1)} %copy-done.16) | copy-start | bytes 294916
  162.0 16.2 %all-to-all-start.9 = ((bf16[4,64,768]{2,1,0:T(8,128)(2,1)}), bf16[4,64,768]{2,1,0:T(8,128)(2,1)S(1)}, u32[]{:S(2)}, u32[]{:S(2)}) async-start(bf16[4,64,768]{2,1,0:T(8,128)(2,1)} %shard_map.84), calls=%async_computation.9 | async-start | bytes 786432 | tf_op jit(solution)/shard_map/all_to_all | solution.py:167
  165.4 43.6 %collective-permute-start.9 = (bf16[256,768]{1,0:T(8,128)(2,1)}, bf16[256,768]{1,0:T(8,128)(2,1)}, u32[]{:S(2)}, u32[]{:S(2)}) collective-permute-start(bf16[256,768]{1,0:T(8,128)(2,1)} %bitcast.59), channel_id=1, source_target_pairs={{0,32},{32,0},{1,33},{33,1},{2,34},{34,2},{3,35},{35,3},{4,36},{36... | collective-permute-start | bytes 1179656 | tf_op jit(solution)/shard_map/ppermute | solution.py:163
  178.9 1.0 copy-start.12
  181.6 5.4 %copy-start.19 = (bf16[64,768]{1,0:T(8,128)(2,1)S(1)}, bf16[64,768]{1,0:T(8,128)(2,1)}, u32[]{:S(2)}) copy-start(bf16[64,768]{1,0:T(8,128)(2,1)} %copy-done.18) | copy-start | bytes 294916
  181.6 25.4 %copy-start.3 = (bf16[32,8,1536]{2,1,0:T(8,128)(2,1)S(1)}, bf16[32,8,1536]{2,1,0:T(8,128)(2,1)}, u32[]{:S(2)}) copy-start(bf16[32,8,1536]{2,1,0:T(8,128)(2,1)} %copy-done.2) | copy-start | bytes 2359300
  181.6 34.7 %all-to-all-start.10 = ((bf16[32,8,1536]{2,1,0:T(8,128)(2,1)}), bf16[32,8,1536]{2,1,0:T(8,128)(2,1)S(1)}, u32[]{:S(2)}, u32[]{:S(2)}) async-start(bf16[32,8,1536]{2,1,0:T(8,128)(2,1)} %bitcast.22), calls=%async_computation.10 | async-start | bytes 1572864 | tf_op jit(solution)/shard_map/all_to_all | solution.py:167
  197.2 11.7 %copy-start.10 = (bf16[4,64,768]{2,1,0:T(8,128)(2,1)S(1)}, bf16[4,64,768]{2,1,0:T(8,128)(2,1)}, u32[]{:S(2)}) copy-start(bf16[4,64,768]{2,1,0:T(8,128)(2,1)} %copy-done.9) | copy-start | bytes 1179652
  197.2 11.8 %copy-start.13 = (bf16[4,64,768]{2,1,0:T(8,128)(2,1)S(1)}, bf16[4,64,768]{2,1,0:T(8,128)(2,1)}, u32[]{:S(2)}) copy-start(bf16[4,64,768]{2,1,0:T(8,128)(2,1)} %copy-done.11) | copy-start | bytes 1179652
  197.2 12.2 %copy-start.8 = (bf16[4,64,768]{2,1,0:T(8,128)(2,1)S(1)}, bf16[4,64,768]{2,1,0:T(8,128)(2,1)}, u32[]{:S(2)}) copy-start(bf16[4,64,768]{2,1,0:T(8,128)(2,1)} %copy-done.7) | copy-start | bytes 1179652
  197.2 12.2 %copy-start.25 = (bf16[256,768]{1,0:T(8,128)(2,1)S(1)}, bf16[256,768]{1,0:T(8,128)(2,1)}, u32[]{:S(2)}) copy-start(bf16[256,768]{1,0:T(8,128)(2,1)} %copy-done.24) | copy-start | bytes 1179652
  197.2 12.2 %copy-start.30 = (bf16[256,768]{1,0:T(8,128)(2,1)S(1)}, bf16[256,768]{1,0:T(8,128)(2,1)}, u32[]{:S(2)}) copy-start(bf16[256,768]{1,0:T(8,128)(2,1)} %copy-done.29) | copy-start | bytes 1179652
  197.2 12.2 %collective-permute-start.10 = (bf16[256,768]{1,0:T(8,128)(2,1)S(1)}, bf16[256,768]{1,0:T(8,128)(2,1)S(1)}, u32[]{:S(2)}, u32[]{:S(2)}) collective-permute-start(bf16[256,768]{1,0:T(8,128)(2,1)S(1)} %all_gather.3), channel_id=1, source_target_pairs={{0,32},{32,0},{1,33},{33,1},{2,34},{34,2},{3,35},{35,3},{4,36},{36... | collective-permute-start | bytes 1179656 | tf_op jit(solution)/shard_map/ppermute | solution.py:163
  207.1 2.4 %collective-permute-start.11 = (bf16[256,768]{1,0:T(8,128)(2,1)S(1)}, bf16[256,768]{1,0:T(8,128)(2,1)S(1)}, u32[]{:S(2)}, u32[]{:S(2)}) collective-permute-start(bf16[256,768]{1,0:T(8,128)(2,1)S(1)} %get-tuple-element.36), channel_id=1, source_target_pairs={{0,32},{32,0},{1,33},{33,1},{2,34},{34,2},{3,35},{35,3},{4,36},{36... | collective-permute-start | bytes 1179656 | tf_op jit(solution)/shard_map/ppermute | solution.py:163
  208.3 5.1 %collective-permute-start.6 = (bf16[256,768]{1,0:T(8,128)(2,1)S(1)}, bf16[256,768]{1,0:T(8,128)(2,1)S(1)}, u32[]{:S(2)}, u32[]{:S(2)}) collective-permute-start(bf16[256,768]{1,0:T(8,128)(2,1)S(1)} %get-tuple-element.38), channel_id=1, source_target_pairs={{0,32},{32,0},{1,33},{33,1},{2,34},{34,2},{3,35},{35,3},{4,36},{36... | collective-permute-start | bytes 1179656 | tf_op jit(solution)/shard_map/ppermute | solution.py:163
  208.9 4.5 %collective-permute-start.8 = (bf16[256,768]{1,0:T(8,128)(2,1)S(1)}, bf16[256,768]{1,0:T(8,128)(2,1)S(1)}, u32[]{:S(2)}, u32[]{:S(2)}) collective-permute-start(bf16[256,768]{1,0:T(8,128)(2,1)S(1)} %bitcast.62), channel_id=1, source_target_pairs={{0,32},{32,0},{1,33},{33,1},{2,34},{34,2},{3,35},{35,3},{4,36},{36... | collective-permute-start | bytes 1179656 | tf_op jit(solution)/shard_map/ppermute | solution.py:163
  209.0 4.4 %collective-permute-start.7 = (bf16[256,768]{1,0:T(8,128)(2,1)S(1)}, bf16[256,768]{1,0:T(8,128)(2,1)S(1)}, u32[]{:S(2)}, u32[]{:S(2)}) collective-permute-start(bf16[256,768]{1,0:T(8,128)(2,1)S(1)} %bitcast.65), channel_id=1, source_target_pairs={{0,32},{32,0},{1,33},{33,1},{2,34},{34,2},{3,35},{35,3},{4,36},{36... | collective-permute-start | bytes 1179656 | tf_op jit(solution)/shard_map/ppermute | solution.py:163
  209.5 4.0 %copy-start.23 = (bf16[256,768]{1,0:T(8,128)(2,1)S(1)}, bf16[256,768]{1,0:T(8,128)(2,1)}, u32[]{:S(2)}) copy-start(bf16[256,768]{1,0:T(8,128)(2,1)} %copy-done.22) | copy-start | bytes 1179652
  209.5 4.0 %copy-start.28 = (bf16[256,768]{1,0:T(8,128)(2,1)S(1)}, bf16[256,768]{1,0:T(8,128)(2,1)}, u32[]{:S(2)}) copy-start(bf16[256,768]{1,0:T(8,128)(2,1)} %copy-done.27) | copy-start | bytes 1179652
  213.4 2.9 %copy-start.21 = (f32[8,1536]{1,0:T(8,128)S(1)}, f32[8,1536]{1,0:T(8,128)}, u32[]{:S(2)}) copy-start(f32[8,1536]{1,0:T(8,128)} %copy-done.20) | copy-start | bytes 147460
  216.4 1.3 collective-permute-start.12
  (1 other events, 0.7 us)

commit v3 on v2

--- a/solution.py
+++ b/solution.py
@@ -184,10 +184,11 @@
         other = lax.dynamic_index_in_dim(cut, 1 - core, 1, keepdims=False)
         return own, other
 
-    def own_rows(full):
-        own, other = halves(full)
-        mine = lax.dynamic_index_in_dim(own, place, 0, keepdims=False)
-        theirs = lax.dynamic_index_in_dim(other, place, 0, keepdims=False)
+    def own_rows(*terms):
+        first = 2 * eight * place
+        pair = sum(lax.dynamic_slice_in_dim(full, first, 2 * eight, 0) for full in terms)
+        mine = lax.dynamic_slice_in_dim(pair, eight * core, eight, 0)
+        theirs = lax.dynamic_slice_in_dim(pair, eight * (1 - core), eight, 0)
         return jnp.concatenate([mine, swap(theirs)], axis=1)
 
     def rounded_halves(full):
@@ -220,10 +221,22 @@
     inner_one = exchange(inner_one, "y").reshape(half, deep)
 
     part = widen(dot_t, inner_one, w_up, up_other)
-    grad_one, error_one = sum_and_copy(
-        exchange(part.reshape(n_h, eight, 2 * wide), HIDDEN), own_rows(target_one + target_two)
-    )
+    landed = exchange(part.reshape(n_h, eight, 2 * wide), HIDDEN)
+    act_one = lax.all_gather(act_one, "y", axis=0, tiled=True)
+    landed, act_one = lax.optimization_barrier((landed, act_one))
+    grad_one, error_one = sum_and_copy(landed, own_rows(target_one, target_two))
     error_one = exchange(error_one, HIDDEN).reshape(half, 2 * wide)
+    grad_up = t_dot(
+        jnp.concatenate([input_one[:, :wide], swap(input_one[:, wide:])], axis=0),
+        jnp.concatenate([inner_one, swap(inner_one)], axis=0),
+    )
+    grad_down = t_dot(
+        jnp.concatenate([act_one, swap(act_one)], axis=0), jnp.concatenate([two_own, two_other], axis=0)
+    )
+    act_zero_other = swap(act_zero)
+    error_one, grad_up, grad_down, act_zero_other = lax.optimization_barrier(
+        (error_one, grad_up, grad_down, act_zero_other)
+    )
 
     back_part = narrow(dot_t, error_one, w_down, down_other)
     inner_zero = back_through(exchange(back_part.reshape(n_y, quarter, deep), "y"), pre_zero)
@@ -232,14 +245,13 @@
     part = widen(dot_t, inner_zero, w_up, up_other)
     landed = exchange(part.reshape(n_h, eight, 2 * wide), HIDDEN)
 
-    act_one = lax.all_gather(act_one, "y", axis=0, tiled=True)
-    grad_down = t_dot(
-        jnp.concatenate([act_zero, swap(act_zero), act_one, swap(act_one)], axis=0),
-        jnp.concatenate([error_one[:, :wide], swap(error_one[:, wide:]), two_own, two_other], axis=0),
-    )
-    grad_up = t_dot(
-        jnp.concatenate([start_own, start_other, input_one[:, :wide], swap(input_one[:, wide:])], axis=0),
-        jnp.concatenate([inner_zero, swap(inner_zero), inner_one, swap(inner_one)], axis=0),
+    grad_down = grad_down + t_dot(
+        jnp.concatenate([act_zero, act_zero_other], axis=0),
+        jnp.concatenate([error_one[:, :wide], swap(error_one[:, wide:])], axis=0),
+    )
+    grad_up = grad_up + t_dot(
+        jnp.concatenate([start_own, start_other], axis=0),
+        jnp.concatenate([inner_zero, swap(inner_zero)], axis=0),
     )
     landed, grad_up, grad_down = lax.optimization_barrier((landed, grad_up, grad_down))
 

time: 219 us -> 224 us (1.023)
  blocking collectives: 79.6 us -> 69.3 us
  waiting for transfers between devices: 27.3 us -> 32.4 us
  local copies, waits for them, and re-layouts: 9.59 us -> 13.3 us
  starting transfers between devices: 77.4 us -> 80.3 us
    all_to_all x6, blocking collectives: 69.5 us -> 57.9 us  [exchange(): return lax.all_to_all(parts, axes, 0, 0, tiled=True)]
    all_to_all x5, starting transfers between devices: 34.6 us -> 43.5 us  [exchange(): return lax.all_to_all(parts, axes, 0, 0, tiled=True)]
    ppermute x13, starting transfers between devices: 42.8 us -> 36.8 us  [swap(): return lax.ppermute(block, 'core', [(0, 1), (1, 0)])]
    all_to_all x5, waiting for transfers between devices: 21.5 us -> 24.5 us  [exchange(): return lax.all_to_all(parts, axes, 0, 0, tiled=True)]
    unnamed x62 -> x64, local copies, waits for them, and re-layouts: 4.54 us -> 6.96 us
    dot_general x2 -> x4, matrix products: 6.8 us -> 7.19 us  [t_dot(): lax.dot_general(a, b, (((0,), (0,)), ((), ())), preferred_element_type=f32)]
  transfers between devices with their start and end apart: 18 -> 18, of which waited for: 8 -> 11; matrix products, arithmetic and copies ran while one was open for 7% -> 9% of each run, Pallas kernels for 1% -> 0%
where the time goes in v3:
time: 224 us; the launch traced here: 223 us
  starting transfers between devices  80.3 us (36%)
  blocking collectives  69.3 us (31%)
  waiting for transfers between devices  32.4 us (14%)
  local copies, waits for them, and re-layouts  13.3 us (6%)
  Pallas kernels  10.8 us (5%)
  matrix products  9.9 us (4%)
  other arithmetic  5.53 us (2%)
    all_to_all x6, blocking collectives, exchange(): return lax.all_to_all(parts, axes, 0, 0, tiled=True)  57.9 us
    all_to_all x5, starting transfers between devices, exchange(): return lax.all_to_all(parts, axes, 0, 0, tiled=True)  43.5 us
    ppermute x13, starting transfers between devices, swap(): return lax.ppermute(block, 'core', [(0, 1), (1, 0)])  36.8 us
    all_to_all x5, waiting for transfers between devices, exchange(): return lax.all_to_all(parts, axes, 0, 0, tiled=True)  24.5 us
    all_gather x1, blocking collectives, shards(): act_one = lax.all_gather(act_one, 'y', axis=0, tiled=True)  11.4 us
    pallas_call x11, Pallas kernels, call(): pl.pallas_call(body, out_shape=[jax.ShapeDtypeStruct(s, t) for s, t in ou...  10.8 us
    ppermute x13, waiting for transfers between devices, swap(): return lax.ppermute(block, 'core', [(0, 1), (1, 0)])  7.86 us
    dot_general x4, matrix products, t_dot(): lax.dot_general(a, b, (((0,), (0,)), ((), ())), preferred_element_type=f32)  7.19 us
  transfers between devices with their start and end apart: 18, of which 11 were waited for; matrix products, arithmetic and copies ran while one was open for 9% of the time, Pallas kernels for 0%

profile of v3, /device:TPU:1, one launch (start us, length us, event | category | flops | bytes accessed | tf_op | source)
XLA Modules:
  0.0 222.6 jit_solution(13698020760455933171)
XLA Ops:
  0.7 1.6 fusion.29
  2.9 3.3 %collective-permute-start = (bf16[256,768]{1,0:T(8,128)(2,1)S(1)}, bf16[256,768]{1,0:T(8,128)(2,1)S(1)}, u32[]{:S(2)}, u32[]{:S(2)}) collective-permute-start(bf16[256,768]{1,0:T(8,128)(2,1)S(1)} %convolution_convert_fusion.1), channel_id=1, source_target_pairs={{0,32},{32,0},{1,33},{33,1},{2,34},{34,2},{3,35},{35,3},{4,36},{36... | collective-permute-start | bytes 1179656 | tf_op jit(solution)/shard_map/ppermute | solution.py:163
  6.3 1.2 collective-permute-done
  8.0 10.1 %all_to_all.55.l_ref = bf16[4,64,768]{2,1,0:T(8,128)(2,1)S(1)} all-to-all(bf16[4,64,768]{2,1,0:T(8,128)(2,1)S(1)} %bitcast.43), channel_id=1, replica_groups=mesh['y'=4,'core'=2,'x'=4,'z'=8] {'y'}, dimensions={0} | all-to-all | bytes 786432 | tf_op jit(solution)/shard_map/all_to_all | solution.py:167
  18.2 8.8 %all_to_all.56 = bf16[4,64,768]{2,1,0:T(8,128)(2,1)S(1)} all-to-all(bf16[4,64,768]{2,1,0:T(8,128)(2,1)S(1)} %get-tuple-element.21), channel_id=1, replica_groups=mesh['y'=4,'core'=2,'x'=4,'z'=8] {'y'}, dimensions={0} | all-to-all | bytes 786432 | tf_op jit(solution)/shard_map/all_to_all | solution.py:167
  27.1 1.7 shard_map.77
  28.8 10.2 %all-to-all-start.2 = ((bf16[32,8,1536]{2,1,0:T(8,128)(2,1)}), bf16[32,8,1536]{2,1,0:T(8,128)(2,1)S(1)}, u32[]{:S(2)}, u32[]{:S(2)}) async-start(bf16[32,8,1536]{2,1,0:T(8,128)(2,1)} %bitcast.5), calls=%async_computation.2 | async-start | bytes 1572864 | tf_op jit(solution)/shard_map/all_to_all | solution.py:167
  39.0 0.9 constant_dynamic-slice_fusion.3
  39.9 3.3 %collective-permute-start.2 = (f32[8,768]{1,0:T(8,128)S(1)}, f32[8,768]{1,0:T(8,128)S(1)}, u32[]{:S(2)}, u32[]{:S(2)}) collective-permute-start(f32[8,768]{1,0:T(8,128)S(1)} %get-tuple-element.40), channel_id=1, source_target_pairs={{0,32},{32,0},{1,33},{33,1},{2,34},{34,2},{3,35},{35,3},{4,36},{36... | collective-permute-start | bytes 73736 | tf_op jit(solution)/shard_map/ppermute | solution.py:163
  43.2 0.8 collective-permute-done.2
  44.1 11.4 %all-to-all-done.2.l_ref = bf16[32,8,1536]{2,1,0:T(8,128)(2,1)S(1)} async-done(((bf16[32,8,1536]{2,1,0:T(8,128)(2,1)}), bf16[32,8,1536]{2,1,0:T(8,128)(2,1)S(1)}, u32[]{:S(2)}, u32[]{:S(2)}) %all-to-all-start.2) | async-done | bytes 786464 | tf_op jit(solution)/shard_map/all_to_all | solution.py:167
  56.3 0.9 copy-done.13
  57.2 8.7 %all-to-all-start.3 = ((bf16[32,8,1536]{2,1,0:T(8,128)(2,1)}), bf16[32,8,1536]{2,1,0:T(8,128)(2,1)}, u32[]{:S(2)}, u32[]{:S(2)}) async-start(bf16[32,8,1536]{2,1,0:T(8,128)(2,1)} %copy-done.13), calls=%async_computation.3 | async-start | bytes 1572864 | tf_op jit(solution)/shard_map/all_to_all | solution.py:167
  65.9 4.0 %collective-permute-start.3 = (bf16[768,768]{1,0:T(8,128)(2,1)S(1)}, bf16[768,768]{1,0:T(8,128)(2,1)S(1)}, u32[]{:S(2)}, u32[]{:S(2)}) collective-permute-start(bf16[768,768]{1,0:T(8,128)(2,1)S(1)} %copy-done), channel_id=1, source_target_pairs={{0,32},{32,0},{1,33},{33,1},{2,34},{34,2},{3,35},{35,3},{4,36},{36... | collective-permute-start | bytes 3538952 | tf_op jit(solution)/shard_map/ppermute | solution.py:163
  69.9 1.4 fusion.31
  72.0 1.7 collective-permute-done.4
  73.7 1.3 add_convert_fusion
  75.0 6.8 %all-to-all-done.3 = bf16[32,8,1536]{2,1,0:T(8,128)(2,1)} async-done(((bf16[32,8,1536]{2,1,0:T(8,128)(2,1)}), bf16[32,8,1536]{2,1,0:T(8,128)(2,1)}, u32[]{:S(2)}, u32[]{:S(2)}) %all-to-all-start.3) | async-done | bytes 786464 | tf_op jit(solution)/shard_map/all_to_all | solution.py:167
  81.8 2.0 shard_map.79
  83.8 10.7 %all_to_all.57.l_ref = bf16[4,64,1536]{2,1,0:T(8,128)(2,1)S(1)} all-to-all(bf16[4,64,1536]{2,1,0:T(8,128)(2,1)S(1)} %pad_maximum_fusion), channel_id=1, replica_groups=mesh['y'=4,'core'=2,'x'=4,'z'=8] {'y'}, dimensions={0} | all-to-all | bytes 1572864 | tf_op jit(solution)/shard_map/all_to_all | solution.py:167
  95.5 9.7 %all_to_all.58 = bf16[4,64,768]{2,1,0:T(8,128)(2,1)S(1)} all-to-all(bf16[4,64,768]{2,1,0:T(8,128)(2,1)S(1)} %get-tuple-element.23), channel_id=1, replica_groups=mesh['y'=4,'core'=2,'x'=4,'z'=8] {'y'}, dimensions={0} | all-to-all | bytes 786432 | tf_op jit(solution)/shard_map/all_to_all | solution.py:167
  106.0 0.9 copy-done.4
  106.9 7.4 %all-to-all-start.6 = ((bf16[32,8,1536]{2,1,0:T(8,128)(2,1)}), bf16[32,8,1536]{2,1,0:T(8,128)(2,1)}, u32[]{:S(2)}, u32[]{:S(2)}) async-start(bf16[32,8,1536]{2,1,0:T(8,128)(2,1)} %bitcast.30), calls=%async_computation.6 | async-start | bytes 1572864 | tf_op jit(solution)/shard_map/all_to_all | solution.py:167
  115.2 7.5 %collective-permute-start.5 = (f32[8,768]{1,0:T(8,128)S(1)}, f32[8,768]{1,0:T(8,128)S(1)}, u32[]{:S(2)}, u32[]{:S(2)}) collective-permute-start(f32[8,768]{1,0:T(8,128)S(1)} %get-tuple-element.50), channel_id=1, source_target_pairs={{0,32},{32,0},{1,33},{33,1},{2,34},{34,2},{3,35},{35,3},{4,36},{36... | collective-permute-start | bytes 73736 | tf_op jit(solution)/shard_map/ppermute | solution.py:163
  122.7 0.8 collective-permute-done.5
  124.2 11.4 %all_gather.3 = bf16[256,768]{1,0:T(8,128)(2,1)} all-gather(bf16[64,768]{1,0:T(8,128)(2,1)} %copy-done.17), channel_id=1, replica_groups=mesh['y'=4,'core'=2,'x'=4,'z'=8] {'y'}, dimensions={0}, use_global_device_ids=true | all-gather | bytes 491520 | tf_op jit(solution)/shard_map/all_gather | solution.py:225
  136.4 1.3 shard_map.82
  137.7 0.9 copy-done.12
  139.2 9.3 %all-to-all-start.7 = ((bf16[32,8,1536]{2,1,0:T(8,128)(2,1)}), bf16[32,8,1536]{2,1,0:T(8,128)(2,1)}, u32[]{:S(2)}, u32[]{:S(2)}) async-start(bf16[32,8,1536]{2,1,0:T(8,128)(2,1)} %copy-done.12), calls=%async_computation.7 | async-start | bytes 1572864 | tf_op jit(solution)/shard_map/all_to_all | solution.py:167
  148.5 1.3 fusion.37
  149.8 3.0 %collective-permute-start.6 = (bf16[256,768]{1,0:T(8,128)(2,1)S(1)}, bf16[256,768]{1,0:T(8,128)(2,1)S(1)}, u32[]{:S(2)}, u32[]{:S(2)}) collective-permute-start(bf16[256,768]{1,0:T(8,128)(2,1)S(1)} %get-tuple-element.48), channel_id=1, source_target_pairs={{0,32},{32,0},{1,33},{33,1},{2,34},{34,2},{3,35},{35,3},{4,36},{36... | collective-permute-start | bytes 1179656 | tf_op jit(solution)/shard_map/ppermute | solution.py:163
  154.7 2.2 fusion
  156.9 2.2 fusion.7
  159.1 6.2 %all-to-all-done.7 = bf16[32,8,1536]{2,1,0:T(8,128)(2,1)} async-done(((bf16[32,8,1536]{2,1,0:T(8,128)(2,1)}), bf16[32,8,1536]{2,1,0:T(8,128)(2,1)}, u32[]{:S(2)}, u32[]{:S(2)}) %all-to-all-start.7) | async-done | bytes 786464 | tf_op jit(solution)/shard_map/all_to_all | solution.py:167
  165.4 1.3 copy-done.3
  166.6 2.0 shard_map.83
  168.6 9.3 %all_to_all.59.l_ref = bf16[4,64,768]{2,1,0:T(8,128)(2,1)S(1)} all-to-all(bf16[4,64,768]{2,1,0:T(8,128)(2,1)S(1)} %bitcast.41), channel_id=1, replica_groups=mesh['y'=4,'core'=2,'x'=4,'z'=8] {'y'}, dimensions={0} | all-to-all | bytes 786432 | tf_op jit(solution)/shard_map/all_to_all | solution.py:167
  178.1 9.2 %all_to_all.60 = bf16[4,64,768]{2,1,0:T(8,128)(2,1)S(1)} all-to-all(bf16[4,64,768]{2,1,0:T(8,128)(2,1)S(1)} %shard_map.84), channel_id=1, replica_groups=mesh['y'=4,'core'=2,'x'=4,'z'=8] {'y'}, dimensions={0} | all-to-all | bytes 786432 | tf_op jit(solution)/shard_map/all_to_all | solution.py:167
  187.3 1.7 shard_map.85
  189.1 7.9 %all-to-all-start.10 = ((bf16[32,8,1536]{2,1,0:T(8,128)(2,1)}), bf16[32,8,1536]{2,1,0:T(8,128)(2,1)S(1)}, u32[]{:S(2)}, u32[]{:S(2)}) async-start(bf16[32,8,1536]{2,1,0:T(8,128)(2,1)} %bitcast.17), calls=%async_computation.10 | async-start | bytes 1572864 | tf_op jit(solution)/shard_map/all_to_all | solution.py:167
  197.0 1.2 fusion.36
  198.1 6.0 %collective-permute-start.11 = (bf16[256,768]{1,0:T(8,128)(2,1)S(1)}, bf16[256,768]{1,0:T(8,128)(2,1)S(1)}, u32[]{:S(2)}, u32[]{:S(2)}) collective-permute-start(bf16[256,768]{1,0:T(8,128)(2,1)S(1)} %get-tuple-element.46), channel_id=1, source_target_pairs={{0,32},{32,0},{1,33},{33,1},{2,34},{34,2},{3,35},{35,3},{4,36},{36... | collective-permute-start | bytes 1179656 | tf_op jit(solution)/shard_map/ppermute | solution.py:163
  204.2 1.2 collective-permute-done.11
  205.5 2.0 fusion.21
  207.5 1.7 add.55
  210.9 1.7 add.54
  212.7 8.5 %collective-permute-start.12 = (f32[8,768]{1,0:T(8,128)S(1)}, f32[8,768]{1,0:T(8,128)S(1)}, u32[]{:S(2)}, u32[]{:S(2)}) collective-permute-start(f32[8,768]{1,0:T(8,128)S(1)} %get-tuple-element.36), channel_id=1, source_target_pairs={{0,32},{32,0},{1,33},{33,1},{2,34},{34,2},{3,35},{35,3},{4,36},{36... | collective-permute-start | bytes 73736 | tf_op jit(solution)/shard_map/ppermute | solution.py:163
  221.2 0.8 collective-permute-done.12
  (91 shorter events, 12.0 us)
Async XLA Ops:
  0.6 1.7 copy-start
  0.6 5.5 %copy-start.1 = (bf16[768,768]{1,0:T(8,128)(2,1)S(1)}, bf16[768,768]{1,0:T(8,128)(2,1)}, u32[]{:S(2)}) copy-start(bf16[768,768]{1,0:T(8,128)(2,1)} %a_ref.8) | copy-start | bytes 3538948
  2.3 5.8 %copy-start.22 = (bf16[256,768]{1,0:T(8,128)(2,1)}, bf16[256,768]{1,0:T(8,128)(2,1)S(1)}, u32[]{:S(2)}) copy-start(bf16[256,768]{1,0:T(8,128)(2,1)S(1)} %get-tuple-element.42) | copy-start | bytes 1179652
  2.3 5.8 %copy-start.27 = (bf16[256,768]{1,0:T(8,128)(2,1)}, bf16[256,768]{1,0:T(8,128)(2,1)S(1)}, u32[]{:S(2)}) copy-start(bf16[256,768]{1,0:T(8,128)(2,1)S(1)} %get-tuple-element.41) | copy-start | bytes 1179652
  2.9 4.7 %collective-permute-start = (bf16[256,768]{1,0:T(8,128)(2,1)S(1)}, bf16[256,768]{1,0:T(8,128)(2,1)S(1)}, u32[]{:S(2)}, u32[]{:S(2)}) collective-permute-start(bf16[256,768]{1,0:T(8,128)(2,1)S(1)} %convolution_convert_fusion.1), channel_id=1, source_target_pairs={{0,32},{32,0},{1,33},{33,1},{2,34},{34,2},{3,35},{35,3},{4,36},{36... | collective-permute-start | bytes 1179656 | tf_op jit(solution)/shard_map/ppermute | solution.py:163
  6.2 20.9 %collective-permute-start.1 = (bf16[768,768]{1,0:T(8,128)(2,1)S(1)}, bf16[768,768]{1,0:T(8,128)(2,1)S(1)}, u32[]{:S(2)}, u32[]{:S(2)}) collective-permute-start(bf16[768,768]{1,0:T(8,128)(2,1)S(1)} %copy-done.1), channel_id=1, source_target_pairs={{0,32},{32,0},{1,33},{33,1},{2,34},{34,2},{3,35},{35,3},{4,36},{36... | collective-permute-start | bytes 3538952 | tf_op jit(solution)/shard_map/ppermute | solution.py:163
  18.2 8.9 %copy-start.15 = (bf16[64,768]{1,0:T(8,128)(2,1)}, bf16[64,768]{1,0:T(8,128)(2,1)S(1)}, u32[]{:S(2)}) copy-start(bf16[64,768]{1,0:T(8,128)(2,1)S(1)} %get-tuple-element.29.p_ref) | copy-start | bytes 294916
  27.1 1.7 copy-start.5
  27.1 1.7 copy-start.2
  28.8 26.8 %all-to-all-start.2 = ((bf16[32,8,1536]{2,1,0:T(8,128)(2,1)}), bf16[32,8,1536]{2,1,0:T(8,128)(2,1)S(1)}, u32[]{:S(2)}, u32[]{:S(2)}) async-start(bf16[32,8,1536]{2,1,0:T(8,128)(2,1)} %bitcast.5), calls=%async_computation.2 | async-start | bytes 1572864 | tf_op jit(solution)/shard_map/all_to_all | solution.py:167
  39.9 4.2 %collective-permute-start.2 = (f32[8,768]{1,0:T(8,128)S(1)}, f32[8,768]{1,0:T(8,128)S(1)}, u32[]{:S(2)}, u32[]{:S(2)}) collective-permute-start(f32[8,768]{1,0:T(8,128)S(1)} %get-tuple-element.40), channel_id=1, source_target_pairs={{0,32},{32,0},{1,33},{33,1},{2,34},{34,2},{3,35},{35,3},{4,36},{36... | collective-permute-start | bytes 73736 | tf_op jit(solution)/shard_map/ppermute | solution.py:163
  56.3 0.9 copy-start.13
  57.2 24.6 %all-to-all-start.3 = ((bf16[32,8,1536]{2,1,0:T(8,128)(2,1)}), bf16[32,8,1536]{2,1,0:T(8,128)(2,1)}, u32[]{:S(2)}, u32[]{:S(2)}) async-start(bf16[32,8,1536]{2,1,0:T(8,128)(2,1)} %copy-done.13), calls=%async_computation.3 | async-start | bytes 1572864 | tf_op jit(solution)/shard_map/all_to_all | solution.py:167
  65.9 9.1 %collective-permute-start.3 = (bf16[768,768]{1,0:T(8,128)(2,1)S(1)}, bf16[768,768]{1,0:T(8,128)(2,1)S(1)}, u32[]{:S(2)}, u32[]{:S(2)}) collective-permute-start(bf16[768,768]{1,0:T(8,128)(2,1)S(1)} %copy-done), channel_id=1, source_target_pairs={{0,32},{32,0},{1,33},{33,1},{2,34},{34,2},{3,35},{35,3},{4,36},{36... | collective-permute-start | bytes 3538952 | tf_op jit(solution)/shard_map/ppermute | solution.py:163
  71.3 3.6 %copy-start.24 = (bf16[256,768]{1,0:T(8,128)(2,1)}, bf16[256,768]{1,0:T(8,128)(2,1)S(1)}, u32[]{:S(2)}) copy-start(bf16[256,768]{1,0:T(8,128)(2,1)S(1)} %get-tuple-element.44) | copy-start | bytes 1179652
  71.4 3.6 %copy-start.29 = (bf16[256,768]{1,0:T(8,128)(2,1)}, bf16[256,768]{1,0:T(8,128)(2,1)S(1)}, u32[]{:S(2)}) copy-start(bf16[256,768]{1,0:T(8,128)(2,1)S(1)} %get-tuple-element.43) | copy-start | bytes 1179652
  71.9 1.8 collective-permute-start.4
  81.8 2.0 copy-start.26
  105.2 0.8 copy-start.8
  106.0 0.9 copy-start.4
  106.9 28.7 %all-to-all-start.6 = ((bf16[32,8,1536]{2,1,0:T(8,128)(2,1)}), bf16[32,8,1536]{2,1,0:T(8,128)(2,1)}, u32[]{:S(2)}, u32[]{:S(2)}) async-start(bf16[32,8,1536]{2,1,0:T(8,128)(2,1)} %bitcast.30), calls=%async_computation.6 | async-start | bytes 1572864 | tf_op jit(solution)/shard_map/all_to_all | solution.py:167
  115.2 8.4 %collective-permute-start.5 = (f32[8,768]{1,0:T(8,128)S(1)}, f32[8,768]{1,0:T(8,128)S(1)}, u32[]{:S(2)}, u32[]{:S(2)}) collective-permute-start(f32[8,768]{1,0:T(8,128)S(1)} %get-tuple-element.50), channel_id=1, source_target_pairs={{0,32},{32,0},{1,33},{33,1},{2,34},{34,2},{3,35},{35,3},{4,36},{36... | collective-permute-start | bytes 73736 | tf_op jit(solution)/shard_map/ppermute | solution.py:163
  135.6 0.8 copy-start.14
  137.7 0.9 copy-start.12
  139.2 26.2 %all-to-all-start.7 = ((bf16[32,8,1536]{2,1,0:T(8,128)(2,1)}), bf16[32,8,1536]{2,1,0:T(8,128)(2,1)}, u32[]{:S(2)}, u32[]{:S(2)}) async-start(bf16[32,8,1536]{2,1,0:T(8,128)(2,1)} %copy-done.12), calls=%async_computation.7 | async-start | bytes 1572864 | tf_op jit(solution)/shard_map/all_to_all | solution.py:167
  148.5 4.3 %copy-start.9 = (bf16[4,64,768]{2,1,0:T(8,128)(2,1)S(1)}, bf16[4,64,768]{2,1,0:T(8,128)(2,1)}, u32[]{:S(2)}) copy-start(bf16[4,64,768]{2,1,0:T(8,128)(2,1)} %copy-done.8) | copy-start | bytes 1179652
  148.5 4.4 %copy-start.31 = (bf16[256,768]{1,0:T(8,128)(2,1)S(1)}, bf16[256,768]{1,0:T(8,128)(2,1)}, u32[]{:S(2)}) copy-start(bf16[256,768]{1,0:T(8,128)(2,1)} %all_gather.3) | copy-start | bytes 1179652
  148.5 4.8 %copy-start.6 = (bf16[4,64,768]{2,1,0:T(8,128)(2,1)S(1)}, bf16[4,64,768]{2,1,0:T(8,128)(2,1)}, u32[]{:S(2)}) copy-start(bf16[4,64,768]{2,1,0:T(8,128)(2,1)} %copy-done.5) | copy-start | bytes 1179652
  149.8 4.4 %collective-permute-start.6 = (bf16[256,768]{1,0:T(8,128)(2,1)S(1)}, bf16[256,768]{1,0:T(8,128)(2,1)S(1)}, u32[]{:S(2)}, u32[]{:S(2)}) collective-permute-start(bf16[256,768]{1,0:T(8,128)(2,1)S(1)} %get-tuple-element.48), channel_id=1, source_target_pairs={{0,32},{32,0},{1,33},{33,1},{2,34},{34,2},{3,35},{35,3},{4,36},{36... | collective-permute-start | bytes 1179656 | tf_op jit(solution)/shard_map/ppermute | solution.py:163
  152.8 1.9 collective-permute-start.7
  152.9 4.0 %collective-permute-start.8 = (bf16[256,768]{1,0:T(8,128)(2,1)S(1)}, bf16[256,768]{1,0:T(8,128)(2,1)S(1)}, u32[]{:S(2)}, u32[]{:S(2)}) collective-permute-start(bf16[256,768]{1,0:T(8,128)(2,1)S(1)} %copy-done.31), channel_id=1, source_target_pairs={{0,32},{32,0},{1,33},{33,1},{2,34},{34,2},{3,35},{35,3},{4,36},{36... | collective-permute-start | bytes 1179656 | tf_op jit(solution)/shard_map/ppermute | solution.py:163
  153.3 5.8 %collective-permute-start.9 = (bf16[256,768]{1,0:T(8,128)(2,1)S(1)}, bf16[256,768]{1,0:T(8,128)(2,1)}, u32[]{:S(2)}, u32[]{:S(2)}) collective-permute-start(bf16[256,768]{1,0:T(8,128)(2,1)S(1)} %bitcast.32), channel_id=1, source_target_pairs={{0,32},{32,0},{1,33},{33,1},{2,34},{34,2},{3,35},{35,3},{4,36},{36... | collective-permute-start | bytes 1179656 | tf_op jit(solution)/shard_map/ppermute | solution.py:163
  154.7 2.2 copy-start.25
  154.7 2.2 copy-start.30
  165.4 1.3 copy-start.3
  166.6 11.3 %copy-start.16 = (bf16[64,768]{1,0:T(8,128)(2,1)S(1)}, bf16[64,768]{1,0:T(8,128)(2,1)}, u32[]{:S(2)}) copy-start(bf16[64,768]{1,0:T(8,128)(2,1)} %copy-done.15) | copy-start | bytes 294916
  187.3 1.7 copy-start.10
  189.1 15.1 %copy-start.11 = (bf16[4,64,768]{2,1,0:T(8,128)(2,1)S(1)}, bf16[4,64,768]{2,1,0:T(8,128)(2,1)}, u32[]{:S(2)}) copy-start(bf16[4,64,768]{2,1,0:T(8,128)(2,1)} %copy-done.10) | copy-start | bytes 1179652
  189.1 16.4 %copy-start.7 = (bf16[4,64,768]{2,1,0:T(8,128)(2,1)S(1)}, bf16[4,64,768]{2,1,0:T(8,128)(2,1)}, u32[]{:S(2)}) copy-start(bf16[4,64,768]{2,1,0:T(8,128)(2,1)} %copy-done.5) | copy-start | bytes 1179652
  189.1 23.5 %all-to-all-start.10 = ((bf16[32,8,1536]{2,1,0:T(8,128)(2,1)}), bf16[32,8,1536]{2,1,0:T(8,128)(2,1)S(1)}, u32[]{:S(2)}, u32[]{:S(2)}) async-start(bf16[32,8,1536]{2,1,0:T(8,128)(2,1)} %bitcast.17), calls=%async_computation.10 | async-start | bytes 1572864 | tf_op jit(solution)/shard_map/all_to_all | solution.py:167
  198.1 7.4 %collective-permute-start.11 = (bf16[256,768]{1,0:T(8,128)(2,1)S(1)}, bf16[256,768]{1,0:T(8,128)(2,1)S(1)}, u32[]{:S(2)}, u32[]{:S(2)}) collective-permute-start(bf16[256,768]{1,0:T(8,128)(2,1)S(1)} %get-tuple-element.46), channel_id=1, source_target_pairs={{0,32},{32,0},{1,33},{33,1},{2,34},{34,2},{3,35},{35,3},{4,36},{36... | collective-permute-start | bytes 1179656 | tf_op jit(solution)/shard_map/ppermute | solution.py:163
  204.1 5.0 %collective-permute-start.10 = (bf16[256,768]{1,0:T(8,128)(2,1)S(1)}, bf16[256,768]{1,0:T(8,128)(2,1)S(1)}, u32[]{:S(2)}, u32[]{:S(2)}) collective-permute-start(bf16[256,768]{1,0:T(8,128)(2,1)S(1)} %bitcast.38), channel_id=1, source_target_pairs={{0,32},{32,0},{1,33},{33,1},{2,34},{34,2},{3,35},{35,3},{4,36},{36... | collective-permute-start | bytes 1179656 | tf_op jit(solution)/shard_map/ppermute | solution.py:163
  205.5 2.0 copy-start.21
  207.5 1.7 copy-start.23
  207.5 1.7 copy-start.28
  209.2 1.7 copy-start.20
  210.9 1.7 copy-start.19
  212.7 9.3 %collective-permute-start.12 = (f32[8,768]{1,0:T(8,128)S(1)}, f32[8,768]{1,0:T(8,128)S(1)}, u32[]{:S(2)}, u32[]{:S(2)}) collective-permute-start(f32[8,768]{1,0:T(8,128)S(1)} %get-tuple-element.36), channel_id=1, source_target_pairs={{0,32},{32,0},{1,33},{33,1},{2,34},{34,2},{3,35},{35,3},{4,36},{36... | collective-permute-start | bytes 73736 | tf_op jit(solution)/shard_map/ppermute | solution.py:163
  (2 other events, 1.3 us)

commit v4 on v3

--- a/solution.py
+++ b/solution.py
@@ -54,11 +54,11 @@
 
 
 def widen(product, rows_deep, own_block, other_block):
-    rows, wide = rows_deep.shape[0], rows_deep.shape[1]
+    rows, wide = rows_deep.shape[0], own_block.shape[0]
 
     def body(x_ref, a_ref, b_ref, o_ref):
-        o_ref[:, :wide] = product(x_ref[...], a_ref[...]).astype(bf16)
-        o_ref[:, wide:] = product(x_ref[...], b_ref[...]).astype(bf16)
+        o_ref[:, :wide] = product(x_ref[:, :wide], a_ref[...]).astype(bf16)
+        o_ref[:, wide:] = product(x_ref[:, :wide], b_ref[...]).astype(bf16)
 
     return call(
         body, [((rows, 2 * wide), bf16)], rows_deep, own_block, other_block, flops=4 * rows * wide * wide
@@ -132,17 +132,19 @@
 def activate_and_back(landed):
     count, rows, deep = landed.shape[0], landed.shape[1], landed.shape[2] // 2
 
-    def body(l_ref, v_ref, c_ref):
+    def body(l_ref, c_ref):
         for cols in strips(deep, 128):
+            far = slice(cols.start + deep, cols.stop + deep)
             pre = add_up(l_ref, cols).astype(bf16)
             value, slope = gelu_parts(pre.astype(f32))
-            v_ref[:, cols] = value.astype(bf16)
-            back = add_up(l_ref, slice(cols.start + deep, cols.stop + deep)).astype(bf16)
+            value = value.astype(bf16)
+            back = add_up(l_ref, far).astype(bf16)
             inner = (back.astype(f32) * slope).astype(bf16)
             for k in range(count):
                 c_ref[k, :, cols] = inner
-
-    return call(body, [((rows, deep), bf16), ((count, rows, deep), bf16)], landed)
+                c_ref[k, :, far] = value
+
+    return call(body, [(landed.shape, bf16)], landed)
 
 
 def back_through(landed, pre):
@@ -198,7 +200,6 @@
     def both_cores(own, other_part):
         return (own + swap(other_part.astype(bf16)).astype(f32)).astype(bf16)
 
-    up_other = swap(w_up)
     down_other = swap(w_down)
 
     start_own, start_other = rounded_halves(start_latent)
@@ -207,36 +208,41 @@
     act_zero = exchange(act_zero, "y").reshape(half, deep)
 
     part = widen(dot, act_zero, w_down, down_other)
-    latent_one, input_one = sum_and_copy(
-        exchange(part.reshape(n_h, eight, 2 * wide), HIDDEN), own_rows(start_latent)
-    )
-    input_one = exchange(input_one, HIDDEN).reshape(half, 2 * wide)
-
+    landed = exchange(part.reshape(n_h, eight, 2 * wide), HIDDEN)
+    up_other = swap(w_up)
     two_own, two_other = rounded_halves(target_two)
     back_part = both_cores(dot_t(two_own, w_down), dot_t(two_other, w_down))
+    start_rows = own_rows(start_latent)
+    target_rows = own_rows(target_one, target_two)
+    landed, up_other, back_part, start_rows, target_rows = lax.optimization_barrier(
+        (landed, up_other, back_part, start_rows, target_rows)
+    )
+    latent_one, input_one = sum_and_copy(landed, start_rows)
+    input_one = exchange(input_one, HIDDEN).reshape(half, 2 * wide)
 
     pre_part = narrow(dot, input_one, w_up, up_other)
     both = jnp.concatenate([pre_part.reshape(n_y, quarter, deep), back_part.reshape(n_y, quarter, deep)], axis=2)
-    act_one, inner_one = activate_and_back(exchange(both, "y"))
-    inner_one = exchange(inner_one, "y").reshape(half, deep)
-
-    part = widen(dot_t, inner_one, w_up, up_other)
+    one = activate_and_back(exchange(both, "y"))
+    one = exchange(one, "y").reshape(half, 2 * deep)
+
+    part = widen(dot_t, one, w_up, up_other)
     landed = exchange(part.reshape(n_h, eight, 2 * wide), HIDDEN)
-    act_one = lax.all_gather(act_one, "y", axis=0, tiled=True)
-    landed, act_one = lax.optimization_barrier((landed, act_one))
-    grad_one, error_one = sum_and_copy(landed, own_rows(target_one, target_two))
+    one_other = swap(one)
+    input_far = swap(input_one[:, wide:])
+    act_zero_other = swap(act_zero)
+    grad_up = t_dot(
+        jnp.concatenate([input_one[:, :wide], input_far], axis=0),
+        jnp.concatenate([one[:, :deep], one_other[:, :deep]], axis=0),
+    )
+    grad_down = t_dot(
+        jnp.concatenate([one[:, deep:], one_other[:, deep:]], axis=0),
+        jnp.concatenate([two_own, two_other], axis=0),
+    )
+    landed, grad_up, grad_down, act_zero_other = lax.optimization_barrier(
+        (landed, grad_up, grad_down, act_zero_other)
+    )
+    grad_one, error_one = sum_and_copy(landed, target_rows)
     error_one = exchange(error_one, HIDDEN).reshape(half, 2 * wide)
-    grad_up = t_dot(
-        jnp.concatenate([input_one[:, :wide], swap(input_one[:, wide:])], axis=0),
-        jnp.concatenate([inner_one, swap(inner_one)], axis=0),
-    )
-    grad_down = t_dot(
-        jnp.concatenate([act_one, swap(act_one)], axis=0), jnp.concatenate([two_own, two_other], axis=0)
-    )
-    act_zero_other = swap(act_zero)
-    error_one, grad_up, grad_down, act_zero_other = lax.optimization_barrier(
-        (error_one, grad_up, grad_down, act_zero_other)
-    )
 
     back_part = narrow(dot_t, error_one, w_down, down_other)
     inner_zero = back_through(exchange(back_part.reshape(n_y, quarter, deep), "y"), pre_zero)

time: 224 us -> 214 us (0.955)
  blocking collectives: 69.3 us -> 111 us
  waiting for transfers between devices: 32.4 us -> 6.52 us
  starting transfers between devices: 80.3 us -> 55.6 us
    all_to_all x6 -> x8, blocking collectives: 57.9 us -> 111 us  [exchange(): return lax.all_to_all(parts, axes, 0, 0, tiled=True)]
    all_to_all x5 -> x3, waiting for transfers between devices: 24.5 us -> 2.39 us  [exchange(): return lax.all_to_all(parts, axes, 0, 0, tiled=True)]
    all_to_all x5 -> x3, starting transfers between devices: 43.5 us -> 22.2 us  [exchange(): return lax.all_to_all(parts, axes, 0, 0, tiled=True)]
    all_gather x1 -> x0, blocking collectives: 11.4 us -> none  [shards(): act_one = lax.all_gather(act_one, 'y', axis=0, tiled=True)]
    ppermute x13 -> x12, waiting for transfers between devices: 7.86 us -> 4.12 us  [swap(): return lax.ppermute(block, 'core', [(0, 1), (1, 0)])]
    ppermute x13 -> x12, starting transfers between devices: 36.8 us -> 33.3 us  [swap(): return lax.ppermute(block, 'core', [(0, 1), (1, 0)])]
    unnamed x64 -> x56, local copies, waits for them, and re-layouts: 6.96 us -> 5.57 us
  transfers between devices with their start and end apart: 18 -> 15, of which waited for: 11 -> 6; matrix products, arithmetic and copies ran while one was open for 9% -> 10% of each run, Pallas kernels for 0% -> 0%
where the time goes in v4:
time: 214 us; the launch traced here: 213 us
  blocking collectives  111 us (52%)
  starting transfers between devices  55.6 us (26%)
  matrix products  11.8 us (6%)
  local copies, waits for them, and re-layouts  11.6 us (5%)
  Pallas kernels  9.71 us (5%)
  waiting for transfers between devices  6.52 us (3%)
  other arithmetic  6.13 us (3%)
    all_to_all x8, blocking collectives, exchange(): return lax.all_to_all(parts, axes, 0, 0, tiled=True)  111 us
    ppermute x12, starting transfers between devices, swap(): return lax.ppermute(block, 'core', [(0, 1), (1, 0)])  33.3 us
    all_to_all x3, starting transfers between devices, exchange(): return lax.all_to_all(parts, axes, 0, 0, tiled=True)  22.2 us
    pallas_call x11, Pallas kernels, call(): pl.pallas_call(body, out_shape=[jax.ShapeDtypeStruct(s, t) for s, t in ou...  9.71 us
    dot_general x4, matrix products, t_dot(): lax.dot_general(a, b, (((0,), (0,)), ((), ())), preferred_element_type=f32)  7.19 us
    unnamed x56, local copies, waits for them, and re-layouts  5.57 us
  transfers between devices with their start and end apart: 15, of which 6 were waited for; matrix products, arithmetic and copies ran while one was open for 10% of the time, Pallas kernels for 0%

profile of v4, /device:TPU:1, one launch (start us, length us, event | category | flops | bytes accessed | tf_op | source)
XLA Modules:
  0.0 212.8 jit_solution(7307728008744359011)
XLA Ops:
  0.7 1.6 fusion.29
  2.9 3.3 %collective-permute-start = (bf16[256,768]{1,0:T(8,128)(2,1)S(1)}, bf16[256,768]{1,0:T(8,128)(2,1)S(1)}, u32[]{:S(2)}, u32[]{:S(2)}) collective-permute-start(bf16[256,768]{1,0:T(8,128)(2,1)S(1)} %convolution_convert_fusion.1), channel_id=1, source_target_pairs={{0,32},{32,0},{1,33},{33,1},{2,34},{34,2},{3,35},{35,3},{4,36},{36... | collective-permute-start | bytes 1179656 | tf_op jit(solution)/shard_map/ppermute | solution.py:165
  6.3 1.2 collective-permute-done
  8.0 10.1 %all_to_all.55.l_ref = bf16[4,64,768]{2,1,0:T(8,128)(2,1)S(1)} all-to-all(bf16[4,64,768]{2,1,0:T(8,128)(2,1)S(1)} %bitcast.47), channel_id=1, replica_groups=mesh['y'=4,'core'=2,'x'=4,'z'=8] {'y'}, dimensions={0} | all-to-all | bytes 786432 | tf_op jit(solution)/shard_map/all_to_all | solution.py:169
  18.2 0.6 copy-done.14
  18.9 8.8 %all_to_all.56 = bf16[4,64,768]{2,1,0:T(8,128)(2,1)S(1)} all-to-all(bf16[4,64,768]{2,1,0:T(8,128)(2,1)S(1)} %get-tuple-element.22), channel_id=1, replica_groups=mesh['y'=4,'core'=2,'x'=4,'z'=8] {'y'}, dimensions={0} | all-to-all | bytes 786432 | tf_op jit(solution)/shard_map/all_to_all | solution.py:169
  27.7 1.7 shard_map.77
  29.4 10.3 %all-to-all-start.2 = ((bf16[32,8,1536]{2,1,0:T(8,128)(2,1)}), bf16[32,8,1536]{2,1,0:T(8,128)(2,1)}, u32[]{:S(2)}, u32[]{:S(2)}) async-start(bf16[32,8,1536]{2,1,0:T(8,128)(2,1)} %bitcast.5), calls=%async_computation.2 | async-start | bytes 1572864 | tf_op jit(solution)/shard_map/all_to_all | solution.py:169
  39.7 3.3 %collective-permute-start.2 = (bf16[768,768]{1,0:T(8,128)(2,1)S(1)}, bf16[768,768]{1,0:T(8,128)(2,1)S(1)}, u32[]{:S(2)}, u32[]{:S(2)}) collective-permute-start(bf16[768,768]{1,0:T(8,128)(2,1)S(1)} %copy-done), channel_id=1, source_target_pairs={{0,32},{32,0},{1,33},{33,1},{2,34},{34,2},{3,35},{35,3},{4,36},{36... | collective-permute-start | bytes 3538952 | tf_op jit(solution)/shard_map/ppermute | solution.py:165
  43.1 2.2 %fusion.31 = (bf16[256,768]{1,0:T(8,128)(2,1)S(1)}, bf16[256,768]{1,0:T(8,128)(2,1)}) fusion(f32[32,2,8,768]{3,2,1,0:T(8,128)} %bitcast.49, s32[]{:T(128)S(6)} %select_n.38, s32[]{:T(128)S(6)} %select_n.37), kind=kLoop, calls=%fused_computation.40 | loop fusion | bytes 1572872 | tf_op jit(solution)/shard_map/convert_element_type | solution.py:198
  45.3 0.8 copy-done.26
  46.0 1.3 convolution_convert_fusion
  47.3 0.9 constant_dynamic-slice_fusion.3
  48.8 0.8 dynamic-slice_add_fusion
  51.5 2.4 %add_convert_fusion = bf16[256,768]{1,0:T(8,128)(2,1)} fusion(bf16[256,768]{1,0:T(8,128)(2,1)} %collective-permute-done.3, bf16[256,768]{1,0:T(8,128)(2,1)} %get-tuple-element.44, bf16[768,768]{1,0:T(8,128)(2,1)S(1)} %copy-done.1), kind=kOutput, calls=%fused_computation.31 | convolution fusion | flops 302579712 | bytes 2359296 | tf_op jit(solution)/shard_map/dot_general | solution.py:35
  53.9 2.4 %all-to-all-done.2.l_ref = bf16[32,8,1536]{2,1,0:T(8,128)(2,1)} async-done(((bf16[32,8,1536]{2,1,0:T(8,128)(2,1)}), bf16[32,8,1536]{2,1,0:T(8,128)(2,1)}, u32[]{:S(2)}, u32[]{:S(2)}) %all-to-all-start.2) | async-done | bytes 786464 | tf_op jit(solution)/shard_map/all_to_all | solution.py:169
  56.3 0.8 copy-done.13
  57.1 1.9 shard_map.78
  58.9 24.3 %all_to_all.57 = bf16[32,8,1536]{2,1,0:T(8,128)(2,1)S(1)} all-to-all(bf16[32,8,1536]{2,1,0:T(8,128)(2,1)S(1)} %get-tuple-element.25), channel_id=1, replica_groups=mesh['y'=4,'core'=2,'x'=4,'z'=8] {'x','z'}, dimensions={0} | all-to-all | bytes 1572864 | tf_op jit(solution)/shard_map/all_to_all | solution.py:169
  83.3 0.8 shard_map.79
  84.6 10.7 %all_to_all.58.l_ref = bf16[4,64,1536]{2,1,0:T(8,128)(2,1)S(1)} all-to-all(bf16[4,64,1536]{2,1,0:T(8,128)(2,1)S(1)} %pad_maximum_fusion), channel_id=1, replica_groups=mesh['y'=4,'core'=2,'x'=4,'z'=8] {'y'}, dimensions={0} | all-to-all | bytes 1572864 | tf_op jit(solution)/shard_map/all_to_all | solution.py:169
  95.6 12.4 %all_to_all.59 = bf16[4,64,1536]{2,1,0:T(8,128)(2,1)S(1)} all-to-all(bf16[4,64,1536]{2,1,0:T(8,128)(2,1)S(1)} %shard_map.80), channel_id=1, replica_groups=mesh['y'=4,'core'=2,'x'=4,'z'=8] {'y'}, dimensions={0} | all-to-all | bytes 1572864 | tf_op jit(solution)/shard_map/all_to_all | solution.py:169
  108.0 0.8 shard_map.81
  108.9 0.9 copy-done.9
  109.8 6.8 %all-to-all-start.6 = ((bf16[32,8,1536]{2,1,0:T(8,128)(2,1)}), bf16[32,8,1536]{2,1,0:T(8,128)(2,1)}, u32[]{:S(2)}, u32[]{:S(2)}) async-start(bf16[32,8,1536]{2,1,0:T(8,128)(2,1)} %bitcast.37), calls=%async_computation.6 | async-start | bytes 1572864 | tf_op jit(solution)/shard_map/all_to_all | solution.py:169
  116.6 8.1 %collective-permute-start.7 = (bf16[256,1536]{1,0:T(8,128)(2,1)}, bf16[256,1536]{1,0:T(8,128)(2,1)S(1)}, u32[]{:S(2)}, u32[]{:S(2)}) collective-permute-start(bf16[256,1536]{1,0:T(8,128)(2,1)} %bitcast.35), channel_id=1, source_target_pairs={{0,32},{32,0},{1,33},{33,1},{2,34},{34,2},{3,35},{35,3},{4,36},{36... | collective-permute-start | bytes 2359304 | tf_op jit(solution)/shard_map/ppermute | solution.py:165
  124.9 1.2 fusion.39
  126.0 0.7 collective-permute-start.6
  127.1 2.2 %fusion.7 = f32[768,768]{1,0:T(8,128)} fusion(bf16[256,768]{1,0:T(8,128)(2,1)S(1)} %get-tuple-element.51, bf16[256,768]{1,0:T(8,128)(2,1)S(1)} %get-tuple-element.49, bf16[256,768]{1,0:T(8,128)(2,1)S(1)} %copy-done.27, bf16[256,768]{1,0:T(8,128)(2,1)S(1)} %copy-done.22), kind=kOutput, calls=%fused_computation.10 | convolution fusion | flops 607125504 | bytes 3932160 | tf_op jit(solution)/shard_map/dot_general | solution.py:39
  129.4 2.2 %fusion = f32[768,768]{1,0:T(8,128)} fusion(bf16[256,768]{1,0:T(8,128)(2,1)S(1)} %collective-permute-done.6, bf16[256,768]{1,0:T(8,128)(2,1)S(1)} %get-tuple-element.53, bf16[256,768]{1,0:T(8,128)(2,1)S(1)} %get-tuple-element.52, bf16[256,768]{1,0:T(8,128)(2,1)S(1)} %get-tuple-element.50), kind=kOutput, calls=%fused_computation.3 | convolution fusion | flops 607125504 | bytes 3932160 | tf_op jit(solution)/shard_map/dot_general | solution.py:39
  131.6 0.8 copy-done.12
  132.4 1.4 shard_map.82
  133.8 25.3 %all_to_all.60 = bf16[32,8,1536]{2,1,0:T(8,128)(2,1)S(1)} all-to-all(bf16[32,8,1536]{2,1,0:T(8,128)(2,1)S(1)} %get-tuple-element.30), channel_id=1, replica_groups=mesh['y'=4,'core'=2,'x'=4,'z'=8] {'x','z'}, dimensions={0} | all-to-all | bytes 1572864 | tf_op jit(solution)/shard_map/all_to_all | solution.py:169
  159.1 0.8 shard_map.83
  160.0 8.6 %all_to_all.61.l_ref = bf16[4,64,768]{2,1,0:T(8,128)(2,1)S(1)} all-to-all(bf16[4,64,768]{2,1,0:T(8,128)(2,1)S(1)} %bitcast.45), channel_id=1, replica_groups=mesh['y'=4,'core'=2,'x'=4,'z'=8] {'y'}, dimensions={0} | all-to-all | bytes 786432 | tf_op jit(solution)/shard_map/all_to_all | solution.py:169
  168.8 10.2 %all_to_all.62 = bf16[4,64,768]{2,1,0:T(8,128)(2,1)S(1)} all-to-all(bf16[4,64,768]{2,1,0:T(8,128)(2,1)S(1)} %shard_map.84), channel_id=1, replica_groups=mesh['y'=4,'core'=2,'x'=4,'z'=8] {'y'}, dimensions={0} | all-to-all | bytes 786432 | tf_op jit(solution)/shard_map/all_to_all | solution.py:169
  179.1 1.7 shard_map.85
  180.8 5.1 %all-to-all-start.10 = ((bf16[32,8,1536]{2,1,0:T(8,128)(2,1)}), bf16[32,8,1536]{2,1,0:T(8,128)(2,1)S(1)}, u32[]{:S(2)}, u32[]{:S(2)}) async-start(bf16[32,8,1536]{2,1,0:T(8,128)(2,1)} %bitcast.17), calls=%async_computation.10 | async-start | bytes 1572864 | tf_op jit(solution)/shard_map/all_to_all | solution.py:169
  185.9 9.8 %collective-permute-start.10 = (bf16[256,768]{1,0:T(8,128)(2,1)S(1)}, bf16[256,768]{1,0:T(8,128)(2,1)S(1)}, u32[]{:S(2)}, u32[]{:S(2)}) collective-permute-start(bf16[256,768]{1,0:T(8,128)(2,1)S(1)} %get-tuple-element.48), channel_id=1, source_target_pairs={{0,32},{32,0},{1,33},{33,1},{2,34},{34,2},{3,35},{35,3},{4,36},{36... | collective-permute-start | bytes 1179656 | tf_op jit(solution)/shard_map/ppermute | solution.py:165
  195.8 1.2 collective-permute-done.10
  197.1 2.0 fusion.21
  199.1 1.7 add.55
  200.8 0.8 fusion.14
  201.6 0.8 copy-done.19
  202.4 1.7 add.54
  204.3 7.1 %collective-permute-start.11 = (f32[8,768]{1,0:T(8,128)S(1)}, f32[8,768]{1,0:T(8,128)S(1)}, u32[]{:S(2)}, u32[]{:S(2)}) collective-permute-start(f32[8,768]{1,0:T(8,128)S(1)} %get-tuple-element.38), channel_id=1, source_target_pairs={{0,32},{32,0},{1,33},{33,1},{2,34},{34,2},{3,35},{35,3},{4,36},{36... | collective-permute-start | bytes 73736 | tf_op jit(solution)/shard_map/ppermute | solution.py:165
  211.3 0.8 collective-permute-done.11
  212.2 0.6 maximum_select_fusion
  (80 shorter events, 5.8 us)
Async XLA Ops:
  0.6 1.7 copy-start
  0.6 5.5 %copy-start.1 = (bf16[768,768]{1,0:T(8,128)(2,1)S(1)}, bf16[768,768]{1,0:T(8,128)(2,1)}, u32[]{:S(2)}) copy-start(bf16[768,768]{1,0:T(8,128)(2,1)} %a_ref.8) | copy-start | bytes 3538948
  2.3 5.8 %copy-start.20 = (bf16[256,768]{1,0:T(8,128)(2,1)}, bf16[256,768]{1,0:T(8,128)(2,1)S(1)}, u32[]{:S(2)}) copy-start(bf16[256,768]{1,0:T(8,128)(2,1)S(1)} %get-tuple-element.46) | copy-start | bytes 1179652
  2.3 5.8 %copy-start.24 = (bf16[256,768]{1,0:T(8,128)(2,1)}, bf16[256,768]{1,0:T(8,128)(2,1)S(1)}, u32[]{:S(2)}) copy-start(bf16[256,768]{1,0:T(8,128)(2,1)S(1)} %get-tuple-element.45) | copy-start | bytes 1179652
  2.9 4.7 %collective-permute-start = (bf16[256,768]{1,0:T(8,128)(2,1)S(1)}, bf16[256,768]{1,0:T(8,128)(2,1)S(1)}, u32[]{:S(2)}, u32[]{:S(2)}) collective-permute-start(bf16[256,768]{1,0:T(8,128)(2,1)S(1)} %convolution_convert_fusion.1), channel_id=1, source_target_pairs={{0,32},{32,0},{1,33},{33,1},{2,34},{34,2},{3,35},{35,3},{4,36},{36... | collective-permute-start | bytes 1179656 | tf_op jit(solution)/shard_map/ppermute | solution.py:165
  6.2 21.5 %collective-permute-start.1 = (bf16[768,768]{1,0:T(8,128)(2,1)S(1)}, bf16[768,768]{1,0:T(8,128)(2,1)S(1)}, u32[]{:S(2)}, u32[]{:S(2)}) collective-permute-start(bf16[768,768]{1,0:T(8,128)(2,1)S(1)} %copy-done.1), channel_id=1, source_target_pairs={{0,32},{32,0},{1,33},{33,1},{2,34},{34,2},{3,35},{35,3},{4,36},{36... | collective-permute-start | bytes 3538952 | tf_op jit(solution)/shard_map/ppermute | solution.py:165
  18.2 0.6 copy-start.14
  27.7 1.7 copy-start.10
  27.7 1.7 copy-start.7
  29.4 26.9 %all-to-all-start.2 = ((bf16[32,8,1536]{2,1,0:T(8,128)(2,1)}), bf16[32,8,1536]{2,1,0:T(8,128)(2,1)}, u32[]{:S(2)}, u32[]{:S(2)}) async-start(bf16[32,8,1536]{2,1,0:T(8,128)(2,1)} %bitcast.5), calls=%async_computation.2 | async-start | bytes 1572864 | tf_op jit(solution)/shard_map/all_to_all | solution.py:169
  39.7 14.1 %collective-permute-start.2 = (bf16[768,768]{1,0:T(8,128)(2,1)S(1)}, bf16[768,768]{1,0:T(8,128)(2,1)S(1)}, u32[]{:S(2)}, u32[]{:S(2)}) collective-permute-start(bf16[768,768]{1,0:T(8,128)(2,1)S(1)} %copy-done), channel_id=1, source_target_pairs={{0,32},{32,0},{1,33},{33,1},{2,34},{34,2},{3,35},{35,3},{4,36},{36... | collective-permute-start | bytes 3538952 | tf_op jit(solution)/shard_map/ppermute | solution.py:165
  45.3 0.8 copy-start.26
  47.3 4.2 %collective-permute-start.3 = (bf16[256,768]{1,0:T(8,128)(2,1)}, bf16[256,768]{1,0:T(8,128)(2,1)}, u32[]{:S(2)}, u32[]{:S(2)}) collective-permute-start(bf16[256,768]{1,0:T(8,128)(2,1)} %convolution_convert_fusion), channel_id=1, source_target_pairs={{0,32},{32,0},{1,33},{33,1},{2,34},{34,2},{3,35},{35,3},{4,36},{36... | collective-permute-start | bytes 1179656 | tf_op jit(solution)/shard_map/ppermute | solution.py:165
  48.2 1.5 collective-permute-start.4
  49.6 1.3 collective-permute-start.5
  56.3 0.8 copy-start.13
  83.2 0.9 copy-start.2
  83.2 1.3 copy-start.23
  108.0 0.9 copy-start.5
  108.9 0.9 copy-start.9
  109.8 21.8 %all-to-all-start.6 = ((bf16[32,8,1536]{2,1,0:T(8,128)(2,1)}), bf16[32,8,1536]{2,1,0:T(8,128)(2,1)}, u32[]{:S(2)}, u32[]{:S(2)}) async-start(bf16[32,8,1536]{2,1,0:T(8,128)(2,1)} %bitcast.37), calls=%async_computation.6 | async-start | bytes 1572864 | tf_op jit(solution)/shard_map/all_to_all | solution.py:169
  116.6 10.1 %copy-start.6 = (bf16[4,64,1536]{2,1,0:T(8,128)(2,1)S(1)}, bf16[4,64,1536]{2,1,0:T(8,128)(2,1)}, u32[]{:S(2)}) copy-start(bf16[4,64,1536]{2,1,0:T(8,128)(2,1)} %copy-done.5) | copy-start | bytes 2359300
  116.6 10.4 %collective-permute-start.7 = (bf16[256,1536]{1,0:T(8,128)(2,1)}, bf16[256,1536]{1,0:T(8,128)(2,1)S(1)}, u32[]{:S(2)}, u32[]{:S(2)}) collective-permute-start(bf16[256,1536]{1,0:T(8,128)(2,1)} %bitcast.35), channel_id=1, source_target_pairs={{0,32},{32,0},{1,33},{33,1},{2,34},{34,2},{3,35},{35,3},{4,36},{36... | collective-permute-start | bytes 2359304 | tf_op jit(solution)/shard_map/ppermute | solution.py:165
  124.8 6.8 %collective-permute-start.8 = (bf16[256,768]{1,0:T(8,128)(2,1)}, bf16[256,768]{1,0:T(8,128)(2,1)}, u32[]{:S(2)}, u32[]{:S(2)}) collective-permute-start(bf16[256,768]{1,0:T(8,128)(2,1)} %bitcast.39), channel_id=1, source_target_pairs={{0,32},{32,0},{1,33},{33,1},{2,34},{34,2},{3,35},{35,3},{4,36},{36... | collective-permute-start | bytes 1179656 | tf_op jit(solution)/shard_map/ppermute | solution.py:165
  126.0 1.0 copy-start.22
  126.0 1.1 copy-start.27
  126.0 3.3 %collective-permute-start.6 = (bf16[256,768]{1,0:T(8,128)(2,1)S(1)}, bf16[256,768]{1,0:T(8,128)(2,1)S(1)}, u32[]{:S(2)}, u32[]{:S(2)}) collective-permute-start(bf16[256,768]{1,0:T(8,128)(2,1)S(1)} %get-tuple-element.54), channel_id=1, source_target_pairs={{0,32},{32,0},{1,33},{33,1},{2,34},{34,2},{3,35},{35,3},{4,36},{36... | collective-permute-start | bytes 1179656 | tf_op jit(solution)/shard_map/ppermute | solution.py:165
  131.6 0.8 copy-start.12
  132.4 26.7 %copy-start.8 = (bf16[768,768]{1,0:T(8,128)(2,1)S(1)}, bf16[768,768]{1,0:T(8,128)(2,1)}, u32[]{:S(2)}) copy-start(bf16[768,768]{1,0:T(8,128)(2,1)} %copy-done.7) | copy-start | bytes 3538948
  133.7 26.2 %copy-start.16 = (f32[8,1536]{1,0:T(8,128)}, f32[8,1536]{1,0:T(8,128)S(1)}, u32[]{:S(2)}) copy-start(f32[8,1536]{1,0:T(8,128)S(1)} %get-tuple-element.36.a_ref) | copy-start | bytes 147460
  159.1 0.9 copy-start.3
  159.1 9.5 %copy-start.15 = (bf16[64,768]{1,0:T(8,128)(2,1)S(1)}, bf16[64,768]{1,0:T(8,128)(2,1)}, u32[]{:S(2)}) copy-start(bf16[64,768]{1,0:T(8,128)(2,1)} %copy-done.14) | copy-start | bytes 294916
  180.8 5.1 %copy-start.4 = (bf16[32,8,1536]{2,1,0:T(8,128)(2,1)S(1)}, bf16[32,8,1536]{2,1,0:T(8,128)(2,1)}, u32[]{:S(2)}) copy-start(bf16[32,8,1536]{2,1,0:T(8,128)(2,1)} %copy-done.3) | copy-start | bytes 2359300
  180.8 16.3 %copy-start.11 = (bf16[4,64,768]{2,1,0:T(8,128)(2,1)S(1)}, bf16[4,64,768]{2,1,0:T(8,128)(2,1)}, u32[]{:S(2)}) copy-start(bf16[4,64,768]{2,1,0:T(8,128)(2,1)} %copy-done.10) | copy-start | bytes 1179652
  180.8 23.4 %all-to-all-start.10 = ((bf16[32,8,1536]{2,1,0:T(8,128)(2,1)}), bf16[32,8,1536]{2,1,0:T(8,128)(2,1)S(1)}, u32[]{:S(2)}, u32[]{:S(2)}) async-start(bf16[32,8,1536]{2,1,0:T(8,128)(2,1)} %bitcast.17), calls=%async_computation.10 | async-start | bytes 1572864 | tf_op jit(solution)/shard_map/all_to_all | solution.py:169
  185.9 11.2 %collective-permute-start.10 = (bf16[256,768]{1,0:T(8,128)(2,1)S(1)}, bf16[256,768]{1,0:T(8,128)(2,1)S(1)}, u32[]{:S(2)}, u32[]{:S(2)}) collective-permute-start(bf16[256,768]{1,0:T(8,128)(2,1)S(1)} %get-tuple-element.48), channel_id=1, source_target_pairs={{0,32},{32,0},{1,33},{33,1},{2,34},{34,2},{3,35},{35,3},{4,36},{36... | collective-permute-start | bytes 1179656 | tf_op jit(solution)/shard_map/ppermute | solution.py:165
  195.7 5.0 %collective-permute-start.9 = (bf16[256,768]{1,0:T(8,128)(2,1)S(1)}, bf16[256,768]{1,0:T(8,128)(2,1)S(1)}, u32[]{:S(2)}, u32[]{:S(2)}) collective-permute-start(bf16[256,768]{1,0:T(8,128)(2,1)S(1)} %bitcast.42), channel_id=1, source_target_pairs={{0,32},{32,0},{1,33},{33,1},{2,34},{34,2},{3,35},{35,3},{4,36},{36... | collective-permute-start | bytes 1179656 | tf_op jit(solution)/shard_map/ppermute | solution.py:165
  197.1 2.0 copy-start.18
  199.0 1.7 copy-start.21
  199.1 1.7 copy-start.25
  200.8 1.7 copy-start.19
  202.4 1.7 copy-start.17
  204.3 7.9 %collective-permute-start.11 = (f32[8,768]{1,0:T(8,128)S(1)}, f32[8,768]{1,0:T(8,128)S(1)}, u32[]{:S(2)}, u32[]{:S(2)}) collective-permute-start(f32[8,768]{1,0:T(8,128)S(1)} %get-tuple-element.38), channel_id=1, source_target_pairs={{0,32},{32,0},{1,33},{33,1},{2,34},{34,2},{3,35},{35,3},{4,36},{36... | collective-permute-start | bytes 73736 | tf_op jit(solution)/shard_map/ppermute | solution.py:165

commit v5 on v4

--- a/solution.py
+++ b/solution.py
@@ -230,16 +230,8 @@
     one_other = swap(one)
     input_far = swap(input_one[:, wide:])
     act_zero_other = swap(act_zero)
-    grad_up = t_dot(
-        jnp.concatenate([input_one[:, :wide], input_far], axis=0),
-        jnp.concatenate([one[:, :deep], one_other[:, :deep]], axis=0),
-    )
-    grad_down = t_dot(
-        jnp.concatenate([one[:, deep:], one_other[:, deep:]], axis=0),
-        jnp.concatenate([two_own, two_other], axis=0),
-    )
-    landed, grad_up, grad_down, act_zero_other = lax.optimization_barrier(
-        (landed, grad_up, grad_down, act_zero_other)
+    landed, one_other, input_far, act_zero_other = lax.optimization_barrier(
+        (landed, one_other, input_far, act_zero_other)
     )
     grad_one, error_one = sum_and_copy(landed, target_rows)
     error_one = exchange(error_one, HIDDEN).reshape(half, 2 * wide)
@@ -251,13 +243,13 @@
     part = widen(dot_t, inner_zero, w_up, up_other)
     landed = exchange(part.reshape(n_h, eight, 2 * wide), HIDDEN)
 
-    grad_down = grad_down + t_dot(
-        jnp.concatenate([act_zero, act_zero_other], axis=0),
-        jnp.concatenate([error_one[:, :wide], swap(error_one[:, wide:])], axis=0),
-    )
-    grad_up = grad_up + t_dot(
-        jnp.concatenate([start_own, start_other], axis=0),
-        jnp.concatenate([inner_zero, swap(inner_zero)], axis=0),
+    grad_down = t_dot(
+        jnp.concatenate([act_zero, act_zero_other, one[:, deep:], one_other[:, deep:]], axis=0),
+        jnp.concatenate([error_one[:, :wide], swap(error_one[:, wide:]), two_own, two_other], axis=0),
+    )
+    grad_up = t_dot(
+        jnp.concatenate([start_own, start_other, input_one[:, :wide], input_far], axis=0),
+        jnp.concatenate([inner_zero, swap(inner_zero), one[:, :deep], one_other[:, :deep]], axis=0),
     )
     landed, grad_up, grad_down = lax.optimization_barrier((landed, grad_up, grad_down))
 

time: 214 us -> 214 us (level)
  waiting for transfers between devices: 6.52 us -> 11.7 us
  blocking collectives: 111 us -> 107 us
  starting transfers between devices: 55.6 us -> 59.6 us
  other arithmetic: 6.13 us -> 2.75 us
  matrix products: 11.8 us -> 8.44 us
    all_to_all x3, waiting for transfers between devices: 2.39 us -> 7.82 us  [exchange(): return lax.all_to_all(parts, axes, 0, 0, tiled=True)]
    all_to_all x8, blocking collectives: 111 us -> 107 us  [exchange(): return lax.all_to_all(parts, axes, 0, 0, tiled=True)]
    add x2 -> x0, other arithmetic: 3.38 us -> none  [the longest x1 1.69 us: shards(): grad_down + t_dot(jnp.concatenate([act_zero, act_zero_other], axis=0), jn...]
    dot_general x4 -> x2, matrix products: 7.19 us -> 5.73 us  [t_dot(): lax.dot_general(a, b, (((0,), (0,)), ((), ())), preferred_element_type=f32)]
    unnamed x56 -> x70, local copies, waits for them, and re-layouts: 5.57 us -> 6.47 us
  transfers between devices with their start and end apart: 15 -> 15, of which waited for: 6 -> 7; matrix products, arithmetic and copies ran while one was open for 10% -> 7% of each run, Pallas kernels for 0% -> 0%
where the time goes in v5:
time: 214 us; the launch traced here: 212 us
  blocking collectives  107 us (50%)
  starting transfers between devices  59.6 us (28%)
  local copies, waits for them, and re-layouts  13.6 us (6%)
  waiting for transfers between devices  11.7 us (5%)
  Pallas kernels  8.79 us (4%)
  matrix products  8.44 us (4%)
  other arithmetic  2.75 us (1%)
    all_to_all x8, blocking collectives, exchange(): return lax.all_to_all(parts, axes, 0, 0, tiled=True)  107 us
    ppermute x12, starting transfers between devices, swap(): return lax.ppermute(block, 'core', [(0, 1), (1, 0)])  35.3 us
    all_to_all x3, starting transfers between devices, exchange(): return lax.all_to_all(parts, axes, 0, 0, tiled=True)  24.2 us
    pallas_call x11, Pallas kernels, call(): pl.pallas_call(body, out_shape=[jax.ShapeDtypeStruct(s, t) for s, t in ou...  8.79 us
    all_to_all x3, waiting for transfers between devices, exchange(): return lax.all_to_all(parts, axes, 0, 0, tiled=True)  7.82 us
    unnamed x70, local copies, waits for them, and re-layouts  6.47 us
    dot_general x2, matrix products, t_dot(): lax.dot_general(a, b, (((0,), (0,)), ((), ())), preferred_element_type=f32)  5.73 us
  transfers between devices with their start and end apart: 15, of which 7 were waited for; matrix products, arithmetic and copies ran while one was open for 7% of the time, Pallas kernels for 0%

profile of v5, /device:TPU:1, one launch (start us, length us, event | category | flops | bytes accessed | tf_op | source)
XLA Modules:
  0.0 212.5 jit_solution(13919520896084900198)
XLA Ops:
  0.7 1.6 fusion.31
  3.0 3.2 %collective-permute-start = (bf16[256,768]{1,0:T(8,128)(2,1)S(1)}, bf16[256,768]{1,0:T(8,128)(2,1)S(1)}, u32[]{:S(2)}, u32[]{:S(2)}) collective-permute-start(bf16[256,768]{1,0:T(8,128)(2,1)S(1)} %convolution_convert_fusion.1), channel_id=1, source_target_pairs={{0,32},{32,0},{1,33},{33,1},{2,34},{34,2},{3,35},{35,3},{4,36},{36... | collective-permute-start | bytes 1179656 | tf_op jit(solution)/shard_map/ppermute | solution.py:165
  6.3 1.3 collective-permute-done
  8.1 10.1 %all_to_all.55.l_ref = bf16[4,64,768]{2,1,0:T(8,128)(2,1)S(1)} all-to-all(bf16[4,64,768]{2,1,0:T(8,128)(2,1)S(1)} %bitcast.64), channel_id=1, replica_groups=mesh['y'=4,'core'=2,'x'=4,'z'=8] {'y'}, dimensions={0} | all-to-all | bytes 786432 | tf_op jit(solution)/shard_map/all_to_all | solution.py:169
  18.3 0.6 copy-done.17
  18.9 8.8 %all_to_all.56 = bf16[4,64,768]{2,1,0:T(8,128)(2,1)S(1)} all-to-all(bf16[4,64,768]{2,1,0:T(8,128)(2,1)S(1)} %get-tuple-element.22), channel_id=1, replica_groups=mesh['y'=4,'core'=2,'x'=4,'z'=8] {'y'}, dimensions={0} | all-to-all | bytes 786432 | tf_op jit(solution)/shard_map/all_to_all | solution.py:169
  27.8 1.7 shard_map.77
  29.4 10.3 %all-to-all-start.2 = ((bf16[32,8,1536]{2,1,0:T(8,128)(2,1)}), bf16[32,8,1536]{2,1,0:T(8,128)(2,1)}, u32[]{:S(2)}, u32[]{:S(2)}) async-start(bf16[32,8,1536]{2,1,0:T(8,128)(2,1)} %bitcast.5), calls=%async_computation.2 | async-start | bytes 1572864 | tf_op jit(solution)/shard_map/all_to_all | solution.py:169
  39.8 3.3 %collective-permute-start.2 = (bf16[768,768]{1,0:T(8,128)(2,1)S(1)}, bf16[768,768]{1,0:T(8,128)(2,1)S(1)}, u32[]{:S(2)}, u32[]{:S(2)}) collective-permute-start(bf16[768,768]{1,0:T(8,128)(2,1)S(1)} %copy-done), channel_id=1, source_target_pairs={{0,32},{32,0},{1,33},{33,1},{2,34},{34,2},{3,35},{35,3},{4,36},{36... | collective-permute-start | bytes 3538952 | tf_op jit(solution)/shard_map/ppermute | solution.py:165
  43.1 0.9 constant_dynamic-slice_fusion.3
  44.1 0.8 dynamic-slice_add_fusion
  45.5 1.4 fusion.33
  47.6 0.6 pad_maximum_fusion.1.a_ref
  48.3 0.6 pad_maximum_fusion.2.a_ref
  49.3 1.3 add_convert_fusion
  50.6 5.7 %all-to-all-done.2.l_ref = bf16[32,8,1536]{2,1,0:T(8,128)(2,1)} async-done(((bf16[32,8,1536]{2,1,0:T(8,128)(2,1)}), bf16[32,8,1536]{2,1,0:T(8,128)(2,1)}, u32[]{:S(2)}, u32[]{:S(2)}) %all-to-all-start.2) | async-done | bytes 786464 | tf_op jit(solution)/shard_map/all_to_all | solution.py:169
  56.3 0.8 copy-done.16
  57.1 1.9 shard_map.78
  59.0 24.3 %all_to_all.57 = bf16[32,8,1536]{2,1,0:T(8,128)(2,1)S(1)} all-to-all(bf16[32,8,1536]{2,1,0:T(8,128)(2,1)S(1)} %get-tuple-element.25), channel_id=1, replica_groups=mesh['y'=4,'core'=2,'x'=4,'z'=8] {'x','z'}, dimensions={0} | all-to-all | bytes 1572864 | tf_op jit(solution)/shard_map/all_to_all | solution.py:169
  83.3 0.8 shard_map.79
  84.6 10.7 %all_to_all.58.l_ref = bf16[4,64,1536]{2,1,0:T(8,128)(2,1)S(1)} all-to-all(bf16[4,64,1536]{2,1,0:T(8,128)(2,1)S(1)} %pad_maximum_fusion), channel_id=1, replica_groups=mesh['y'=4,'core'=2,'x'=4,'z'=8] {'y'}, dimensions={0} | all-to-all | bytes 1572864 | tf_op jit(solution)/shard_map/all_to_all | solution.py:169
  95.6 12.4 %all_to_all.59 = bf16[4,64,1536]{2,1,0:T(8,128)(2,1)S(1)} all-to-all(bf16[4,64,1536]{2,1,0:T(8,128)(2,1)S(1)} %shard_map.80), channel_id=1, replica_groups=mesh['y'=4,'core'=2,'x'=4,'z'=8] {'y'}, dimensions={0} | all-to-all | bytes 1572864 | tf_op jit(solution)/shard_map/all_to_all | solution.py:169
  108.0 0.8 shard_map.81
  108.9 0.9 copy-done.10
  109.8 6.8 %all-to-all-start.6 = ((bf16[32,8,1536]{2,1,0:T(8,128)(2,1)}), bf16[32,8,1536]{2,1,0:T(8,128)(2,1)}, u32[]{:S(2)}, u32[]{:S(2)}) async-start(bf16[32,8,1536]{2,1,0:T(8,128)(2,1)} %bitcast.54), calls=%async_computation.6 | async-start | bytes 1572864 | tf_op jit(solution)/shard_map/all_to_all | solution.py:169
  116.7 8.1 %collective-permute-start.6 = (bf16[256,1536]{1,0:T(8,128)(2,1)}, bf16[256,1536]{1,0:T(8,128)(2,1)}, u32[]{:S(2)}, u32[]{:S(2)}) collective-permute-start(bf16[256,1536]{1,0:T(8,128)(2,1)} %bitcast.51), channel_id=1, source_target_pairs={{0,32},{32,0},{1,33},{33,1},{2,34},{34,2},{3,35},{35,3},{4,36},{36... | collective-permute-start | bytes 2359304 | tf_op jit(solution)/shard_map/ppermute | solution.py:165
  124.9 1.9 fusion.39
  127.5 1.1 collective-permute-done.7
  128.6 0.8 copy-done.31
  129.3 2.1 all-to-all-done.6.l_ref
  131.4 0.8 copy-done.15
  132.2 1.4 shard_map.82
  133.6 22.0 %all_to_all.60 = bf16[32,8,1536]{2,1,0:T(8,128)(2,1)S(1)} all-to-all(bf16[32,8,1536]{2,1,0:T(8,128)(2,1)S(1)} %get-tuple-element.30), channel_id=1, replica_groups=mesh['y'=4,'core'=2,'x'=4,'z'=8] {'x','z'}, dimensions={0} | all-to-all | bytes 1572864 | tf_op jit(solution)/shard_map/all_to_all | solution.py:169
  155.6 0.8 shard_map.83
  156.5 8.6 %all_to_all.61.l_ref = bf16[4,64,768]{2,1,0:T(8,128)(2,1)S(1)} all-to-all(bf16[4,64,768]{2,1,0:T(8,128)(2,1)S(1)} %bitcast.62), channel_id=1, replica_groups=mesh['y'=4,'core'=2,'x'=4,'z'=8] {'y'}, dimensions={0} | all-to-all | bytes 786432 | tf_op jit(solution)/shard_map/all_to_all | solution.py:169
  165.3 9.6 %all_to_all.62 = bf16[4,64,768]{2,1,0:T(8,128)(2,1)S(1)} all-to-all(bf16[4,64,768]{2,1,0:T(8,128)(2,1)S(1)} %shard_map.84), channel_id=1, replica_groups=mesh['y'=4,'core'=2,'x'=4,'z'=8] {'y'}, dimensions={0} | all-to-all | bytes 786432 | tf_op jit(solution)/shard_map/all_to_all | solution.py:169
  174.8 0.8 shard_map.85
  175.7 0.9 copy-done.9
  176.6 0.7 copy-done.13
  177.3 7.0 %all-to-all-start.10 = ((bf16[32,8,1536]{2,1,0:T(8,128)(2,1)}), bf16[32,8,1536]{2,1,0:T(8,128)(2,1)S(1)}, u32[]{:S(2)}, u32[]{:S(2)}) async-start(bf16[32,8,1536]{2,1,0:T(8,128)(2,1)} %bitcast.53), calls=%async_computation.10 | async-start | bytes 1572864 | tf_op jit(solution)/shard_map/all_to_all | solution.py:169
  184.5 10.7 %collective-permute-start.10 = (bf16[256,768]{1,0:T(8,128)(2,1)S(1)}, bf16[256,768]{1,0:T(8,128)(2,1)S(1)}, u32[]{:S(2)}, u32[]{:S(2)}) collective-permute-start(bf16[256,768]{1,0:T(8,128)(2,1)S(1)} %get-tuple-element.48), channel_id=1, source_target_pairs={{0,32},{32,0},{1,33},{33,1},{2,34},{34,2},{3,35},{35,3},{4,36},{36... | collective-permute-start | bytes 1179656 | tf_op jit(solution)/shard_map/ppermute | solution.py:165
  195.3 0.7 collective-permute-start.9
  196.0 1.2 fusion.38
  197.3 2.9 %fusion.15 = f32[768,768]{1,0:T(8,128)} fusion(bf16[256,768]{1,0:T(8,128)(2,1)S(1)} %get-tuple-element.51, bf16[256,768]{1,0:T(8,128)(2,1)S(1)} %get-tuple-element.49, bf16[256,768]{1,0:T(8,128)(2,1)S(1)} %copy-done.34, bf16[256,768]{1,0:T(8,128)(2,1)S(1)} %bitcast.57, bf16[256,768]{1,0:T(8,128)(2,1)S(1)} %copy-done.29, ...), kind=kOutput, calls=%fused_computation.15 | convolution fusion | flops 1220542464 | bytes 5505024 | tf_op jit(solution)/shard_map/dot_general | solution.py:39
  200.2 2.9 %fusion = f32[768,768]{1,0:T(8,128)} fusion(bf16[256,768]{1,0:T(8,128)(2,1)S(1)} %copy-done.32, bf16[256,768]{1,0:T(8,128)(2,1)S(1)} %copy-done.30, bf16[256,768]{1,0:T(8,128)(2,1)S(1)} %copy-done.27, bf16[256,768]{1,0:T(8,128)(2,1)S(1)} %copy-done.22, bf16[256,768]{1,0:T(8,128)(2,1)S(1)} %get-tuple-element.52, bf16[256,768]{1,0:T(8,128)(2,1)S(1)} %get-tuple-element.50, ...), kind=kOutput, calls=%fused_computation | convolution fusion | flops 1220542464 | bytes 5505024 | tf_op jit(solution)/shard_map/dot_general | solution.py:39
  203.2 7.8 %collective-permute-start.11 = (f32[8,768]{1,0:T(8,128)S(1)}, f32[8,768]{1,0:T(8,128)S(1)}, u32[]{:S(2)}, u32[]{:S(2)}) collective-permute-start(f32[8,768]{1,0:T(8,128)S(1)} %get-tuple-element.38), channel_id=1, source_target_pairs={{0,32},{32,0},{1,33},{33,1},{2,34},{34,2},{3,35},{35,3},{4,36},{36... | collective-permute-start | bytes 73736 | tf_op jit(solution)/shard_map/ppermute | solution.py:165
  211.0 0.8 collective-permute-done.11
  211.9 0.6 maximum_select_fusion
  (90 shorter events, 5.4 us)
Async XLA Ops:
  0.6 1.7 copy-start
  0.6 5.6 %copy-start.1 = (bf16[768,768]{1,0:T(8,128)(2,1)S(1)}, bf16[768,768]{1,0:T(8,128)(2,1)}, u32[]{:S(2)}) copy-start(bf16[768,768]{1,0:T(8,128)(2,1)} %a_ref.8) | copy-start | bytes 3538948
  2.3 0.7 copy-start.26
  2.3 5.8 %copy-start.21 = (bf16[256,768]{1,0:T(8,128)(2,1)}, bf16[256,768]{1,0:T(8,128)(2,1)S(1)}, u32[]{:S(2)}) copy-start(bf16[256,768]{1,0:T(8,128)(2,1)S(1)} %get-tuple-element.46) | copy-start | bytes 1179652
  3.0 4.6 %collective-permute-start = (bf16[256,768]{1,0:T(8,128)(2,1)S(1)}, bf16[256,768]{1,0:T(8,128)(2,1)S(1)}, u32[]{:S(2)}, u32[]{:S(2)}) collective-permute-start(bf16[256,768]{1,0:T(8,128)(2,1)S(1)} %convolution_convert_fusion.1), channel_id=1, source_target_pairs={{0,32},{32,0},{1,33},{33,1},{2,34},{34,2},{3,35},{35,3},{4,36},{36... | collective-permute-start | bytes 1179656 | tf_op jit(solution)/shard_map/ppermute | solution.py:165
  6.3 21.5 %collective-permute-start.1 = (bf16[768,768]{1,0:T(8,128)(2,1)S(1)}, bf16[768,768]{1,0:T(8,128)(2,1)S(1)}, u32[]{:S(2)}, u32[]{:S(2)}) collective-permute-start(bf16[768,768]{1,0:T(8,128)(2,1)S(1)} %copy-done.1), channel_id=1, source_target_pairs={{0,32},{32,0},{1,33},{33,1},{2,34},{34,2},{3,35},{35,3},{4,36},{36... | collective-permute-start | bytes 3538952 | tf_op jit(solution)/shard_map/ppermute | solution.py:165
  27.8 1.7 copy-start.11
  27.8 1.7 copy-start.7
  29.4 26.9 %all-to-all-start.2 = ((bf16[32,8,1536]{2,1,0:T(8,128)(2,1)}), bf16[32,8,1536]{2,1,0:T(8,128)(2,1)}, u32[]{:S(2)}, u32[]{:S(2)}) async-start(bf16[32,8,1536]{2,1,0:T(8,128)(2,1)} %bitcast.5), calls=%async_computation.2 | async-start | bytes 1572864 | tf_op jit(solution)/shard_map/all_to_all | solution.py:169
  39.8 10.8 %collective-permute-start.2 = (bf16[768,768]{1,0:T(8,128)(2,1)S(1)}, bf16[768,768]{1,0:T(8,128)(2,1)S(1)}, u32[]{:S(2)}, u32[]{:S(2)}) collective-permute-start(bf16[768,768]{1,0:T(8,128)(2,1)S(1)} %copy-done), channel_id=1, source_target_pairs={{0,32},{32,0},{1,33},{33,1},{2,34},{34,2},{3,35},{35,3},{4,36},{36... | collective-permute-start | bytes 3538952 | tf_op jit(solution)/shard_map/ppermute | solution.py:165
  44.0 3.6 %collective-permute-start.4 = (f32[8,768]{1,0:T(8,128)S(1)}, f32[8,768]{1,0:T(8,128)S(1)}, u32[]{:S(2)}, u32[]{:S(2)}) collective-permute-start(f32[8,768]{1,0:T(8,128)S(1)} %get-tuple-element.42), channel_id=1, source_target_pairs={{0,32},{32,0},{1,33},{33,1},{2,34},{34,2},{3,35},{35,3},{4,36},{36... | collective-permute-start | bytes 73736 | tf_op jit(solution)/shard_map/ppermute | solution.py:165
  45.0 3.3 %collective-permute-start.5 = (f32[8,768]{1,0:T(8,128)S(1)}, f32[8,768]{1,0:T(8,128)S(1)}, u32[]{:S(2)}, u32[]{:S(2)}) collective-permute-start(f32[8,768]{1,0:T(8,128)S(1)} %get-tuple-element.56), channel_id=1, source_target_pairs={{0,32},{32,0},{1,33},{33,1},{2,34},{34,2},{3,35},{35,3},{4,36},{36... | collective-permute-start | bytes 73736 | tf_op jit(solution)/shard_map/ppermute | solution.py:165
  47.0 3.6 %copy-start.23 = (bf16[256,768]{1,0:T(8,128)(2,1)}, bf16[256,768]{1,0:T(8,128)(2,1)S(1)}, u32[]{:S(2)}) copy-start(bf16[256,768]{1,0:T(8,128)(2,1)S(1)} %get-tuple-element.44) | copy-start | bytes 1179652
  47.0 3.6 %copy-start.28 = (bf16[256,768]{1,0:T(8,128)(2,1)}, bf16[256,768]{1,0:T(8,128)(2,1)S(1)}, u32[]{:S(2)}) copy-start(bf16[256,768]{1,0:T(8,128)(2,1)S(1)} %get-tuple-element.43) | copy-start | bytes 1179652
  47.5 1.8 collective-permute-start.3
  56.3 0.8 copy-start.16
  83.3 0.9 copy-start.2
  83.3 1.3 copy-start.25
  108.0 0.9 copy-start.5
  108.9 0.9 copy-start.10
  109.8 21.6 %all-to-all-start.6 = ((bf16[32,8,1536]{2,1,0:T(8,128)(2,1)}), bf16[32,8,1536]{2,1,0:T(8,128)(2,1)}, u32[]{:S(2)}, u32[]{:S(2)}) async-start(bf16[32,8,1536]{2,1,0:T(8,128)(2,1)} %bitcast.54), calls=%async_computation.6 | async-start | bytes 1572864 | tf_op jit(solution)/shard_map/all_to_all | solution.py:169
  116.7 12.7 %collective-permute-start.6 = (bf16[256,1536]{1,0:T(8,128)(2,1)}, bf16[256,1536]{1,0:T(8,128)(2,1)}, u32[]{:S(2)}, u32[]{:S(2)}) collective-permute-start(bf16[256,1536]{1,0:T(8,128)(2,1)} %bitcast.51), channel_id=1, source_target_pairs={{0,32},{32,0},{1,33},{33,1},{2,34},{34,2},{3,35},{35,3},{4,36},{36... | collective-permute-start | bytes 2359304 | tf_op jit(solution)/shard_map/ppermute | solution.py:165
  124.8 2.7 %collective-permute-start.8 = (bf16[256,768]{1,0:T(8,128)(2,1)}, bf16[256,768]{1,0:T(8,128)(2,1)S(1)}, u32[]{:S(2)}, u32[]{:S(2)}) collective-permute-start(bf16[256,768]{1,0:T(8,128)(2,1)} %bitcast.56), channel_id=1, source_target_pairs={{0,32},{32,0},{1,33},{33,1},{2,34},{34,2},{3,35},{35,3},{4,36},{36... | collective-permute-start | bytes 1179656 | tf_op jit(solution)/shard_map/ppermute | solution.py:165
  126.8 1.8 collective-permute-start.7
  127.5 1.1 copy-start.33
  128.6 0.8 copy-start.31
  131.4 0.8 copy-start.15
  132.2 23.4 %copy-start.8 = (bf16[768,768]{1,0:T(8,128)(2,1)S(1)}, bf16[768,768]{1,0:T(8,128)(2,1)}, u32[]{:S(2)}) copy-start(bf16[768,768]{1,0:T(8,128)(2,1)} %copy-done.7) | copy-start | bytes 3538948
  133.6 22.8 %copy-start.19 = (f32[8,1536]{1,0:T(8,128)}, f32[8,1536]{1,0:T(8,128)S(1)}, u32[]{:S(2)}) copy-start(f32[8,1536]{1,0:T(8,128)S(1)} %get-tuple-element.36.a_ref) | copy-start | bytes 147460
  155.6 0.9 copy-start.3
  155.6 9.5 %copy-start.18 = (bf16[64,768]{1,0:T(8,128)(2,1)S(1)}, bf16[64,768]{1,0:T(8,128)(2,1)}, u32[]{:S(2)}) copy-start(bf16[64,768]{1,0:T(8,128)(2,1)} %copy-done.17) | copy-start | bytes 294916
  175.7 0.9 copy-start.9
  177.3 7.1 %copy-start.4 = (bf16[32,8,1536]{2,1,0:T(8,128)(2,1)S(1)}, bf16[32,8,1536]{2,1,0:T(8,128)(2,1)}, u32[]{:S(2)}) copy-start(bf16[32,8,1536]{2,1,0:T(8,128)(2,1)} %copy-done.3) | copy-start | bytes 2359300
  177.3 17.9 %copy-start.6 = (bf16[4,64,1536]{2,1,0:T(8,128)(2,1)S(1)}, bf16[4,64,1536]{2,1,0:T(8,128)(2,1)}, u32[]{:S(2)}) copy-start(bf16[4,64,1536]{2,1,0:T(8,128)(2,1)} %copy-done.5) | copy-start | bytes 2359300
  177.3 25.7 %all-to-all-start.10 = ((bf16[32,8,1536]{2,1,0:T(8,128)(2,1)}), bf16[32,8,1536]{2,1,0:T(8,128)(2,1)S(1)}, u32[]{:S(2)}, u32[]{:S(2)}) async-start(bf16[32,8,1536]{2,1,0:T(8,128)(2,1)} %bitcast.53), calls=%async_computation.10 | async-start | bytes 1572864 | tf_op jit(solution)/shard_map/all_to_all | solution.py:169
  184.4 10.9 %copy-start.14 = (bf16[4,64,768]{2,1,0:T(8,128)(2,1)S(1)}, bf16[4,64,768]{2,1,0:T(8,128)(2,1)}, u32[]{:S(2)}) copy-start(bf16[4,64,768]{2,1,0:T(8,128)(2,1)} %copy-done.13) | copy-start | bytes 1179652
  184.5 12.8 %copy-start.12 = (bf16[4,64,768]{2,1,0:T(8,128)(2,1)S(1)}, bf16[4,64,768]{2,1,0:T(8,128)(2,1)}, u32[]{:S(2)}) copy-start(bf16[4,64,768]{2,1,0:T(8,128)(2,1)} %copy-done.11) | copy-start | bytes 1179652
  184.5 12.8 %copy-start.24 = (bf16[256,768]{1,0:T(8,128)(2,1)S(1)}, bf16[256,768]{1,0:T(8,128)(2,1)}, u32[]{:S(2)}) copy-start(bf16[256,768]{1,0:T(8,128)(2,1)} %copy-done.23) | copy-start | bytes 1179652
  184.5 12.8 %copy-start.29 = (bf16[256,768]{1,0:T(8,128)(2,1)S(1)}, bf16[256,768]{1,0:T(8,128)(2,1)}, u32[]{:S(2)}) copy-start(bf16[256,768]{1,0:T(8,128)(2,1)} %copy-done.28) | copy-start | bytes 1179652
  184.5 12.8 %copy-start.34 = (bf16[256,768]{1,0:T(8,128)(2,1)S(1)}, bf16[256,768]{1,0:T(8,128)(2,1)}, u32[]{:S(2)}) copy-start(bf16[256,768]{1,0:T(8,128)(2,1)} %copy-done.33) | copy-start | bytes 1179652
  184.5 12.7 %collective-permute-start.10 = (bf16[256,768]{1,0:T(8,128)(2,1)S(1)}, bf16[256,768]{1,0:T(8,128)(2,1)S(1)}, u32[]{:S(2)}, u32[]{:S(2)}) collective-permute-start(bf16[256,768]{1,0:T(8,128)(2,1)S(1)} %get-tuple-element.48), channel_id=1, source_target_pairs={{0,32},{32,0},{1,33},{33,1},{2,34},{34,2},{3,35},{35,3},{4,36},{36... | collective-permute-start | bytes 1179656 | tf_op jit(solution)/shard_map/ppermute | solution.py:165
  195.3 4.9 %collective-permute-start.9 = (bf16[256,768]{1,0:T(8,128)(2,1)S(1)}, bf16[256,768]{1,0:T(8,128)(2,1)S(1)}, u32[]{:S(2)}, u32[]{:S(2)}) collective-permute-start(bf16[256,768]{1,0:T(8,128)(2,1)S(1)} %bitcast.59), channel_id=1, source_target_pairs={{0,32},{32,0},{1,33},{33,1},{2,34},{34,2},{3,35},{35,3},{4,36},{36... | collective-permute-start | bytes 1179656 | tf_op jit(solution)/shard_map/ppermute | solution.py:165
  197.3 2.9 %copy-start.22 = (bf16[256,768]{1,0:T(8,128)(2,1)S(1)}, bf16[256,768]{1,0:T(8,128)(2,1)}, u32[]{:S(2)}) copy-start(bf16[256,768]{1,0:T(8,128)(2,1)} %copy-done.21) | copy-start | bytes 1179652
  197.3 2.9 %copy-start.27 = (bf16[256,768]{1,0:T(8,128)(2,1)S(1)}, bf16[256,768]{1,0:T(8,128)(2,1)}, u32[]{:S(2)}) copy-start(bf16[256,768]{1,0:T(8,128)(2,1)} %copy-done.26) | copy-start | bytes 1179652
  197.3 2.9 %copy-start.30 = (bf16[256,768]{1,0:T(8,128)(2,1)S(1)}, bf16[256,768]{1,0:T(8,128)(2,1)}, u32[]{:S(2)}) copy-start(bf16[256,768]{1,0:T(8,128)(2,1)} %get-tuple-element.53) | copy-start | bytes 1179652
  197.3 2.9 %copy-start.32 = (bf16[256,768]{1,0:T(8,128)(2,1)S(1)}, bf16[256,768]{1,0:T(8,128)(2,1)}, u32[]{:S(2)}) copy-start(bf16[256,768]{1,0:T(8,128)(2,1)} %copy-done.31) | copy-start | bytes 1179652
  200.2 2.9 %copy-start.20 = (f32[8,1536]{1,0:T(8,128)S(1)}, f32[8,1536]{1,0:T(8,128)}, u32[]{:S(2)}) copy-start(f32[8,1536]{1,0:T(8,128)} %copy-done.19) | copy-start | bytes 147460
  203.2 8.6 %collective-permute-start.11 = (f32[8,768]{1,0:T(8,128)S(1)}, f32[8,768]{1,0:T(8,128)S(1)}, u32[]{:S(2)}, u32[]{:S(2)}) collective-permute-start(f32[8,768]{1,0:T(8,128)S(1)} %get-tuple-element.38), channel_id=1, source_target_pairs={{0,32},{32,0},{1,33},{33,1},{2,34},{34,2},{3,35},{35,3},{4,36},{36... | collective-permute-start | bytes 73736 | tf_op jit(solution)/shard_map/ppermute | solution.py:165
  (2 other events, 1.4 us)

commit v6 on v5

--- a/solution.py
+++ b/solution.py
@@ -53,16 +53,33 @@
     return got[0] if len(outs) == 1 else got
 
 
-def widen(product, rows_deep, own_block, other_block):
+def widen(product, rows_deep, own_block, other_block, by_rows):
     rows, wide = rows_deep.shape[0], own_block.shape[0]
-
-    def body(x_ref, a_ref, b_ref, o_ref):
-        o_ref[:, :wide] = product(x_ref[:, :wide], a_ref[...]).astype(bf16)
-        o_ref[:, wide:] = product(x_ref[:, :wide], b_ref[...]).astype(bf16)
-
-    return call(
-        body, [((rows, 2 * wide), bf16)], rows_deep, own_block, other_block, flops=4 * rows * wide * wide
-    )
+    cut = wide // 2
+
+    def body(x_ref, a_ref, b_ref, o_ref, held, sems):
+        copies = []
+        for part in range(4):
+            block, first = (a_ref, b_ref)[part // 2], (part % 2) * cut
+            piece = block[first : first + cut, :] if by_rows else block[:, first : first + cut]
+            held[part] = product(x_ref[:, :wide], piece).astype(bf16)
+            copies.append(
+                pltpu.make_async_copy(held.at[part], o_ref.at[:, pl.ds(part * cut, cut)], sems.at[part])
+            )
+            copies[-1].start()
+        for copy in copies:
+            copy.wait()
+
+    size = 2 * (rows_deep.size + 2 * own_block.size + 2 * rows * wide)
+    return pl.pallas_call(
+        body,
+        out_shape=pltpu.HBM((rows, 2 * wide), bf16),
+        in_specs=[pl.BlockSpec(memory_space=pltpu.VMEM)] * 3,
+        out_specs=pl.BlockSpec(memory_space=pltpu.HBM),
+        scratch_shapes=[pltpu.VMEM((4, rows, cut), bf16), pltpu.SemaphoreType.DMA((4,))],
+        cost_estimate=pl.CostEstimate(flops=4 * rows * wide * wide, bytes_accessed=size, transcendentals=0),
+        compiler_params=pltpu.CompilerParams(vmem_limit_bytes=24 * 2**20),
+    )(rows_deep, own_block, other_block)
 
 
 def narrow(product, rows_wide, own_block, other_block):
@@ -163,6 +180,11 @@
 
 def swap(block):
     return lax.ppermute(block, "core", [(0, 1), (1, 0)])
+
+
+def swap_parts(block):
+    step = block.shape[0] // 2
+    return jnp.concatenate([swap(block[first : first + step]) for first in range(0, block.shape[0], step)], axis=0)
 
 
 def exchange(parts, axes):
@@ -201,21 +223,23 @@
         return (own + swap(other_part.astype(bf16)).astype(f32)).astype(bf16)
 
     down_other = swap(w_down)
+    up_other = swap(w_up)
 
     start_own, start_other = rounded_halves(start_latent)
     pre_part = both_cores(dot(start_own, w_up), dot(start_other, w_up))
     pre_zero, act_zero = activate(exchange(pre_part.reshape(n_y, quarter, deep), "y"))
-    act_zero = exchange(act_zero, "y").reshape(half, deep)
-
-    part = widen(dot, act_zero, w_down, down_other)
+    act_zero, up_other = lax.optimization_barrier((exchange(act_zero, "y").reshape(half, deep), up_other))
+
+    part = widen(dot, act_zero, w_down, down_other, False)
     landed = exchange(part.reshape(n_h, eight, 2 * wide), HIDDEN)
-    up_other = swap(w_up)
     two_own, two_other = rounded_halves(target_two)
-    back_part = both_cores(dot_t(two_own, w_down), dot_t(two_other, w_down))
+    two_far = swap(two_other)
+    start_far = swap(start_other)
+    back_part = (dot_t(two_own, w_down) + dot_t(two_far, down_other)).astype(bf16)
     start_rows = own_rows(start_latent)
     target_rows = own_rows(target_one, target_two)
-    landed, up_other, back_part, start_rows, target_rows = lax.optimization_barrier(
-        (landed, up_other, back_part, start_rows, target_rows)
+    landed, back_part, start_rows, target_rows, start_far = lax.optimization_barrier(
+        (landed, back_part, start_rows, target_rows, start_far)
     )
     latent_one, input_one = sum_and_copy(landed, start_rows)
     input_one = exchange(input_one, HIDDEN).reshape(half, 2 * wide)
@@ -225,14 +249,8 @@
     one = activate_and_back(exchange(both, "y"))
     one = exchange(one, "y").reshape(half, 2 * deep)
 
-    part = widen(dot_t, one, w_up, up_other)
+    part = widen(dot_t, one, w_up, up_other, True)
     landed = exchange(part.reshape(n_h, eight, 2 * wide), HIDDEN)
-    one_other = swap(one)
-    input_far = swap(input_one[:, wide:])
-    act_zero_other = swap(act_zero)
-    landed, one_other, input_far, act_zero_other = lax.optimization_barrier(
-        (landed, one_other, input_far, act_zero_other)
-    )
     grad_one, error_one = sum_and_copy(landed, target_rows)
     error_one = exchange(error_one, HIDDEN).reshape(half, 2 * wide)
 
@@ -240,17 +258,18 @@
     inner_zero = back_through(exchange(back_part.reshape(n_y, quarter, deep), "y"), pre_zero)
     inner_zero = exchange(inner_zero, "y").reshape(half, deep)
 
-    part = widen(dot_t, inner_zero, w_up, up_other)
+    part = widen(dot_t, inner_zero, w_up, up_other, True)
+    part, inner_zero, error_one, one, act_zero, input_one = lax.optimization_barrier(
+        (part, inner_zero, error_one, one, act_zero, input_one)
+    )
     landed = exchange(part.reshape(n_h, eight, 2 * wide), HIDDEN)
 
-    grad_down = t_dot(
-        jnp.concatenate([act_zero, act_zero_other, one[:, deep:], one_other[:, deep:]], axis=0),
-        jnp.concatenate([error_one[:, :wide], swap(error_one[:, wide:]), two_own, two_other], axis=0),
-    )
-    grad_up = t_dot(
-        jnp.concatenate([start_own, start_other, input_one[:, :wide], input_far], axis=0),
-        jnp.concatenate([inner_zero, swap(inner_zero), one[:, :deep], one_other[:, :deep]], axis=0),
-    )
+    inner_both = jnp.concatenate([inner_zero, one[:, :deep]], axis=0)
+    act_both = jnp.concatenate([act_zero, one[:, deep:]], axis=0)
+    up_far = t_dot(jnp.concatenate([start_far, input_one[:, wide:]], axis=0), inner_both).astype(bf16)
+    down_far = t_dot(act_both, jnp.concatenate([error_one[:, wide:], two_far], axis=0)).astype(bf16)
+    grad_up = t_dot(jnp.concatenate([start_own, input_one[:, :wide]], axis=0), inner_both) + swap_parts(up_far)
+    grad_down = t_dot(act_both, jnp.concatenate([error_one[:, :wide], two_own], axis=0)) + swap_parts(down_far)
     landed, grad_up, grad_down = lax.optimization_barrier((landed, grad_up, grad_down))
 
     mine, theirs = sum_last(landed, grad_one)

time: 214 us -> 210 us (0.981)
  blocking collectives: 107 us -> 128 us
  starting transfers between devices: 59.6 us -> 43 us
  local copies, waits for them, and re-layouts: 13.6 us -> 6.83 us
  waiting for transfers between devices: 11.7 us -> 8.28 us
    all_to_all x8 -> x9, blocking collectives: 107 us -> 128 us  [exchange(): return lax.all_to_all(parts, axes, 0, 0, tiled=True)]
    ppermute x12, starting transfers between devices: 35.3 us -> 25.5 us  [swap(): return lax.ppermute(block, 'core', [(0, 1), (1, 0)])]
    all_to_all x3 -> x2, starting transfers between devices: 24.2 us -> 17.5 us  [exchange(): return lax.all_to_all(parts, axes, 0, 0, tiled=True)]
    pallas_call x0 -> x3, Pallas kernels: none -> 5.1 us  [widen(): pl.pallas_call(body, out_shape=pltpu.HBM((rows, 2 * wide), bf16), in_spec...]
    pallas_call x11 -> x8, Pallas kernels: 8.79 us -> 4.3 us  [call(): pl.pallas_call(body, out_shape=[jax.ShapeDtypeStruct(s, t) for s, t in ou...]
    unnamed x70 -> x58, local copies, waits for them, and re-layouts: 6.47 us -> 2.58 us
    all_to_all x3 -> x2, waiting for transfers between devices: 7.82 us -> 6.12 us  [exchange(): return lax.all_to_all(parts, axes, 0, 0, tiled=True)]
    dot_general x2 -> x4, matrix products: 5.73 us -> 7.1 us  [t_dot(): lax.dot_general(a, b, (((0,), (0,)), ((), ())), preferred_element_type=f32)]
  transfers between devices with their start and end apart: 15 -> 14, of which waited for: 7 -> 4; matrix products, arithmetic and copies ran while one was open for 7% -> 7% of each run, Pallas kernels for 0% -> 0%
where the time goes in v6:
time: 210 us; the launch traced here: 209 us
  blocking collectives  128 us (61%)
  starting transfers between devices  43 us (20%)
  matrix products  9.83 us (5%)
  Pallas kernels  9.4 us (4%)
  waiting for transfers between devices  8.28 us (4%)
  local copies, waits for them, and re-layouts  6.83 us (3%)
  other arithmetic  2.75 us (1%)
    all_to_all x9, blocking collectives, exchange(): return lax.all_to_all(parts, axes, 0, 0, tiled=True)  128 us
    ppermute x12, starting transfers between devices, swap(): return lax.ppermute(block, 'core', [(0, 1), (1, 0)])  25.5 us
    all_to_all x2, starting transfers between devices, exchange(): return lax.all_to_all(parts, axes, 0, 0, tiled=True)  17.5 us
    dot_general x4, matrix products, t_dot(): lax.dot_general(a, b, (((0,), (0,)), ((), ())), preferred_element_type=f32)  7.1 us
    all_to_all x2, waiting for transfers between devices, exchange(): return lax.all_to_all(parts, axes, 0, 0, tiled=True)  6.12 us
    pallas_call x3, Pallas kernels, widen(): pl.pallas_call(body, out_shape=pltpu.HBM((rows, 2 * wide), bf16), in_spec...  5.1 us
    pallas_call x8, Pallas kernels, call(): pl.pallas_call(body, out_shape=[jax.ShapeDtypeStruct(s, t) for s, t in ou...  4.3 us
  transfers between devices with their start and end apart: 14, of which 4 were waited for; matrix products, arithmetic and copies ran while one was open for 7% of the time, Pallas kernels for 0%

profile of v6, /device:TPU:1, one launch (start us, length us, event | category | flops | bytes accessed | tf_op | source)
XLA Modules:
  0.0 209.0 jit_solution(8579687750522476805)
XLA Ops:
  0.7 1.6 fusion.20
  2.4 0.5 convolution_convert_fusion.2
  3.0 3.2 %collective-permute-start = (bf16[256,768]{1,0:T(8,128)(2,1)S(1)}, bf16[256,768]{1,0:T(8,128)(2,1)S(1)}, u32[]{:S(2)}, u32[]{:S(2)}) collective-permute-start(bf16[256,768]{1,0:T(8,128)(2,1)S(1)} %convolution_convert_fusion.2), channel_id=1, source_target_pairs={{0,32},{32,0},{1,33},{33,1},{2,34},{34,2},{3,35},{35,3},{4,36},{36... | collective-permute-start | bytes 1179656 | tf_op jit(solution)/shard_map/ppermute | solution.py:182
  6.3 0.5 collective-permute-start.2
  6.8 0.8 collective-permute-done
  7.6 0.5 add_convert_fusion
  8.1 10.1 %all_to_all.55.l_ref = bf16[4,64,768]{2,1,0:T(8,128)(2,1)S(1)} all-to-all(bf16[4,64,768]{2,1,0:T(8,128)(2,1)S(1)} %bitcast.63), channel_id=1, replica_groups=mesh['y'=4,'core'=2,'x'=4,'z'=8] {'y'}, dimensions={0} | all-to-all | bytes 786432 | tf_op jit(solution)/shard_map/all_to_all | solution.py:191
  18.3 8.8 %all_to_all.56 = bf16[4,64,768]{2,1,0:T(8,128)(2,1)S(1)} all-to-all(bf16[4,64,768]{2,1,0:T(8,128)(2,1)S(1)} %get-tuple-element.26), channel_id=1, replica_groups=mesh['y'=4,'core'=2,'x'=4,'z'=8] {'y'}, dimensions={0} | all-to-all | bytes 786432 | tf_op jit(solution)/shard_map/all_to_all | solution.py:191
  27.2 1.7 shard_map.77
  28.9 10.3 %all-to-all-start.2 = ((bf16[32,8,1536]{2,1,0:T(8,128)(2,1)}), bf16[32,8,1536]{2,1,0:T(8,128)(2,1)}, u32[]{:S(2)}, u32[]{:S(2)}) async-start(bf16[32,8,1536]{2,1,0:T(8,128)(2,1)} %bitcast.60), calls=%async_computation.2 | async-start | bytes 1572864 | tf_op jit(solution)/shard_map/all_to_all | solution.py:191
  39.3 3.3 %collective-permute-start.6 = (bf16[256,768]{1,0:T(8,128)(2,1)}, bf16[256,768]{1,0:T(8,128)(2,1)}, u32[]{:S(2)}, u32[]{:S(2)}) collective-permute-start(bf16[256,768]{1,0:T(8,128)(2,1)} %copy-done.25), channel_id=1, source_target_pairs={{0,32},{32,0},{1,33},{33,1},{2,34},{34,2},{3,35},{35,3},{4,36},{36... | collective-permute-start | bytes 1179656 | tf_op jit(solution)/shard_map/ppermute | solution.py:182
  42.6 0.9 constant_dynamic-slice_fusion.3
  43.6 0.8 dynamic-slice_add_fusion
  44.5 0.5 collective-permute-start.5
  45.0 1.4 fusion.22
  46.6 0.5 fusion.32
  47.1 0.6 pad_maximum_fusion.7.a_ref
  47.8 0.6 pad_maximum_fusion.8.a_ref
  48.4 1.3 fusion
  49.7 6.1 %all-to-all-done.2.l_ref = bf16[32,8,1536]{2,1,0:T(8,128)(2,1)} async-done(((bf16[32,8,1536]{2,1,0:T(8,128)(2,1)}), bf16[32,8,1536]{2,1,0:T(8,128)(2,1)}, u32[]{:S(2)}, u32[]{:S(2)}) %all-to-all-start.2) | async-done | bytes 786464 | tf_op jit(solution)/shard_map/all_to_all | solution.py:191
  55.8 0.8 copy-done.16
  56.6 1.9 shard_map.78
  58.5 24.3 %all_to_all.57 = bf16[32,8,1536]{2,1,0:T(8,128)(2,1)S(1)} all-to-all(bf16[32,8,1536]{2,1,0:T(8,128)(2,1)S(1)} %get-tuple-element.30), channel_id=1, replica_groups=mesh['y'=4,'core'=2,'x'=4,'z'=8] {'x','z'}, dimensions={0} | all-to-all | bytes 1572864 | tf_op jit(solution)/shard_map/all_to_all | solution.py:191
  82.8 0.8 shard_map.79
  83.7 0.4 copy-done.26
  84.1 10.7 %all_to_all.58.l_ref = bf16[4,64,1536]{2,1,0:T(8,128)(2,1)S(1)} all-to-all(bf16[4,64,1536]{2,1,0:T(8,128)(2,1)S(1)} %pad_maximum_fusion), channel_id=1, replica_groups=mesh['y'=4,'core'=2,'x'=4,'z'=8] {'y'}, dimensions={0} | all-to-all | bytes 1572864 | tf_op jit(solution)/shard_map/all_to_all | solution.py:191
  94.8 0.3 shard_map.80
  95.1 12.4 %all_to_all.59 = bf16[4,64,1536]{2,1,0:T(8,128)(2,1)S(1)} all-to-all(bf16[4,64,1536]{2,1,0:T(8,128)(2,1)S(1)} %shard_map.80), channel_id=1, replica_groups=mesh['y'=4,'core'=2,'x'=4,'z'=8] {'y'}, dimensions={0} | all-to-all | bytes 1572864 | tf_op jit(solution)/shard_map/all_to_all | solution.py:191
  107.5 1.7 shard_map.81
  109.3 21.7 %all_to_all.60.l_ref = bf16[32,8,1536]{2,1,0:T(8,128)(2,1)S(1)} all-to-all(bf16[32,8,1536]{2,1,0:T(8,128)(2,1)} %bitcast.62), channel_id=1, replica_groups=mesh['y'=4,'core'=2,'x'=4,'z'=8] {'x','z'}, dimensions={0} | all-to-all | bytes 1572864 | tf_op jit(solution)/shard_map/all_to_all | solution.py:191
  131.1 21.6 %all_to_all.61 = bf16[32,8,1536]{2,1,0:T(8,128)(2,1)S(1)} all-to-all(bf16[32,8,1536]{2,1,0:T(8,128)(2,1)S(1)} %get-tuple-element.34), channel_id=1, replica_groups=mesh['y'=4,'core'=2,'x'=4,'z'=8] {'x','z'}, dimensions={0} | all-to-all | bytes 1572864 | tf_op jit(solution)/shard_map/all_to_all | solution.py:191
  152.7 0.8 shard_map.83
  153.6 8.6 %all_to_all.62.l_ref = bf16[4,64,768]{2,1,0:T(8,128)(2,1)S(1)} all-to-all(bf16[4,64,768]{2,1,0:T(8,128)(2,1)S(1)} %bitcast.59), channel_id=1, replica_groups=mesh['y'=4,'core'=2,'x'=4,'z'=8] {'y'}, dimensions={0} | all-to-all | bytes 786432 | tf_op jit(solution)/shard_map/all_to_all | solution.py:191
  162.2 0.2 shard_map.84
  162.4 9.5 %all_to_all.63 = bf16[4,64,768]{2,1,0:T(8,128)(2,1)S(1)} all-to-all(bf16[4,64,768]{2,1,0:T(8,128)(2,1)S(1)} %shard_map.84), channel_id=1, replica_groups=mesh['y'=4,'core'=2,'x'=4,'z'=8] {'y'}, dimensions={0} | all-to-all | bytes 786432 | tf_op jit(solution)/shard_map/all_to_all | solution.py:191
  171.9 1.7 shard_map.85
  173.7 7.2 %all-to-all-start.10 = ((bf16[32,8,1536]{2,1,0:T(8,128)(2,1)}), bf16[32,8,1536]{2,1,0:T(8,128)(2,1)S(1)}, u32[]{:S(2)}, u32[]{:S(2)}) async-start(bf16[32,8,1536]{2,1,0:T(8,128)(2,1)} %bitcast.61), calls=%async_computation.10 | async-start | bytes 1572864 | tf_op jit(solution)/shard_map/all_to_all | solution.py:191
  181.1 0.9 copy-done.14
  182.0 1.8 convolution_convert_fusion.1
  183.9 10.7 %collective-permute-start.7 = (bf16[384,768]{1,0:T(8,128)(2,1)S(1)}, bf16[384,768]{1,0:T(8,128)(2,1)S(1)}, u32[]{:S(2)}, u32[]{:S(2)}) collective-permute-start(bf16[384,768]{1,0:T(8,128)(2,1)S(1)} %get-tuple-element.57), channel_id=1, source_target_pairs={{0,32},{32,0},{1,33},{33,1},{2,34},{34,2},{3,35},{35,3},{4,36},{36... | collective-permute-start | bytes 1769480 | tf_op jit(solution)/shard_map/ppermute | solution.py:182
  194.8 0.8 convolution_convert_fusion
  195.7 0.9 collective-permute-start.9
  196.7 0.5 collective-permute-done.8
  197.1 2.2 %convert_add_fusion.1 = f32[768,768]{1,0:T(8,128)} fusion(bf16[384,768]{1,0:T(8,128)(2,1)S(1)} %collective-permute-done.8, bf16[384,768]{1,0:T(8,128)(2,1)S(1)} %collective-permute-done.7, bf16[256,768]{1,0:T(8,128)(2,1)S(1)} %get-tuple-element.63, bf16[256,768]{1,0:T(8,128)(2,1)S(1)} %copy-done.22, bf16[256,768]{1,0:T(8,128)(2,1)S(1)} %get-tuple-element.67, ...), kind=kOutput, calls=%fused_computation.1 | convolution fusion | flops 610074624 | bytes 5111808 | tf_op jit(solution)/shard_map/dot_general | solution.py:39
  199.4 2.2 %convert_add_fusion = f32[768,768]{1,0:T(8,128)} fusion(bf16[384,768]{1,0:T(8,128)(2,1)S(1)} %collective-permute-done.10, bf16[384,768]{1,0:T(8,128)(2,1)S(1)} %collective-permute-done.9, bf16[256,768]{1,0:T(8,128)(2,1)S(1)} %copy-done.24, bf16[256,768]{1,0:T(8,128)(2,1)S(1)} %get-tuple-element.59, bf16[256,768]{1,0:T(8,128)(2,1)S(1)} %get-tuple-element.68, ...), kind=kOutput, calls=%fused_computation | convolution fusion | flops 610074624 | bytes 5111808 | tf_op jit(solution)/shard_map/dot_general | solution.py:39
  201.8 5.7 %collective-permute-start.11 = (f32[8,768]{1,0:T(8,128)S(1)}, f32[8,768]{1,0:T(8,128)S(1)}, u32[]{:S(2)}, u32[]{:S(2)}) collective-permute-start(f32[8,768]{1,0:T(8,128)S(1)} %get-tuple-element.46), channel_id=1, source_target_pairs={{0,32},{32,0},{1,33},{33,1},{2,34},{34,2},{3,35},{35,3},{4,36},{36... | collective-permute-start | bytes 73736 | tf_op jit(solution)/shard_map/ppermute | solution.py:182
  207.5 0.8 collective-permute-done.11
  208.4 0.6 maximum_select_fusion
  (79 shorter events, 1.8 us)
Async XLA Ops:
  0.6 1.7 copy-start
  0.6 5.7 %copy-start.1 = (bf16[768,768]{1,0:T(8,128)(2,1)S(1)}, bf16[768,768]{1,0:T(8,128)(2,1)}, u32[]{:S(2)}) copy-start(bf16[768,768]{1,0:T(8,128)(2,1)} %a_ref.8) | copy-start | bytes 3538948
  2.3 0.8 copy-start.25
  2.3 5.8 %copy-start.21 = (bf16[256,768]{1,0:T(8,128)(2,1)}, bf16[256,768]{1,0:T(8,128)(2,1)S(1)}, u32[]{:S(2)}) copy-start(bf16[256,768]{1,0:T(8,128)(2,1)S(1)} %get-tuple-element.54) | copy-start | bytes 1179652
  3.0 4.6 %collective-permute-start = (bf16[256,768]{1,0:T(8,128)(2,1)S(1)}, bf16[256,768]{1,0:T(8,128)(2,1)S(1)}, u32[]{:S(2)}, u32[]{:S(2)}) collective-permute-start(bf16[256,768]{1,0:T(8,128)(2,1)S(1)} %convolution_convert_fusion.2), channel_id=1, source_target_pairs={{0,32},{32,0},{1,33},{33,1},{2,34},{34,2},{3,35},{35,3},{4,36},{36... | collective-permute-start | bytes 1179656 | tf_op jit(solution)/shard_map/ppermute | solution.py:182
  6.3 20.9 %collective-permute-start.1 = (bf16[768,768]{1,0:T(8,128)(2,1)S(1)}, bf16[768,768]{1,0:T(8,128)(2,1)S(1)}, u32[]{:S(2)}, u32[]{:S(2)}) collective-permute-start(bf16[768,768]{1,0:T(8,128)(2,1)S(1)} %copy-done), channel_id=1, source_target_pairs={{0,32},{32,0},{1,33},{33,1},{2,34},{34,2},{3,35},{35,3},{4,36},{36... | collective-permute-start | bytes 3538952 | tf_op jit(solution)/shard_map/ppermute | solution.py:182
  6.3 20.9 %collective-permute-start.2 = (bf16[768,768]{1,0:T(8,128)(2,1)S(1)}, bf16[768,768]{1,0:T(8,128)(2,1)S(1)}, u32[]{:S(2)}, u32[]{:S(2)}) collective-permute-start(bf16[768,768]{1,0:T(8,128)(2,1)S(1)} %copy-done.1), channel_id=1, source_target_pairs={{0,32},{32,0},{1,33},{33,1},{2,34},{34,2},{3,35},{35,3},{4,36},{36... | collective-permute-start | bytes 3538952 | tf_op jit(solution)/shard_map/ppermute | solution.py:182
  18.3 10.6 %copy-start.17 = (bf16[64,768]{1,0:T(8,128)(2,1)}, bf16[64,768]{1,0:T(8,128)(2,1)S(1)}, u32[]{:S(2)}) copy-start(bf16[64,768]{1,0:T(8,128)(2,1)S(1)} %get-tuple-element.35.p_ref) | copy-start | bytes 294916
  27.2 1.7 copy-start.11
  27.2 1.7 copy-start.2
  28.9 26.9 %all-to-all-start.2 = ((bf16[32,8,1536]{2,1,0:T(8,128)(2,1)}), bf16[32,8,1536]{2,1,0:T(8,128)(2,1)}, u32[]{:S(2)}, u32[]{:S(2)}) async-start(bf16[32,8,1536]{2,1,0:T(8,128)(2,1)} %bitcast.60), calls=%async_computation.2 | async-start | bytes 1572864 | tf_op jit(solution)/shard_map/all_to_all | solution.py:191
  39.3 10.4 %collective-permute-start.6 = (bf16[256,768]{1,0:T(8,128)(2,1)}, bf16[256,768]{1,0:T(8,128)(2,1)}, u32[]{:S(2)}, u32[]{:S(2)}) collective-permute-start(bf16[256,768]{1,0:T(8,128)(2,1)} %copy-done.25), channel_id=1, source_target_pairs={{0,32},{32,0},{1,33},{33,1},{2,34},{34,2},{3,35},{35,3},{4,36},{36... | collective-permute-start | bytes 1179656 | tf_op jit(solution)/shard_map/ppermute | solution.py:182
  43.5 3.6 %collective-permute-start.4 = (f32[8,768]{1,0:T(8,128)S(1)}, f32[8,768]{1,0:T(8,128)S(1)}, u32[]{:S(2)}, u32[]{:S(2)}) collective-permute-start(f32[8,768]{1,0:T(8,128)S(1)} %get-tuple-element.50), channel_id=1, source_target_pairs={{0,32},{32,0},{1,33},{33,1},{2,34},{34,2},{3,35},{35,3},{4,36},{36... | collective-permute-start | bytes 73736 | tf_op jit(solution)/shard_map/ppermute | solution.py:182
  44.5 3.3 %collective-permute-start.5 = (f32[8,768]{1,0:T(8,128)S(1)}, f32[8,768]{1,0:T(8,128)S(1)}, u32[]{:S(2)}, u32[]{:S(2)}) collective-permute-start(f32[8,768]{1,0:T(8,128)S(1)} %get-tuple-element.66), channel_id=1, source_target_pairs={{0,32},{32,0},{1,33},{33,1},{2,34},{34,2},{3,35},{35,3},{4,36},{36... | collective-permute-start | bytes 73736 | tf_op jit(solution)/shard_map/ppermute | solution.py:182
  46.4 3.2 %copy-start.23 = (bf16[256,768]{1,0:T(8,128)(2,1)}, bf16[256,768]{1,0:T(8,128)(2,1)S(1)}, u32[]{:S(2)}) copy-start(bf16[256,768]{1,0:T(8,128)(2,1)S(1)} %get-tuple-element.52) | copy-start | bytes 1179652
  46.5 1.9 copy-start.3
  46.5 1.9 collective-permute-start.3
  48.4 1.3 copy-start.27
  55.8 0.8 copy-start.16
  82.8 0.9 copy-start.5
  82.8 1.3 copy-start.26
  107.5 1.7 copy-start.9
  109.2 21.7 %copy-start.15 = (f32[8,1536]{1,0:T(8,128)S(1)}, f32[8,1536]{1,0:T(8,128)}, u32[]{:S(2)}) copy-start(f32[8,1536]{1,0:T(8,128)} %pad_maximum_fusion.8.a_ref) | copy-start | bytes 147460
  130.9 21.8 %copy-start.4 = (bf16[768,768]{1,0:T(8,128)(2,1)S(1)}, bf16[768,768]{1,0:T(8,128)(2,1)}, u32[]{:S(2)}) copy-start(bf16[768,768]{1,0:T(8,128)(2,1)} %copy-done.2) | copy-start | bytes 3538948
  131.1 21.7 %copy-start.19 = (f32[8,1536]{1,0:T(8,128)}, f32[8,1536]{1,0:T(8,128)S(1)}, u32[]{:S(2)}) copy-start(f32[8,1536]{1,0:T(8,128)S(1)} %get-tuple-element.44.a_ref) | copy-start | bytes 147460
  152.7 0.9 copy-start.7
  152.7 9.5 %copy-start.18 = (bf16[64,768]{1,0:T(8,128)(2,1)S(1)}, bf16[64,768]{1,0:T(8,128)(2,1)}, u32[]{:S(2)}) copy-start(bf16[64,768]{1,0:T(8,128)(2,1)} %copy-done.17) | copy-start | bytes 294916
  171.9 1.7 copy-start.13
  173.7 7.2 %copy-start.6 = (bf16[32,8,1536]{2,1,0:T(8,128)(2,1)S(1)}, bf16[32,8,1536]{2,1,0:T(8,128)(2,1)}, u32[]{:S(2)}) copy-start(bf16[32,8,1536]{2,1,0:T(8,128)(2,1)} %copy-done.5) | copy-start | bytes 2359300
  173.7 7.3 %copy-start.8 = (bf16[32,8,1536]{2,1,0:T(8,128)(2,1)S(1)}, bf16[32,8,1536]{2,1,0:T(8,128)(2,1)}, u32[]{:S(2)}) copy-start(bf16[32,8,1536]{2,1,0:T(8,128)(2,1)} %copy-done.7) | copy-start | bytes 2359300
  173.7 7.3 %copy-start.10 = (bf16[4,64,1536]{2,1,0:T(8,128)(2,1)S(1)}, bf16[4,64,1536]{2,1,0:T(8,128)(2,1)}, u32[]{:S(2)}) copy-start(bf16[4,64,1536]{2,1,0:T(8,128)(2,1)} %copy-done.9) | copy-start | bytes 2359300
  173.7 27.9 %all-to-all-start.10 = ((bf16[32,8,1536]{2,1,0:T(8,128)(2,1)}), bf16[32,8,1536]{2,1,0:T(8,128)(2,1)S(1)}, u32[]{:S(2)}, u32[]{:S(2)}) async-start(bf16[32,8,1536]{2,1,0:T(8,128)(2,1)} %bitcast.61), calls=%async_computation.10 | async-start | bytes 1572864 | tf_op jit(solution)/shard_map/all_to_all | solution.py:191
  181.0 1.0 copy-start.14
  183.8 11.0 %copy-start.12 = (bf16[4,64,768]{2,1,0:T(8,128)(2,1)S(1)}, bf16[4,64,768]{2,1,0:T(8,128)(2,1)}, u32[]{:S(2)}) copy-start(bf16[4,64,768]{2,1,0:T(8,128)(2,1)} %copy-done.11) | copy-start | bytes 1179652
  183.8 10.9 %copy-start.28 = (bf16[256,768]{1,0:T(8,128)(2,1)S(1)}, bf16[256,768]{1,0:T(8,128)(2,1)}, u32[]{:S(2)}) copy-start(bf16[256,768]{1,0:T(8,128)(2,1)} %copy-done.27) | copy-start | bytes 1179652
  183.9 12.8 %collective-permute-start.7 = (bf16[384,768]{1,0:T(8,128)(2,1)S(1)}, bf16[384,768]{1,0:T(8,128)(2,1)S(1)}, u32[]{:S(2)}, u32[]{:S(2)}) collective-permute-start(bf16[384,768]{1,0:T(8,128)(2,1)S(1)} %get-tuple-element.57), channel_id=1, source_target_pairs={{0,32},{32,0},{1,33},{33,1},{2,34},{34,2},{3,35},{35,3},{4,36},{36... | collective-permute-start | bytes 1769480 | tf_op jit(solution)/shard_map/ppermute | solution.py:182
  194.6 2.5 %collective-permute-start.8 = (bf16[384,768]{1,0:T(8,128)(2,1)S(1)}, bf16[384,768]{1,0:T(8,128)(2,1)S(1)}, u32[]{:S(2)}, u32[]{:S(2)}) collective-permute-start(bf16[384,768]{1,0:T(8,128)(2,1)S(1)} %get-tuple-element.58), channel_id=1, source_target_pairs={{0,32},{32,0},{1,33},{33,1},{2,34},{34,2},{3,35},{35,3},{4,36},{36... | collective-permute-start | bytes 1769480 | tf_op jit(solution)/shard_map/ppermute | solution.py:182
  195.6 1.6 copy-start.22
  195.7 3.7 %collective-permute-start.9 = (bf16[384,768]{1,0:T(8,128)(2,1)S(1)}, bf16[384,768]{1,0:T(8,128)(2,1)S(1)}, u32[]{:S(2)}, u32[]{:S(2)}) collective-permute-start(bf16[384,768]{1,0:T(8,128)(2,1)S(1)} %get-tuple-element.55), channel_id=1, source_target_pairs={{0,32},{32,0},{1,33},{33,1},{2,34},{34,2},{3,35},{35,3},{4,36},{36... | collective-permute-start | bytes 1769480 | tf_op jit(solution)/shard_map/ppermute | solution.py:182
  196.6 2.8 %collective-permute-start.10 = (bf16[384,768]{1,0:T(8,128)(2,1)S(1)}, bf16[384,768]{1,0:T(8,128)(2,1)S(1)}, u32[]{:S(2)}, u32[]{:S(2)}) collective-permute-start(bf16[384,768]{1,0:T(8,128)(2,1)S(1)} %get-tuple-element.56), channel_id=1, source_target_pairs={{0,32},{32,0},{1,33},{33,1},{2,34},{34,2},{3,35},{35,3},{4,36},{36... | collective-permute-start | bytes 1769480 | tf_op jit(solution)/shard_map/ppermute | solution.py:182
  197.1 2.3 %copy-start.24 = (bf16[256,768]{1,0:T(8,128)(2,1)S(1)}, bf16[256,768]{1,0:T(8,128)(2,1)}, u32[]{:S(2)}) copy-start(bf16[256,768]{1,0:T(8,128)(2,1)} %copy-done.23) | copy-start | bytes 1179652
  199.4 2.3 %copy-start.20 = (f32[8,1536]{1,0:T(8,128)S(1)}, f32[8,1536]{1,0:T(8,128)}, u32[]{:S(2)}) copy-start(f32[8,1536]{1,0:T(8,128)} %copy-done.19) | copy-start | bytes 147460
  201.8 6.6 %collective-permute-start.11 = (f32[8,768]{1,0:T(8,128)S(1)}, f32[8,768]{1,0:T(8,128)S(1)}, u32[]{:S(2)}, u32[]{:S(2)}) collective-permute-start(f32[8,768]{1,0:T(8,128)S(1)} %get-tuple-element.46), channel_id=1, source_target_pairs={{0,32},{32,0},{1,33},{33,1},{2,34},{34,2},{3,35},{35,3},{4,36},{36... | collective-permute-start | bytes 73736 | tf_op jit(solution)/shard_map/ppermute | solution.py:182

commit v7 on v6

--- a/solution.py
+++ b/solution.py
@@ -82,16 +82,30 @@
     )(rows_deep, own_block, other_block)
 
 
-def narrow(product, rows_wide, own_block, other_block):
+def widen_near(product, rows_deep, own_block, other_block):
+    rows, wide = rows_deep.shape[0], own_block.shape[0]
+
+    def body(x_ref, a_ref, b_ref, o_ref):
+        o_ref[:, :wide] = product(x_ref[:, :wide], a_ref[...]).astype(bf16)
+        o_ref[:, wide:] = product(x_ref[:, :wide], b_ref[...]).astype(bf16)
+
+    return call(
+        body, [((rows, 2 * wide), bf16)], rows_deep, own_block, other_block, flops=4 * rows * wide * wide
+    )
+
+
+def narrow(product, rows_wide, own_block, other_block, beside=None):
     rows, wide = rows_wide.shape[0], rows_wide.shape[1] // 2
-
-    def body(x_ref, a_ref, b_ref, o_ref):
+    more = [] if beside is None else [beside]
+
+    def body(x_ref, a_ref, b_ref, *refs):
         total = product(x_ref[:, :wide], a_ref[...]) + product(x_ref[:, wide:], b_ref[...])
-        o_ref[...] = total.astype(bf16)
-
-    return call(
-        body, [((rows, wide), bf16)], rows_wide, own_block, other_block, flops=4 * rows * wide * wide
-    )
+        refs[-1][:, :wide] = total.astype(bf16)
+        if more:
+            refs[-1][:, wide:] = refs[0][...]
+
+    out = ((rows, wide * (1 + len(more))), bf16)
+    return call(body, [out], rows_wide, own_block, other_block, *more, flops=4 * rows * wide * wide)
 
 
 def add_up(ref, columns):
@@ -244,12 +258,11 @@
     latent_one, input_one = sum_and_copy(landed, start_rows)
     input_one = exchange(input_one, HIDDEN).reshape(half, 2 * wide)
 
-    pre_part = narrow(dot, input_one, w_up, up_other)
-    both = jnp.concatenate([pre_part.reshape(n_y, quarter, deep), back_part.reshape(n_y, quarter, deep)], axis=2)
+    both = narrow(dot, input_one, w_up, up_other, back_part).reshape(n_y, quarter, 2 * deep)
     one = activate_and_back(exchange(both, "y"))
     one = exchange(one, "y").reshape(half, 2 * deep)
 
-    part = widen(dot_t, one, w_up, up_other, True)
+    part = widen_near(dot_t, one, w_up, up_other)
     landed = exchange(part.reshape(n_h, eight, 2 * wide), HIDDEN)
     grad_one, error_one = sum_and_copy(landed, target_rows)
     error_one = exchange(error_one, HIDDEN).reshape(half, 2 * wide)

time: 210 us -> 209 us (level)
    pallas_call x3 -> x2, Pallas kernels: 5.1 us -> 3.4 us  [widen(): pl.pallas_call(body, out_shape=pltpu.HBM((rows, 2 * wide), bf16), in_spec...]
    pallas_call x8 -> x9, Pallas kernels: 4.3 us -> 5.23 us  [call(): pl.pallas_call(body, out_shape=[jax.ShapeDtypeStruct(s, t) for s, t in ou...]
where the time goes in v7:
time: 209 us; the launch traced here: 208 us
  blocking collectives  129 us (62%)
  starting transfers between devices  43.2 us (21%)
  matrix products  9.83 us (5%)
  Pallas kernels  8.63 us (4%)
  waiting for transfers between devices  8.28 us (4%)
  local copies, waits for them, and re-layouts  5.48 us (3%)
  other arithmetic  2.7 us (1%)
    all_to_all x9, blocking collectives, exchange(): return lax.all_to_all(parts, axes, 0, 0, tiled=True)  129 us
    ppermute x12, starting transfers between devices, swap(): return lax.ppermute(block, 'core', [(0, 1), (1, 0)])  26.5 us
    all_to_all x2, starting transfers between devices, exchange(): return lax.all_to_all(parts, axes, 0, 0, tiled=True)  16.7 us
    dot_general x4, matrix products, t_dot(): lax.dot_general(a, b, (((0,), (0,)), ((), ())), preferred_element_type=f32)  7.09 us
    all_to_all x2, waiting for transfers between devices, exchange(): return lax.all_to_all(parts, axes, 0, 0, tiled=True)  6.12 us
    pallas_call x9, Pallas kernels, call(): pl.pallas_call(body, out_shape=[jax.ShapeDtypeStruct(s, t) for s, t in ou...  5.23 us
  transfers between devices with their start and end apart: 14, of which 4 were waited for; matrix products, arithmetic and copies ran while one was open for 7% of the time, Pallas kernels for 0%

profile of v7, /device:TPU:1, one launch (start us, length us, event | category | flops | bytes accessed | tf_op | source)
XLA Modules:
  0.0 207.8 jit_solution(15057886329914606429)
XLA Ops:
  0.7 1.6 fusion.20
  2.4 0.5 convolution_convert_fusion.2
  2.9 3.3 %collective-permute-start = (bf16[256,768]{1,0:T(8,128)(2,1)S(1)}, bf16[256,768]{1,0:T(8,128)(2,1)S(1)}, u32[]{:S(2)}, u32[]{:S(2)}) collective-permute-start(bf16[256,768]{1,0:T(8,128)(2,1)S(1)} %convolution_convert_fusion.2), channel_id=1, source_target_pairs={{0,32},{32,0},{1,33},{33,1},{2,34},{34,2},{3,35},{35,3},{4,36},{36... | collective-permute-start | bytes 1179656 | tf_op jit(solution)/shard_map/ppermute | solution.py:196
  6.3 0.4 collective-permute-start.2
  6.7 0.8 collective-permute-done
  7.5 0.5 add_convert_fusion
  8.0 10.1 %all_to_all.55.l_ref = bf16[4,64,768]{2,1,0:T(8,128)(2,1)S(1)} all-to-all(bf16[4,64,768]{2,1,0:T(8,128)(2,1)S(1)} %bitcast.62), channel_id=1, replica_groups=mesh['y'=4,'core'=2,'x'=4,'z'=8] {'y'}, dimensions={0} | all-to-all | bytes 786432 | tf_op jit(solution)/shard_map/all_to_all | solution.py:205
  18.2 8.8 %all_to_all.56 = bf16[4,64,768]{2,1,0:T(8,128)(2,1)S(1)} all-to-all(bf16[4,64,768]{2,1,0:T(8,128)(2,1)S(1)} %get-tuple-element.26), channel_id=1, replica_groups=mesh['y'=4,'core'=2,'x'=4,'z'=8] {'y'}, dimensions={0} | all-to-all | bytes 786432 | tf_op jit(solution)/shard_map/all_to_all | solution.py:205
  27.1 1.7 shard_map.77
  28.8 10.3 %all-to-all-start.2 = ((bf16[32,8,1536]{2,1,0:T(8,128)(2,1)}), bf16[32,8,1536]{2,1,0:T(8,128)(2,1)}, u32[]{:S(2)}, u32[]{:S(2)}) async-start(bf16[32,8,1536]{2,1,0:T(8,128)(2,1)} %bitcast.60), calls=%async_computation.2 | async-start | bytes 1572864 | tf_op jit(solution)/shard_map/all_to_all | solution.py:205
  39.2 3.3 %collective-permute-start.6 = (bf16[256,768]{1,0:T(8,128)(2,1)}, bf16[256,768]{1,0:T(8,128)(2,1)}, u32[]{:S(2)}, u32[]{:S(2)}) collective-permute-start(bf16[256,768]{1,0:T(8,128)(2,1)} %copy-done.23), channel_id=1, source_target_pairs={{0,32},{32,0},{1,33},{33,1},{2,34},{34,2},{3,35},{35,3},{4,36},{36... | collective-permute-start | bytes 1179656 | tf_op jit(solution)/shard_map/ppermute | solution.py:196
  42.5 0.9 constant_dynamic-slice_fusion.3
  43.4 0.1 collective-permute-start.4
  43.5 0.8 dynamic-slice_add_fusion
  44.4 0.5 collective-permute-start.5
  44.9 1.4 fusion.22
  46.4 0.1 collective-permute-start.3
  46.5 0.5 fusion.32
  47.0 0.6 pad_maximum_fusion.6.a_ref
  47.7 0.6 pad_maximum_fusion.7.a_ref
  48.3 1.3 fusion.refs_0_
  49.6 6.1 %all-to-all-done.2.l_ref = bf16[32,8,1536]{2,1,0:T(8,128)(2,1)} async-done(((bf16[32,8,1536]{2,1,0:T(8,128)(2,1)}), bf16[32,8,1536]{2,1,0:T(8,128)(2,1)}, u32[]{:S(2)}, u32[]{:S(2)}) %all-to-all-start.2) | async-done | bytes 786464 | tf_op jit(solution)/shard_map/all_to_all | solution.py:205
  55.7 0.8 copy-done.14
  56.5 2.0 shard_map.78
  58.5 24.3 %all_to_all.57 = bf16[32,8,1536]{2,1,0:T(8,128)(2,1)S(1)} all-to-all(bf16[32,8,1536]{2,1,0:T(8,128)(2,1)S(1)} %get-tuple-element.30), channel_id=1, replica_groups=mesh['y'=4,'core'=2,'x'=4,'z'=8] {'x','z'}, dimensions={0} | all-to-all | bytes 1572864 | tf_op jit(solution)/shard_map/all_to_all | solution.py:205
  82.8 0.8 shard_map.79
  83.7 10.7 %all_to_all.58.l_ref = bf16[4,64,1536]{2,1,0:T(8,128)(2,1)S(1)} all-to-all(bf16[4,64,1536]{2,1,0:T(8,128)(2,1)S(1)} %bitcast.51), channel_id=1, replica_groups=mesh['y'=4,'core'=2,'x'=4,'z'=8] {'y'}, dimensions={0} | all-to-all | bytes 1572864 | tf_op jit(solution)/shard_map/all_to_all | solution.py:205
  94.4 0.3 shard_map.80
  94.7 12.4 %all_to_all.59 = bf16[4,64,1536]{2,1,0:T(8,128)(2,1)S(1)} all-to-all(bf16[4,64,1536]{2,1,0:T(8,128)(2,1)S(1)} %shard_map.80), channel_id=1, replica_groups=mesh['y'=4,'core'=2,'x'=4,'z'=8] {'y'}, dimensions={0} | all-to-all | bytes 1572864 | tf_op jit(solution)/shard_map/all_to_all | solution.py:205
  107.1 0.8 shard_map.81
  108.0 21.5 %all_to_all.60.l_ref = bf16[32,8,1536]{2,1,0:T(8,128)(2,1)S(1)} all-to-all(bf16[32,8,1536]{2,1,0:T(8,128)(2,1)S(1)} %bitcast.52), channel_id=1, replica_groups=mesh['y'=4,'core'=2,'x'=4,'z'=8] {'x','z'}, dimensions={0} | all-to-all | bytes 1572864 | tf_op jit(solution)/shard_map/all_to_all | solution.py:205
  129.7 21.9 %all_to_all.61 = bf16[32,8,1536]{2,1,0:T(8,128)(2,1)S(1)} all-to-all(bf16[32,8,1536]{2,1,0:T(8,128)(2,1)S(1)} %get-tuple-element.34), channel_id=1, replica_groups=mesh['y'=4,'core'=2,'x'=4,'z'=8] {'x','z'}, dimensions={0} | all-to-all | bytes 1572864 | tf_op jit(solution)/shard_map/all_to_all | solution.py:205
  151.6 0.8 shard_map.83
  152.5 8.6 %all_to_all.62.l_ref = bf16[4,64,768]{2,1,0:T(8,128)(2,1)S(1)} all-to-all(bf16[4,64,768]{2,1,0:T(8,128)(2,1)S(1)} %bitcast.59), channel_id=1, replica_groups=mesh['y'=4,'core'=2,'x'=4,'z'=8] {'y'}, dimensions={0} | all-to-all | bytes 786432 | tf_op jit(solution)/shard_map/all_to_all | solution.py:205
  161.1 0.2 shard_map.84
  161.3 10.3 %all_to_all.63 = bf16[4,64,768]{2,1,0:T(8,128)(2,1)S(1)} all-to-all(bf16[4,64,768]{2,1,0:T(8,128)(2,1)S(1)} %shard_map.84), channel_id=1, replica_groups=mesh['y'=4,'core'=2,'x'=4,'z'=8] {'y'}, dimensions={0} | all-to-all | bytes 786432 | tf_op jit(solution)/shard_map/all_to_all | solution.py:205
  171.6 1.7 shard_map.85
  173.3 6.3 %all-to-all-start.10 = ((bf16[32,8,1536]{2,1,0:T(8,128)(2,1)}), bf16[32,8,1536]{2,1,0:T(8,128)(2,1)S(1)}, u32[]{:S(2)}, u32[]{:S(2)}) async-start(bf16[32,8,1536]{2,1,0:T(8,128)(2,1)} %bitcast.61), calls=%async_computation.10 | async-start | bytes 1572864 | tf_op jit(solution)/shard_map/all_to_all | solution.py:205
  179.9 1.8 convolution_convert_fusion.1
  181.8 10.7 %collective-permute-start.7 = (bf16[384,768]{1,0:T(8,128)(2,1)S(1)}, bf16[384,768]{1,0:T(8,128)(2,1)S(1)}, u32[]{:S(2)}, u32[]{:S(2)}) collective-permute-start(bf16[384,768]{1,0:T(8,128)(2,1)S(1)} %get-tuple-element.57), channel_id=1, source_target_pairs={{0,32},{32,0},{1,33},{33,1},{2,34},{34,2},{3,35},{35,3},{4,36},{36... | collective-permute-start | bytes 1769480 | tf_op jit(solution)/shard_map/ppermute | solution.py:196
  192.6 0.8 convolution_convert_fusion
  193.5 0.9 collective-permute-start.9
  194.6 0.5 collective-permute-done.8
  195.0 2.2 %convert_add_fusion.1 = f32[768,768]{1,0:T(8,128)} fusion(bf16[384,768]{1,0:T(8,128)(2,1)S(1)} %collective-permute-done.8, bf16[384,768]{1,0:T(8,128)(2,1)S(1)} %collective-permute-done.7, bf16[256,768]{1,0:T(8,128)(2,1)S(1)} %get-tuple-element.63, bf16[256,768]{1,0:T(8,128)(2,1)S(1)} %copy-done.20, bf16[256,768]{1,0:T(8,128)(2,1)S(1)} %get-tuple-element.67, ...), kind=kOutput, calls=%fused_computation.1 | convolution fusion | flops 610074624 | bytes 5111808 | tf_op jit(solution)/shard_map/dot_general | solution.py:39
  197.3 2.2 %convert_add_fusion = f32[768,768]{1,0:T(8,128)} fusion(bf16[384,768]{1,0:T(8,128)(2,1)S(1)} %collective-permute-done.10, bf16[384,768]{1,0:T(8,128)(2,1)S(1)} %collective-permute-done.9, bf16[256,768]{1,0:T(8,128)(2,1)S(1)} %copy-done.22, bf16[256,768]{1,0:T(8,128)(2,1)S(1)} %get-tuple-element.59, bf16[256,768]{1,0:T(8,128)(2,1)S(1)} %get-tuple-element.68, ...), kind=kOutput, calls=%fused_computation | convolution fusion | flops 610074624 | bytes 5111808 | tf_op jit(solution)/shard_map/dot_general | solution.py:39
  199.6 6.6 %collective-permute-start.11 = (f32[8,768]{1,0:T(8,128)S(1)}, f32[8,768]{1,0:T(8,128)S(1)}, u32[]{:S(2)}, u32[]{:S(2)}) collective-permute-start(f32[8,768]{1,0:T(8,128)S(1)} %get-tuple-element.46), channel_id=1, source_target_pairs={{0,32},{32,0},{1,33},{33,1},{2,34},{34,2},{3,35},{35,3},{4,36},{36... | collective-permute-start | bytes 73736 | tf_op jit(solution)/shard_map/ppermute | solution.py:196
  206.3 0.8 collective-permute-done.11
  207.1 0.6 maximum_select_fusion
  (72 shorter events, 1.5 us)
Async XLA Ops:
  0.6 1.7 copy-start
  0.6 5.6 %copy-start.1 = (bf16[768,768]{1,0:T(8,128)(2,1)S(1)}, bf16[768,768]{1,0:T(8,128)(2,1)}, u32[]{:S(2)}) copy-start(bf16[768,768]{1,0:T(8,128)(2,1)} %a_ref.8) | copy-start | bytes 3538948
  2.3 5.8 %copy-start.19 = (bf16[256,768]{1,0:T(8,128)(2,1)}, bf16[256,768]{1,0:T(8,128)(2,1)S(1)}, u32[]{:S(2)}) copy-start(bf16[256,768]{1,0:T(8,128)(2,1)S(1)} %get-tuple-element.54) | copy-start | bytes 1179652
  2.3 5.8 %copy-start.23 = (bf16[256,768]{1,0:T(8,128)(2,1)}, bf16[256,768]{1,0:T(8,128)(2,1)S(1)}, u32[]{:S(2)}) copy-start(bf16[256,768]{1,0:T(8,128)(2,1)S(1)} %get-tuple-element.53) | copy-start | bytes 1179652
  2.9 4.7 %collective-permute-start = (bf16[256,768]{1,0:T(8,128)(2,1)S(1)}, bf16[256,768]{1,0:T(8,128)(2,1)S(1)}, u32[]{:S(2)}, u32[]{:S(2)}) collective-permute-start(bf16[256,768]{1,0:T(8,128)(2,1)S(1)} %convolution_convert_fusion.2), channel_id=1, source_target_pairs={{0,32},{32,0},{1,33},{33,1},{2,34},{34,2},{3,35},{35,3},{4,36},{36... | collective-permute-start | bytes 1179656 | tf_op jit(solution)/shard_map/ppermute | solution.py:196
  6.2 20.9 %collective-permute-start.1 = (bf16[768,768]{1,0:T(8,128)(2,1)S(1)}, bf16[768,768]{1,0:T(8,128)(2,1)S(1)}, u32[]{:S(2)}, u32[]{:S(2)}) collective-permute-start(bf16[768,768]{1,0:T(8,128)(2,1)S(1)} %copy-done), channel_id=1, source_target_pairs={{0,32},{32,0},{1,33},{33,1},{2,34},{34,2},{3,35},{35,3},{4,36},{36... | collective-permute-start | bytes 3538952 | tf_op jit(solution)/shard_map/ppermute | solution.py:196
  6.3 20.8 %collective-permute-start.2 = (bf16[768,768]{1,0:T(8,128)(2,1)S(1)}, bf16[768,768]{1,0:T(8,128)(2,1)S(1)}, u32[]{:S(2)}, u32[]{:S(2)}) collective-permute-start(bf16[768,768]{1,0:T(8,128)(2,1)S(1)} %copy-done.1), channel_id=1, source_target_pairs={{0,32},{32,0},{1,33},{33,1},{2,34},{34,2},{3,35},{35,3},{4,36},{36... | collective-permute-start | bytes 3538952 | tf_op jit(solution)/shard_map/ppermute | solution.py:196
  18.2 10.6 %copy-start.15 = (bf16[64,768]{1,0:T(8,128)(2,1)}, bf16[64,768]{1,0:T(8,128)(2,1)S(1)}, u32[]{:S(2)}) copy-start(bf16[64,768]{1,0:T(8,128)(2,1)S(1)} %get-tuple-element.35.p_ref) | copy-start | bytes 294916
  27.1 1.7 copy-start.10
  27.1 1.7 copy-start.2
  28.8 26.9 %all-to-all-start.2 = ((bf16[32,8,1536]{2,1,0:T(8,128)(2,1)}), bf16[32,8,1536]{2,1,0:T(8,128)(2,1)}, u32[]{:S(2)}, u32[]{:S(2)}) async-start(bf16[32,8,1536]{2,1,0:T(8,128)(2,1)} %bitcast.60), calls=%async_computation.2 | async-start | bytes 1572864 | tf_op jit(solution)/shard_map/all_to_all | solution.py:205
  39.2 10.4 %collective-permute-start.6 = (bf16[256,768]{1,0:T(8,128)(2,1)}, bf16[256,768]{1,0:T(8,128)(2,1)}, u32[]{:S(2)}, u32[]{:S(2)}) collective-permute-start(bf16[256,768]{1,0:T(8,128)(2,1)} %copy-done.23), channel_id=1, source_target_pairs={{0,32},{32,0},{1,33},{33,1},{2,34},{34,2},{3,35},{35,3},{4,36},{36... | collective-permute-start | bytes 1179656 | tf_op jit(solution)/shard_map/ppermute | solution.py:196
  43.4 3.6 %collective-permute-start.4 = (f32[8,768]{1,0:T(8,128)S(1)}, f32[8,768]{1,0:T(8,128)S(1)}, u32[]{:S(2)}, u32[]{:S(2)}) collective-permute-start(f32[8,768]{1,0:T(8,128)S(1)} %get-tuple-element.50), channel_id=1, source_target_pairs={{0,32},{32,0},{1,33},{33,1},{2,34},{34,2},{3,35},{35,3},{4,36},{36... | collective-permute-start | bytes 73736 | tf_op jit(solution)/shard_map/ppermute | solution.py:196
  44.4 3.3 %collective-permute-start.5 = (f32[8,768]{1,0:T(8,128)S(1)}, f32[8,768]{1,0:T(8,128)S(1)}, u32[]{:S(2)}, u32[]{:S(2)}) collective-permute-start(f32[8,768]{1,0:T(8,128)S(1)} %get-tuple-element.66), channel_id=1, source_target_pairs={{0,32},{32,0},{1,33},{33,1},{2,34},{34,2},{3,35},{35,3},{4,36},{36... | collective-permute-start | bytes 73736 | tf_op jit(solution)/shard_map/ppermute | solution.py:196
  46.4 3.2 %copy-start.21 = (bf16[256,768]{1,0:T(8,128)(2,1)}, bf16[256,768]{1,0:T(8,128)(2,1)S(1)}, u32[]{:S(2)}) copy-start(bf16[256,768]{1,0:T(8,128)(2,1)S(1)} %get-tuple-element.52) | copy-start | bytes 1179652
  46.4 1.9 collective-permute-start.3
  48.3 1.3 copy-start.24
  55.7 0.8 copy-start.14
  56.5 26.3 %copy-start.3 = (bf16[768,768]{1,0:T(8,128)(2,1)S(1)}, bf16[768,768]{1,0:T(8,128)(2,1)}, u32[]{:S(2)}) copy-start(bf16[768,768]{1,0:T(8,128)(2,1)} %copy-done.2) | copy-start | bytes 3538948
  56.5 26.3 %copy-start.12 = (bf16[256,768]{1,0:T(8,128)(2,1)S(1)}, bf16[256,768]{1,0:T(8,128)(2,1)}, u32[]{:S(2)}) copy-start(bf16[256,768]{1,0:T(8,128)(2,1)} %fusion.refs_0_) | copy-start | bytes 1179652
  82.8 0.9 copy-start.6
  107.1 0.9 copy-start.8
  108.0 21.5 %copy-start.13 = (f32[8,1536]{1,0:T(8,128)S(1)}, f32[8,1536]{1,0:T(8,128)}, u32[]{:S(2)}) copy-start(f32[8,1536]{1,0:T(8,128)} %pad_maximum_fusion.7.a_ref) | copy-start | bytes 147460
  129.7 21.9 %copy-start.17 = (f32[8,1536]{1,0:T(8,128)}, f32[8,1536]{1,0:T(8,128)S(1)}, u32[]{:S(2)}) copy-start(f32[8,1536]{1,0:T(8,128)S(1)} %get-tuple-element.44.a_ref) | copy-start | bytes 147460
  151.6 0.9 copy-start.4
  151.6 9.5 %copy-start.16 = (bf16[64,768]{1,0:T(8,128)(2,1)S(1)}, bf16[64,768]{1,0:T(8,128)(2,1)}, u32[]{:S(2)}) copy-start(bf16[64,768]{1,0:T(8,128)(2,1)} %copy-done.15) | copy-start | bytes 294916
  173.3 6.4 %copy-start.7 = (bf16[32,8,1536]{2,1,0:T(8,128)(2,1)S(1)}, bf16[32,8,1536]{2,1,0:T(8,128)(2,1)}, u32[]{:S(2)}) copy-start(bf16[32,8,1536]{2,1,0:T(8,128)(2,1)} %copy-done.6) | copy-start | bytes 2359300
  173.3 6.4 %copy-start.5 = (bf16[32,8,1536]{2,1,0:T(8,128)(2,1)S(1)}, bf16[32,8,1536]{2,1,0:T(8,128)(2,1)}, u32[]{:S(2)}) copy-start(bf16[32,8,1536]{2,1,0:T(8,128)(2,1)} %copy-done.4) | copy-start | bytes 2359300
  173.3 6.4 %copy-start.9 = (bf16[4,64,1536]{2,1,0:T(8,128)(2,1)S(1)}, bf16[4,64,1536]{2,1,0:T(8,128)(2,1)}, u32[]{:S(2)}) copy-start(bf16[4,64,1536]{2,1,0:T(8,128)(2,1)} %copy-done.8) | copy-start | bytes 2359300
  173.3 26.2 %all-to-all-start.10 = ((bf16[32,8,1536]{2,1,0:T(8,128)(2,1)}), bf16[32,8,1536]{2,1,0:T(8,128)(2,1)S(1)}, u32[]{:S(2)}, u32[]{:S(2)}) async-start(bf16[32,8,1536]{2,1,0:T(8,128)(2,1)} %bitcast.61), calls=%async_computation.10 | async-start | bytes 1572864 | tf_op jit(solution)/shard_map/all_to_all | solution.py:205
  181.7 11.0 %copy-start.11 = (bf16[4,64,768]{2,1,0:T(8,128)(2,1)S(1)}, bf16[4,64,768]{2,1,0:T(8,128)(2,1)}, u32[]{:S(2)}) copy-start(bf16[4,64,768]{2,1,0:T(8,128)(2,1)} %copy-done.10) | copy-start | bytes 1179652
  181.7 10.9 %copy-start.25 = (bf16[256,768]{1,0:T(8,128)(2,1)S(1)}, bf16[256,768]{1,0:T(8,128)(2,1)}, u32[]{:S(2)}) copy-start(bf16[256,768]{1,0:T(8,128)(2,1)} %copy-done.24) | copy-start | bytes 1179652
  181.8 12.8 %collective-permute-start.7 = (bf16[384,768]{1,0:T(8,128)(2,1)S(1)}, bf16[384,768]{1,0:T(8,128)(2,1)S(1)}, u32[]{:S(2)}, u32[]{:S(2)}) collective-permute-start(bf16[384,768]{1,0:T(8,128)(2,1)S(1)} %get-tuple-element.57), channel_id=1, source_target_pairs={{0,32},{32,0},{1,33},{33,1},{2,34},{34,2},{3,35},{35,3},{4,36},{36... | collective-permute-start | bytes 1769480 | tf_op jit(solution)/shard_map/ppermute | solution.py:196
  192.5 2.5 %collective-permute-start.8 = (bf16[384,768]{1,0:T(8,128)(2,1)S(1)}, bf16[384,768]{1,0:T(8,128)(2,1)S(1)}, u32[]{:S(2)}, u32[]{:S(2)}) collective-permute-start(bf16[384,768]{1,0:T(8,128)(2,1)S(1)} %get-tuple-element.58), channel_id=1, source_target_pairs={{0,32},{32,0},{1,33},{33,1},{2,34},{34,2},{3,35},{35,3},{4,36},{36... | collective-permute-start | bytes 1769480 | tf_op jit(solution)/shard_map/ppermute | solution.py:196
  193.4 1.6 copy-start.20
  193.5 3.7 %collective-permute-start.9 = (bf16[384,768]{1,0:T(8,128)(2,1)S(1)}, bf16[384,768]{1,0:T(8,128)(2,1)S(1)}, u32[]{:S(2)}, u32[]{:S(2)}) collective-permute-start(bf16[384,768]{1,0:T(8,128)(2,1)S(1)} %get-tuple-element.55), channel_id=1, source_target_pairs={{0,32},{32,0},{1,33},{33,1},{2,34},{34,2},{3,35},{35,3},{4,36},{36... | collective-permute-start | bytes 1769480 | tf_op jit(solution)/shard_map/ppermute | solution.py:196
  194.4 2.8 %collective-permute-start.10 = (bf16[384,768]{1,0:T(8,128)(2,1)S(1)}, bf16[384,768]{1,0:T(8,128)(2,1)S(1)}, u32[]{:S(2)}, u32[]{:S(2)}) collective-permute-start(bf16[384,768]{1,0:T(8,128)(2,1)S(1)} %get-tuple-element.56), channel_id=1, source_target_pairs={{0,32},{32,0},{1,33},{33,1},{2,34},{34,2},{3,35},{35,3},{4,36},{36... | collective-permute-start | bytes 1769480 | tf_op jit(solution)/shard_map/ppermute | solution.py:196
  195.0 2.3 %copy-start.22 = (bf16[256,768]{1,0:T(8,128)(2,1)S(1)}, bf16[256,768]{1,0:T(8,128)(2,1)}, u32[]{:S(2)}) copy-start(bf16[256,768]{1,0:T(8,128)(2,1)} %copy-done.21) | copy-start | bytes 1179652
  197.3 2.3 %copy-start.18 = (f32[8,1536]{1,0:T(8,128)S(1)}, f32[8,1536]{1,0:T(8,128)}, u32[]{:S(2)}) copy-start(f32[8,1536]{1,0:T(8,128)} %copy-done.17) | copy-start | bytes 147460
  199.6 7.5 %collective-permute-start.11 = (f32[8,768]{1,0:T(8,128)S(1)}, f32[8,768]{1,0:T(8,128)S(1)}, u32[]{:S(2)}, u32[]{:S(2)}) collective-permute-start(f32[8,768]{1,0:T(8,128)S(1)} %get-tuple-element.46), channel_id=1, source_target_pairs={{0,32},{32,0},{1,33},{33,1},{2,34},{34,2},{3,35},{35,3},{4,36},{36... | collective-permute-start | bytes 73736 | tf_op jit(solution)/shard_map/ppermute | solution.py:196

commit v8 on v7

--- a/solution.py
+++ b/solution.py
@@ -133,17 +133,16 @@
     return call(body, [((eight, wide), f32), ((count, eight, wide), bf16)], landed, added)
 
 
-def sum_last(landed, added):
+def sum_half(landed, added, first):
     count, eight, wide = landed.shape
     half = wide // 2
 
-    def body(l_ref, a_ref, m_ref, t_ref):
+    def body(l_ref, a_ref, o_ref):
         for cols in strips(half, 256):
-            m_ref[:, cols] = a_ref[:, cols] + add_up(l_ref, cols)
-            far = slice(cols.start + half, cols.stop + half)
-            t_ref[:, cols] = a_ref[:, far] + add_up(l_ref, far)
-
-    return call(body, [((eight, half), f32)] * 2, landed, added)
+            taken = slice(cols.start + first, cols.stop + first)
+            o_ref[:, cols] = a_ref[:, taken] + add_up(l_ref, taken)
+
+    return call(body, [((eight, half), f32)], landed, added)
 
 
 def activate(landed):
@@ -285,8 +284,8 @@
     grad_down = t_dot(act_both, jnp.concatenate([error_one[:, :wide], two_own], axis=0)) + swap_parts(down_far)
     landed, grad_up, grad_down = lax.optimization_barrier((landed, grad_up, grad_down))
 
-    mine, theirs = sum_last(landed, grad_one)
-    theirs = swap(theirs)
+    theirs = swap(sum_half(landed, grad_one, wide))
+    mine = sum_half(landed, grad_one, 0)
     grad_start = jnp.where(
         core == 0, jnp.concatenate([mine, theirs], axis=0), jnp.concatenate([theirs, mine], axis=0)
     )

time: 209 us -> 209 us (level)
    pallas_call x9 -> x10, Pallas kernels: 5.23 us -> 5.25 us  [call(): pl.pallas_call(body, out_shape=[jax.ShapeDtypeStruct(s, t) for s, t in ou...]
where the time goes in v8:
time: 209 us; the launch traced here: 208 us
  blocking collectives  129 us (62%)
  starting transfers between devices  43.2 us (21%)
  matrix products  9.81 us (5%)
  Pallas kernels  8.65 us (4%)
  waiting for transfers between devices  8.2 us (4%)
  local copies, waits for them, and re-layouts  5.48 us (3%)
  other arithmetic  2.7 us (1%)
    all_to_all x9, blocking collectives, exchange(): return lax.all_to_all(parts, axes, 0, 0, tiled=True)  129 us
    ppermute x12, starting transfers between devices, swap(): return lax.ppermute(block, 'core', [(0, 1), (1, 0)])  26.5 us
    all_to_all x2, starting transfers between devices, exchange(): return lax.all_to_all(parts, axes, 0, 0, tiled=True)  16.7 us
    dot_general x4, matrix products, t_dot(): lax.dot_general(a, b, (((0,), (0,)), ((), ())), preferred_element_type=f32)  7.06 us
    all_to_all x2, waiting for transfers between devices, exchange(): return lax.all_to_all(parts, axes, 0, 0, tiled=True)  6.11 us
    pallas_call x10, Pallas kernels, call(): pl.pallas_call(body, out_shape=[jax.ShapeDtypeStruct(s, t) for s, t in ou...  5.25 us
  transfers between devices with their start and end apart: 14, of which 4 were waited for; matrix products, arithmetic and copies ran while one was open for 7% of the time, Pallas kernels for 0%

profile of v8, /device:TPU:1, one launch (start us, length us, event | category | flops | bytes accessed | tf_op | source)
XLA Modules:
  0.0 207.7 jit_solution(13691778348903520455)
XLA Ops:
  0.7 1.6 fusion.20
  2.4 0.5 convolution_convert_fusion.2
  2.9 3.3 %collective-permute-start = (bf16[256,768]{1,0:T(8,128)(2,1)S(1)}, bf16[256,768]{1,0:T(8,128)(2,1)S(1)}, u32[]{:S(2)}, u32[]{:S(2)}) collective-permute-start(bf16[256,768]{1,0:T(8,128)(2,1)S(1)} %convolution_convert_fusion.2), channel_id=1, source_target_pairs={{0,32},{32,0},{1,33},{33,1},{2,34},{34,2},{3,35},{35,3},{4,36},{36... | collective-permute-start | bytes 1179656 | tf_op jit(solution)/shard_map/ppermute | solution.py:195
  6.3 0.4 collective-permute-start.2
  6.7 0.8 collective-permute-done
  7.5 0.5 add_convert_fusion
  8.0 10.1 %all_to_all.55.l_ref = bf16[4,64,768]{2,1,0:T(8,128)(2,1)S(1)} all-to-all(bf16[4,64,768]{2,1,0:T(8,128)(2,1)S(1)} %bitcast.62), channel_id=1, replica_groups=mesh['y'=4,'core'=2,'x'=4,'z'=8] {'y'}, dimensions={0} | all-to-all | bytes 786432 | tf_op jit(solution)/shard_map/all_to_all | solution.py:204
  18.2 8.8 %all_to_all.56 = bf16[4,64,768]{2,1,0:T(8,128)(2,1)S(1)} all-to-all(bf16[4,64,768]{2,1,0:T(8,128)(2,1)S(1)} %get-tuple-element.24), channel_id=1, replica_groups=mesh['y'=4,'core'=2,'x'=4,'z'=8] {'y'}, dimensions={0} | all-to-all | bytes 786432 | tf_op jit(solution)/shard_map/all_to_all | solution.py:204
  27.1 1.7 shard_map.77
  28.8 10.3 %all-to-all-start.2 = ((bf16[32,8,1536]{2,1,0:T(8,128)(2,1)}), bf16[32,8,1536]{2,1,0:T(8,128)(2,1)}, u32[]{:S(2)}, u32[]{:S(2)}) async-start(bf16[32,8,1536]{2,1,0:T(8,128)(2,1)} %bitcast.60), calls=%async_computation.2 | async-start | bytes 1572864 | tf_op jit(solution)/shard_map/all_to_all | solution.py:204
  39.2 3.3 %collective-permute-start.6 = (bf16[256,768]{1,0:T(8,128)(2,1)}, bf16[256,768]{1,0:T(8,128)(2,1)}, u32[]{:S(2)}, u32[]{:S(2)}) collective-permute-start(bf16[256,768]{1,0:T(8,128)(2,1)} %copy-done.23), channel_id=1, source_target_pairs={{0,32},{32,0},{1,33},{33,1},{2,34},{34,2},{3,35},{35,3},{4,36},{36... | collective-permute-start | bytes 1179656 | tf_op jit(solution)/shard_map/ppermute | solution.py:195
  42.5 0.9 constant_dynamic-slice_fusion.3
  43.4 0.1 collective-permute-start.4
  43.5 0.8 dynamic-slice_add_fusion
  44.4 0.5 collective-permute-start.5
  44.9 1.4 fusion.22
  46.4 0.1 collective-permute-start.3
  46.5 0.5 fusion.32
  47.0 0.6 pad_maximum_fusion.6.a_ref
  47.7 0.6 pad_maximum_fusion.7.a_ref
  48.3 1.3 fusion.refs_0_
  49.6 6.1 %all-to-all-done.2.l_ref = bf16[32,8,1536]{2,1,0:T(8,128)(2,1)} async-done(((bf16[32,8,1536]{2,1,0:T(8,128)(2,1)}), bf16[32,8,1536]{2,1,0:T(8,128)(2,1)}, u32[]{:S(2)}, u32[]{:S(2)}) %all-to-all-start.2) | async-done | bytes 786464 | tf_op jit(solution)/shard_map/all_to_all | solution.py:204
  55.7 0.8 copy-done.14
  56.5 2.0 shard_map.78
  58.5 24.3 %all_to_all.57 = bf16[32,8,1536]{2,1,0:T(8,128)(2,1)S(1)} all-to-all(bf16[32,8,1536]{2,1,0:T(8,128)(2,1)S(1)} %get-tuple-element.28), channel_id=1, replica_groups=mesh['y'=4,'core'=2,'x'=4,'z'=8] {'x','z'}, dimensions={0} | all-to-all | bytes 1572864 | tf_op jit(solution)/shard_map/all_to_all | solution.py:204
  82.8 0.8 shard_map.79
  83.7 10.7 %all_to_all.58.l_ref = bf16[4,64,1536]{2,1,0:T(8,128)(2,1)S(1)} all-to-all(bf16[4,64,1536]{2,1,0:T(8,128)(2,1)S(1)} %bitcast.51), channel_id=1, replica_groups=mesh['y'=4,'core'=2,'x'=4,'z'=8] {'y'}, dimensions={0} | all-to-all | bytes 1572864 | tf_op jit(solution)/shard_map/all_to_all | solution.py:204
  94.4 0.3 shard_map.80
  94.7 12.4 %all_to_all.59 = bf16[4,64,1536]{2,1,0:T(8,128)(2,1)S(1)} all-to-all(bf16[4,64,1536]{2,1,0:T(8,128)(2,1)S(1)} %shard_map.80), channel_id=1, replica_groups=mesh['y'=4,'core'=2,'x'=4,'z'=8] {'y'}, dimensions={0} | all-to-all | bytes 1572864 | tf_op jit(solution)/shard_map/all_to_all | solution.py:204
  107.1 0.8 shard_map.81
  108.0 21.5 %all_to_all.60.l_ref = bf16[32,8,1536]{2,1,0:T(8,128)(2,1)S(1)} all-to-all(bf16[32,8,1536]{2,1,0:T(8,128)(2,1)S(1)} %bitcast.52), channel_id=1, replica_groups=mesh['y'=4,'core'=2,'x'=4,'z'=8] {'x','z'}, dimensions={0} | all-to-all | bytes 1572864 | tf_op jit(solution)/shard_map/all_to_all | solution.py:204
  129.7 21.9 %all_to_all.61 = bf16[32,8,1536]{2,1,0:T(8,128)(2,1)S(1)} all-to-all(bf16[32,8,1536]{2,1,0:T(8,128)(2,1)S(1)} %get-tuple-element.32), channel_id=1, replica_groups=mesh['y'=4,'core'=2,'x'=4,'z'=8] {'x','z'}, dimensions={0} | all-to-all | bytes 1572864 | tf_op jit(solution)/shard_map/all_to_all | solution.py:204
  151.6 0.8 shard_map.83
  152.5 8.6 %all_to_all.62.l_ref = bf16[4,64,768]{2,1,0:T(8,128)(2,1)S(1)} all-to-all(bf16[4,64,768]{2,1,0:T(8,128)(2,1)S(1)} %bitcast.59), channel_id=1, replica_groups=mesh['y'=4,'core'=2,'x'=4,'z'=8] {'y'}, dimensions={0} | all-to-all | bytes 786432 | tf_op jit(solution)/shard_map/all_to_all | solution.py:204
  161.1 0.2 shard_map.84
  161.3 10.3 %all_to_all.63 = bf16[4,64,768]{2,1,0:T(8,128)(2,1)S(1)} all-to-all(bf16[4,64,768]{2,1,0:T(8,128)(2,1)S(1)} %shard_map.84), channel_id=1, replica_groups=mesh['y'=4,'core'=2,'x'=4,'z'=8] {'y'}, dimensions={0} | all-to-all | bytes 786432 | tf_op jit(solution)/shard_map/all_to_all | solution.py:204
  171.6 1.7 shard_map.85
  173.3 6.3 %all-to-all-start.10 = ((bf16[32,8,1536]{2,1,0:T(8,128)(2,1)}), bf16[32,8,1536]{2,1,0:T(8,128)(2,1)S(1)}, u32[]{:S(2)}, u32[]{:S(2)}) async-start(bf16[32,8,1536]{2,1,0:T(8,128)(2,1)} %bitcast.61), calls=%async_computation.10 | async-start | bytes 1572864 | tf_op jit(solution)/shard_map/all_to_all | solution.py:204
  179.9 1.8 convolution_convert_fusion.1
  181.8 10.7 %collective-permute-start.7 = (bf16[384,768]{1,0:T(8,128)(2,1)S(1)}, bf16[384,768]{1,0:T(8,128)(2,1)S(1)}, u32[]{:S(2)}, u32[]{:S(2)}) collective-permute-start(bf16[384,768]{1,0:T(8,128)(2,1)S(1)} %get-tuple-element.53), channel_id=1, source_target_pairs={{0,32},{32,0},{1,33},{33,1},{2,34},{34,2},{3,35},{35,3},{4,36},{36... | collective-permute-start | bytes 1769480 | tf_op jit(solution)/shard_map/ppermute | solution.py:195
  192.6 0.8 convolution_convert_fusion
  193.5 0.9 collective-permute-start.9
  194.6 0.5 collective-permute-done.8
  195.0 2.2 %convert_add_fusion.1 = f32[768,768]{1,0:T(8,128)} fusion(bf16[384,768]{1,0:T(8,128)(2,1)S(1)} %collective-permute-done.8, bf16[384,768]{1,0:T(8,128)(2,1)S(1)} %collective-permute-done.7, bf16[256,768]{1,0:T(8,128)(2,1)S(1)} %get-tuple-element.59, bf16[256,768]{1,0:T(8,128)(2,1)S(1)} %copy-done.20, bf16[256,768]{1,0:T(8,128)(2,1)S(1)} %get-tuple-element.63, ...), kind=kOutput, calls=%fused_computation.1 | convolution fusion | flops 610074624 | bytes 5111808 | tf_op jit(solution)/shard_map/dot_general | solution.py:39
  197.3 2.2 %convert_add_fusion = f32[768,768]{1,0:T(8,128)} fusion(bf16[384,768]{1,0:T(8,128)(2,1)S(1)} %collective-permute-done.10, bf16[384,768]{1,0:T(8,128)(2,1)S(1)} %collective-permute-done.9, bf16[256,768]{1,0:T(8,128)(2,1)S(1)} %copy-done.22, bf16[256,768]{1,0:T(8,128)(2,1)S(1)} %get-tuple-element.55, bf16[256,768]{1,0:T(8,128)(2,1)S(1)} %get-tuple-element.64, ...), kind=kOutput, calls=%fused_computation | convolution fusion | flops 610074624 | bytes 5111808 | tf_op jit(solution)/shard_map/dot_general | solution.py:39
  199.6 6.7 %collective-permute-start.11 = (f32[8,768]{1,0:T(8,128)S(1)}, f32[8,768]{1,0:T(8,128)S(1)}, u32[]{:S(2)}, u32[]{:S(2)}) collective-permute-start(f32[8,768]{1,0:T(8,128)S(1)} %shard_map.87), channel_id=1, source_target_pairs={{0,32},{32,0},{1,33},{33,1},{2,34},{34,2},{3,35},{35,3},{4,36},{36... | collective-permute-start | bytes 73736 | tf_op jit(solution)/shard_map/ppermute | solution.py:195
  206.3 0.8 collective-permute-done.11
  207.1 0.6 maximum_select_fusion
  (73 shorter events, 1.5 us)
Async XLA Ops:
  0.6 1.7 copy-start
  0.6 5.6 %copy-start.1 = (bf16[768,768]{1,0:T(8,128)(2,1)S(1)}, bf16[768,768]{1,0:T(8,128)(2,1)}, u32[]{:S(2)}) copy-start(bf16[768,768]{1,0:T(8,128)(2,1)} %a_ref.8) | copy-start | bytes 3538948
  2.3 5.8 %copy-start.19 = (bf16[256,768]{1,0:T(8,128)(2,1)}, bf16[256,768]{1,0:T(8,128)(2,1)S(1)}, u32[]{:S(2)}) copy-start(bf16[256,768]{1,0:T(8,128)(2,1)S(1)} %get-tuple-element.50) | copy-start | bytes 1179652
  2.3 5.8 %copy-start.23 = (bf16[256,768]{1,0:T(8,128)(2,1)}, bf16[256,768]{1,0:T(8,128)(2,1)S(1)}, u32[]{:S(2)}) copy-start(bf16[256,768]{1,0:T(8,128)(2,1)S(1)} %get-tuple-element.49) | copy-start | bytes 1179652
  2.9 4.7 %collective-permute-start = (bf16[256,768]{1,0:T(8,128)(2,1)S(1)}, bf16[256,768]{1,0:T(8,128)(2,1)S(1)}, u32[]{:S(2)}, u32[]{:S(2)}) collective-permute-start(bf16[256,768]{1,0:T(8,128)(2,1)S(1)} %convolution_convert_fusion.2), channel_id=1, source_target_pairs={{0,32},{32,0},{1,33},{33,1},{2,34},{34,2},{3,35},{35,3},{4,36},{36... | collective-permute-start | bytes 1179656 | tf_op jit(solution)/shard_map/ppermute | solution.py:195
  6.2 20.9 %collective-permute-start.1 = (bf16[768,768]{1,0:T(8,128)(2,1)S(1)}, bf16[768,768]{1,0:T(8,128)(2,1)S(1)}, u32[]{:S(2)}, u32[]{:S(2)}) collective-permute-start(bf16[768,768]{1,0:T(8,128)(2,1)S(1)} %copy-done), channel_id=1, source_target_pairs={{0,32},{32,0},{1,33},{33,1},{2,34},{34,2},{3,35},{35,3},{4,36},{36... | collective-permute-start | bytes 3538952 | tf_op jit(solution)/shard_map/ppermute | solution.py:195
  6.3 20.8 %collective-permute-start.2 = (bf16[768,768]{1,0:T(8,128)(2,1)S(1)}, bf16[768,768]{1,0:T(8,128)(2,1)S(1)}, u32[]{:S(2)}, u32[]{:S(2)}) collective-permute-start(bf16[768,768]{1,0:T(8,128)(2,1)S(1)} %copy-done.1), channel_id=1, source_target_pairs={{0,32},{32,0},{1,33},{33,1},{2,34},{34,2},{3,35},{35,3},{4,36},{36... | collective-permute-start | bytes 3538952 | tf_op jit(solution)/shard_map/ppermute | solution.py:195
  18.2 10.6 %copy-start.17 = (bf16[64,768]{1,0:T(8,128)(2,1)}, bf16[64,768]{1,0:T(8,128)(2,1)S(1)}, u32[]{:S(2)}) copy-start(bf16[64,768]{1,0:T(8,128)(2,1)S(1)} %get-tuple-element.33.p_ref) | copy-start | bytes 294916
  27.1 1.7 copy-start.10
  27.1 1.7 copy-start.2
  28.8 26.9 %all-to-all-start.2 = ((bf16[32,8,1536]{2,1,0:T(8,128)(2,1)}), bf16[32,8,1536]{2,1,0:T(8,128)(2,1)}, u32[]{:S(2)}, u32[]{:S(2)}) async-start(bf16[32,8,1536]{2,1,0:T(8,128)(2,1)} %bitcast.60), calls=%async_computation.2 | async-start | bytes 1572864 | tf_op jit(solution)/shard_map/all_to_all | solution.py:204
  39.2 10.4 %collective-permute-start.6 = (bf16[256,768]{1,0:T(8,128)(2,1)}, bf16[256,768]{1,0:T(8,128)(2,1)}, u32[]{:S(2)}, u32[]{:S(2)}) collective-permute-start(bf16[256,768]{1,0:T(8,128)(2,1)} %copy-done.23), channel_id=1, source_target_pairs={{0,32},{32,0},{1,33},{33,1},{2,34},{34,2},{3,35},{35,3},{4,36},{36... | collective-permute-start | bytes 1179656 | tf_op jit(solution)/shard_map/ppermute | solution.py:195
  43.4 3.6 %collective-permute-start.4 = (f32[8,768]{1,0:T(8,128)S(1)}, f32[8,768]{1,0:T(8,128)S(1)}, u32[]{:S(2)}, u32[]{:S(2)}) collective-permute-start(f32[8,768]{1,0:T(8,128)S(1)} %get-tuple-element.46), channel_id=1, source_target_pairs={{0,32},{32,0},{1,33},{33,1},{2,34},{34,2},{3,35},{35,3},{4,36},{36... | collective-permute-start | bytes 73736 | tf_op jit(solution)/shard_map/ppermute | solution.py:195
  44.4 3.3 %collective-permute-start.5 = (f32[8,768]{1,0:T(8,128)S(1)}, f32[8,768]{1,0:T(8,128)S(1)}, u32[]{:S(2)}, u32[]{:S(2)}) collective-permute-start(f32[8,768]{1,0:T(8,128)S(1)} %get-tuple-element.62), channel_id=1, source_target_pairs={{0,32},{32,0},{1,33},{33,1},{2,34},{34,2},{3,35},{35,3},{4,36},{36... | collective-permute-start | bytes 73736 | tf_op jit(solution)/shard_map/ppermute | solution.py:195
  46.4 3.2 %copy-start.21 = (bf16[256,768]{1,0:T(8,128)(2,1)}, bf16[256,768]{1,0:T(8,128)(2,1)S(1)}, u32[]{:S(2)}) copy-start(bf16[256,768]{1,0:T(8,128)(2,1)S(1)} %get-tuple-element.48) | copy-start | bytes 1179652
  46.4 1.9 collective-permute-start.3
  48.3 1.3 copy-start.24
  55.7 0.8 copy-start.14
  56.5 26.3 %copy-start.3 = (bf16[768,768]{1,0:T(8,128)(2,1)S(1)}, bf16[768,768]{1,0:T(8,128)(2,1)}, u32[]{:S(2)}) copy-start(bf16[768,768]{1,0:T(8,128)(2,1)} %copy-done.2) | copy-start | bytes 3538948
  56.5 26.3 %copy-start.12 = (bf16[256,768]{1,0:T(8,128)(2,1)S(1)}, bf16[256,768]{1,0:T(8,128)(2,1)}, u32[]{:S(2)}) copy-start(bf16[256,768]{1,0:T(8,128)(2,1)} %fusion.refs_0_) | copy-start | bytes 1179652
  82.8 0.9 copy-start.6
  107.1 0.9 copy-start.8
  108.0 21.5 %copy-start.13 = (f32[8,1536]{1,0:T(8,128)S(1)}, f32[8,1536]{1,0:T(8,128)}, u32[]{:S(2)}) copy-start(f32[8,1536]{1,0:T(8,128)} %pad_maximum_fusion.7.a_ref) | copy-start | bytes 147460
  129.7 21.9 %copy-start.15 = (f32[8,1536]{1,0:T(8,128)}, f32[8,1536]{1,0:T(8,128)S(1)}, u32[]{:S(2)}) copy-start(f32[8,1536]{1,0:T(8,128)S(1)} %get-tuple-element.42.a_ref) | copy-start | bytes 147460
  151.6 0.9 copy-start.4
  151.6 9.5 %copy-start.18 = (bf16[64,768]{1,0:T(8,128)(2,1)S(1)}, bf16[64,768]{1,0:T(8,128)(2,1)}, u32[]{:S(2)}) copy-start(bf16[64,768]{1,0:T(8,128)(2,1)} %copy-done.17) | copy-start | bytes 294916
  173.3 6.4 %copy-start.7 = (bf16[32,8,1536]{2,1,0:T(8,128)(2,1)S(1)}, bf16[32,8,1536]{2,1,0:T(8,128)(2,1)}, u32[]{:S(2)}) copy-start(bf16[32,8,1536]{2,1,0:T(8,128)(2,1)} %copy-done.6) | copy-start | bytes 2359300
  173.3 6.4 %copy-start.5 = (bf16[32,8,1536]{2,1,0:T(8,128)(2,1)S(1)}, bf16[32,8,1536]{2,1,0:T(8,128)(2,1)}, u32[]{:S(2)}) copy-start(bf16[32,8,1536]{2,1,0:T(8,128)(2,1)} %copy-done.4) | copy-start | bytes 2359300
  173.3 6.4 %copy-start.9 = (bf16[4,64,1536]{2,1,0:T(8,128)(2,1)S(1)}, bf16[4,64,1536]{2,1,0:T(8,128)(2,1)}, u32[]{:S(2)}) copy-start(bf16[4,64,1536]{2,1,0:T(8,128)(2,1)} %copy-done.8) | copy-start | bytes 2359300
  173.3 26.2 %all-to-all-start.10 = ((bf16[32,8,1536]{2,1,0:T(8,128)(2,1)}), bf16[32,8,1536]{2,1,0:T(8,128)(2,1)S(1)}, u32[]{:S(2)}, u32[]{:S(2)}) async-start(bf16[32,8,1536]{2,1,0:T(8,128)(2,1)} %bitcast.61), calls=%async_computation.10 | async-start | bytes 1572864 | tf_op jit(solution)/shard_map/all_to_all | solution.py:204
  181.7 10.9 %copy-start.11 = (bf16[4,64,768]{2,1,0:T(8,128)(2,1)S(1)}, bf16[4,64,768]{2,1,0:T(8,128)(2,1)}, u32[]{:S(2)}) copy-start(bf16[4,64,768]{2,1,0:T(8,128)(2,1)} %copy-done.10) | copy-start | bytes 1179652
  181.7 10.9 %copy-start.25 = (bf16[256,768]{1,0:T(8,128)(2,1)S(1)}, bf16[256,768]{1,0:T(8,128)(2,1)}, u32[]{:S(2)}) copy-start(bf16[256,768]{1,0:T(8,128)(2,1)} %copy-done.24) | copy-start | bytes 1179652
  181.8 12.8 %collective-permute-start.7 = (bf16[384,768]{1,0:T(8,128)(2,1)S(1)}, bf16[384,768]{1,0:T(8,128)(2,1)S(1)}, u32[]{:S(2)}, u32[]{:S(2)}) collective-permute-start(bf16[384,768]{1,0:T(8,128)(2,1)S(1)} %get-tuple-element.53), channel_id=1, source_target_pairs={{0,32},{32,0},{1,33},{33,1},{2,34},{34,2},{3,35},{35,3},{4,36},{36... | collective-permute-start | bytes 1769480 | tf_op jit(solution)/shard_map/ppermute | solution.py:195
  192.5 2.5 %collective-permute-start.8 = (bf16[384,768]{1,0:T(8,128)(2,1)S(1)}, bf16[384,768]{1,0:T(8,128)(2,1)S(1)}, u32[]{:S(2)}, u32[]{:S(2)}) collective-permute-start(bf16[384,768]{1,0:T(8,128)(2,1)S(1)} %get-tuple-element.54), channel_id=1, source_target_pairs={{0,32},{32,0},{1,33},{33,1},{2,34},{34,2},{3,35},{35,3},{4,36},{36... | collective-permute-start | bytes 1769480 | tf_op jit(solution)/shard_map/ppermute | solution.py:195
  193.5 1.6 copy-start.20
  193.5 3.7 %collective-permute-start.9 = (bf16[384,768]{1,0:T(8,128)(2,1)S(1)}, bf16[384,768]{1,0:T(8,128)(2,1)S(1)}, u32[]{:S(2)}, u32[]{:S(2)}) collective-permute-start(bf16[384,768]{1,0:T(8,128)(2,1)S(1)} %get-tuple-element.51), channel_id=1, source_target_pairs={{0,32},{32,0},{1,33},{33,1},{2,34},{34,2},{3,35},{35,3},{4,36},{36... | collective-permute-start | bytes 1769480 | tf_op jit(solution)/shard_map/ppermute | solution.py:195
  194.5 2.8 %collective-permute-start.10 = (bf16[384,768]{1,0:T(8,128)(2,1)S(1)}, bf16[384,768]{1,0:T(8,128)(2,1)S(1)}, u32[]{:S(2)}, u32[]{:S(2)}) collective-permute-start(bf16[384,768]{1,0:T(8,128)(2,1)S(1)} %get-tuple-element.52), channel_id=1, source_target_pairs={{0,32},{32,0},{1,33},{33,1},{2,34},{34,2},{3,35},{35,3},{4,36},{36... | collective-permute-start | bytes 1769480 | tf_op jit(solution)/shard_map/ppermute | solution.py:195
  195.0 2.2 %copy-start.22 = (bf16[256,768]{1,0:T(8,128)(2,1)S(1)}, bf16[256,768]{1,0:T(8,128)(2,1)}, u32[]{:S(2)}) copy-start(bf16[256,768]{1,0:T(8,128)(2,1)} %copy-done.21) | copy-start | bytes 1179652
  197.3 2.2 %copy-start.16 = (f32[8,1536]{1,0:T(8,128)S(1)}, f32[8,1536]{1,0:T(8,128)}, u32[]{:S(2)}) copy-start(f32[8,1536]{1,0:T(8,128)} %copy-done.15) | copy-start | bytes 147460
  199.6 7.5 %collective-permute-start.11 = (f32[8,768]{1,0:T(8,128)S(1)}, f32[8,768]{1,0:T(8,128)S(1)}, u32[]{:S(2)}, u32[]{:S(2)}) collective-permute-start(f32[8,768]{1,0:T(8,128)S(1)} %shard_map.87), channel_id=1, source_target_pairs={{0,32},{32,0},{1,33},{33,1},{2,34},{34,2},{3,35},{35,3},{4,36},{36... | collective-permute-start | bytes 73736 | tf_op jit(solution)/shard_map/ppermute | solution.py:195

commit v9 on v8

--- a/solution.py
+++ b/solution.py
@@ -123,7 +123,7 @@
     count, eight, wide = landed.shape
 
     def body(l_ref, a_ref, s_ref, c_ref):
-        for cols in strips(wide, 256):
+        for cols in strips(wide, 128):
             total = a_ref[:, cols] + add_up(l_ref, cols)
             s_ref[:, cols] = total
             rounded = total.astype(bf16)

time: 209 us -> 209 us (level)
  no operation moved by 1% of the time
where the time goes in v9:
time: 209 us; the launch traced here: 208 us
  blocking collectives  129 us (62%)
  starting transfers between devices  43.2 us (21%)
  matrix products  9.81 us (5%)
  Pallas kernels  8.69 us (4%)
  waiting for transfers between devices  8.2 us (4%)
  local copies, waits for them, and re-layouts  5.48 us (3%)
  other arithmetic  2.7 us (1%)
    all_to_all x9, blocking collectives, exchange(): return lax.all_to_all(parts, axes, 0, 0, tiled=True)  129 us
    ppermute x12, starting transfers between devices, swap(): return lax.ppermute(block, 'core', [(0, 1), (1, 0)])  26.5 us
    all_to_all x2, starting transfers between devices, exchange(): return lax.all_to_all(parts, axes, 0, 0, tiled=True)  16.7 us
    dot_general x4, matrix products, t_dot(): lax.dot_general(a, b, (((0,), (0,)), ((), ())), preferred_element_type=f32)  7.06 us
    all_to_all x2, waiting for transfers between devices, exchange(): return lax.all_to_all(parts, axes, 0, 0, tiled=True)  6.11 us
    pallas_call x10, Pallas kernels, call(): pl.pallas_call(body, out_shape=[jax.ShapeDtypeStruct(s, t) for s, t in ou...  5.28 us
  transfers between devices with their start and end apart: 14, of which 4 were waited for; matrix products, arithmetic and copies ran while one was open for 7% of the time, Pallas kernels for 0%

profile of v9, /device:TPU:1, one launch (start us, length us, event | category | flops | bytes accessed | tf_op | source)
XLA Modules:
  0.0 207.8 jit_solution(1941424689909228034)
XLA Ops:
  0.7 1.6 fusion.20
  2.4 0.5 convolution_convert_fusion.2
  2.9 3.3 %collective-permute-start = (bf16[256,768]{1,0:T(8,128)(2,1)S(1)}, bf16[256,768]{1,0:T(8,128)(2,1)S(1)}, u32[]{:S(2)}, u32[]{:S(2)}) collective-permute-start(bf16[256,768]{1,0:T(8,128)(2,1)S(1)} %convolution_convert_fusion.2), channel_id=1, source_target_pairs={{0,32},{32,0},{1,33},{33,1},{2,34},{34,2},{3,35},{35,3},{4,36},{36... | collective-permute-start | bytes 1179656 | tf_op jit(solution)/shard_map/ppermute | solution.py:195
  6.3 0.4 collective-permute-start.2
  6.7 0.8 collective-permute-done
  7.5 0.5 add_convert_fusion
  8.0 10.1 %all_to_all.55.l_ref = bf16[4,64,768]{2,1,0:T(8,128)(2,1)S(1)} all-to-all(bf16[4,64,768]{2,1,0:T(8,128)(2,1)S(1)} %bitcast.62), channel_id=1, replica_groups=mesh['y'=4,'core'=2,'x'=4,'z'=8] {'y'}, dimensions={0} | all-to-all | bytes 786432 | tf_op jit(solution)/shard_map/all_to_all | solution.py:204
  18.2 8.8 %all_to_all.56 = bf16[4,64,768]{2,1,0:T(8,128)(2,1)S(1)} all-to-all(bf16[4,64,768]{2,1,0:T(8,128)(2,1)S(1)} %get-tuple-element.24), channel_id=1, replica_groups=mesh['y'=4,'core'=2,'x'=4,'z'=8] {'y'}, dimensions={0} | all-to-all | bytes 786432 | tf_op jit(solution)/shard_map/all_to_all | solution.py:204
  27.1 1.7 shard_map.77
  28.8 10.3 %all-to-all-start.2 = ((bf16[32,8,1536]{2,1,0:T(8,128)(2,1)}), bf16[32,8,1536]{2,1,0:T(8,128)(2,1)}, u32[]{:S(2)}, u32[]{:S(2)}) async-start(bf16[32,8,1536]{2,1,0:T(8,128)(2,1)} %bitcast.60), calls=%async_computation.2 | async-start | bytes 1572864 | tf_op jit(solution)/shard_map/all_to_all | solution.py:204
  39.2 3.3 %collective-permute-start.6 = (bf16[256,768]{1,0:T(8,128)(2,1)}, bf16[256,768]{1,0:T(8,128)(2,1)}, u32[]{:S(2)}, u32[]{:S(2)}) collective-permute-start(bf16[256,768]{1,0:T(8,128)(2,1)} %copy-done.23), channel_id=1, source_target_pairs={{0,32},{32,0},{1,33},{33,1},{2,34},{34,2},{3,35},{35,3},{4,36},{36... | collective-permute-start | bytes 1179656 | tf_op jit(solution)/shard_map/ppermute | solution.py:195
  42.5 0.9 constant_dynamic-slice_fusion.3
  43.5 0.8 dynamic-slice_add_fusion
  44.4 0.5 collective-permute-start.5
  44.9 1.4 fusion.22
  46.4 0.1 collective-permute-start.3
  46.5 0.5 fusion.32
  47.0 0.6 pad_maximum_fusion.6.a_ref
  47.7 0.6 pad_maximum_fusion.7.a_ref
  48.3 1.3 fusion.refs_0_
  49.6 6.1 %all-to-all-done.2.l_ref = bf16[32,8,1536]{2,1,0:T(8,128)(2,1)} async-done(((bf16[32,8,1536]{2,1,0:T(8,128)(2,1)}), bf16[32,8,1536]{2,1,0:T(8,128)(2,1)}, u32[]{:S(2)}, u32[]{:S(2)}) %all-to-all-start.2) | async-done | bytes 786464 | tf_op jit(solution)/shard_map/all_to_all | solution.py:204
  55.7 0.8 copy-done.14
  56.5 2.0 shard_map.78
  58.5 24.3 %all_to_all.57 = bf16[32,8,1536]{2,1,0:T(8,128)(2,1)S(1)} all-to-all(bf16[32,8,1536]{2,1,0:T(8,128)(2,1)S(1)} %get-tuple-element.28), channel_id=1, replica_groups=mesh['y'=4,'core'=2,'x'=4,'z'=8] {'x','z'}, dimensions={0} | all-to-all | bytes 1572864 | tf_op jit(solution)/shard_map/all_to_all | solution.py:204
  82.8 0.8 shard_map.79
  83.7 10.7 %all_to_all.58.l_ref = bf16[4,64,1536]{2,1,0:T(8,128)(2,1)S(1)} all-to-all(bf16[4,64,1536]{2,1,0:T(8,128)(2,1)S(1)} %bitcast.51), channel_id=1, replica_groups=mesh['y'=4,'core'=2,'x'=4,'z'=8] {'y'}, dimensions={0} | all-to-all | bytes 1572864 | tf_op jit(solution)/shard_map/all_to_all | solution.py:204
  94.5 0.3 shard_map.80
  94.7 12.4 %all_to_all.59 = bf16[4,64,1536]{2,1,0:T(8,128)(2,1)S(1)} all-to-all(bf16[4,64,1536]{2,1,0:T(8,128)(2,1)S(1)} %shard_map.80), channel_id=1, replica_groups=mesh['y'=4,'core'=2,'x'=4,'z'=8] {'y'}, dimensions={0} | all-to-all | bytes 1572864 | tf_op jit(solution)/shard_map/all_to_all | solution.py:204
  107.2 0.8 shard_map.81
  108.1 21.5 %all_to_all.60.l_ref = bf16[32,8,1536]{2,1,0:T(8,128)(2,1)S(1)} all-to-all(bf16[32,8,1536]{2,1,0:T(8,128)(2,1)S(1)} %bitcast.52), channel_id=1, replica_groups=mesh['y'=4,'core'=2,'x'=4,'z'=8] {'x','z'}, dimensions={0} | all-to-all | bytes 1572864 | tf_op jit(solution)/shard_map/all_to_all | solution.py:204
  129.6 0.1 shard_map.82
  129.8 21.9 %all_to_all.61 = bf16[32,8,1536]{2,1,0:T(8,128)(2,1)S(1)} all-to-all(bf16[32,8,1536]{2,1,0:T(8,128)(2,1)S(1)} %get-tuple-element.32), channel_id=1, replica_groups=mesh['y'=4,'core'=2,'x'=4,'z'=8] {'x','z'}, dimensions={0} | all-to-all | bytes 1572864 | tf_op jit(solution)/shard_map/all_to_all | solution.py:204
  151.6 0.8 shard_map.83
  152.5 8.6 %all_to_all.62.l_ref = bf16[4,64,768]{2,1,0:T(8,128)(2,1)S(1)} all-to-all(bf16[4,64,768]{2,1,0:T(8,128)(2,1)S(1)} %bitcast.59), channel_id=1, replica_groups=mesh['y'=4,'core'=2,'x'=4,'z'=8] {'y'}, dimensions={0} | all-to-all | bytes 786432 | tf_op jit(solution)/shard_map/all_to_all | solution.py:204
  161.1 0.2 shard_map.84
  161.3 10.3 %all_to_all.63 = bf16[4,64,768]{2,1,0:T(8,128)(2,1)S(1)} all-to-all(bf16[4,64,768]{2,1,0:T(8,128)(2,1)S(1)} %shard_map.84), channel_id=1, replica_groups=mesh['y'=4,'core'=2,'x'=4,'z'=8] {'y'}, dimensions={0} | all-to-all | bytes 786432 | tf_op jit(solution)/shard_map/all_to_all | solution.py:204
  171.6 1.7 shard_map.85
  173.4 6.3 %all-to-all-start.10 = ((bf16[32,8,1536]{2,1,0:T(8,128)(2,1)}), bf16[32,8,1536]{2,1,0:T(8,128)(2,1)S(1)}, u32[]{:S(2)}, u32[]{:S(2)}) async-start(bf16[32,8,1536]{2,1,0:T(8,128)(2,1)} %bitcast.61), calls=%async_computation.10 | async-start | bytes 1572864 | tf_op jit(solution)/shard_map/all_to_all | solution.py:204
  179.9 1.8 convolution_convert_fusion.1
  181.8 10.7 %collective-permute-start.7 = (bf16[384,768]{1,0:T(8,128)(2,1)S(1)}, bf16[384,768]{1,0:T(8,128)(2,1)S(1)}, u32[]{:S(2)}, u32[]{:S(2)}) collective-permute-start(bf16[384,768]{1,0:T(8,128)(2,1)S(1)} %get-tuple-element.53), channel_id=1, source_target_pairs={{0,32},{32,0},{1,33},{33,1},{2,34},{34,2},{3,35},{35,3},{4,36},{36... | collective-permute-start | bytes 1769480 | tf_op jit(solution)/shard_map/ppermute | solution.py:195
  192.7 0.8 convolution_convert_fusion
  193.6 0.9 collective-permute-start.9
  194.6 0.5 collective-permute-done.8
  195.1 2.2 %convert_add_fusion.1 = f32[768,768]{1,0:T(8,128)} fusion(bf16[384,768]{1,0:T(8,128)(2,1)S(1)} %collective-permute-done.8, bf16[384,768]{1,0:T(8,128)(2,1)S(1)} %collective-permute-done.7, bf16[256,768]{1,0:T(8,128)(2,1)S(1)} %get-tuple-element.59, bf16[256,768]{1,0:T(8,128)(2,1)S(1)} %copy-done.20, bf16[256,768]{1,0:T(8,128)(2,1)S(1)} %get-tuple-element.63, ...), kind=kOutput, calls=%fused_computation.1 | convolution fusion | flops 610074624 | bytes 5111808 | tf_op jit(solution)/shard_map/dot_general | solution.py:39
  197.3 2.2 %convert_add_fusion = f32[768,768]{1,0:T(8,128)} fusion(bf16[384,768]{1,0:T(8,128)(2,1)S(1)} %collective-permute-done.10, bf16[384,768]{1,0:T(8,128)(2,1)S(1)} %collective-permute-done.9, bf16[256,768]{1,0:T(8,128)(2,1)S(1)} %copy-done.22, bf16[256,768]{1,0:T(8,128)(2,1)S(1)} %get-tuple-element.55, bf16[256,768]{1,0:T(8,128)(2,1)S(1)} %get-tuple-element.64, ...), kind=kOutput, calls=%fused_computation | convolution fusion | flops 610074624 | bytes 5111808 | tf_op jit(solution)/shard_map/dot_general | solution.py:39
  199.6 6.7 %collective-permute-start.11 = (f32[8,768]{1,0:T(8,128)S(1)}, f32[8,768]{1,0:T(8,128)S(1)}, u32[]{:S(2)}, u32[]{:S(2)}) collective-permute-start(f32[8,768]{1,0:T(8,128)S(1)} %shard_map.87), channel_id=1, source_target_pairs={{0,32},{32,0},{1,33},{33,1},{2,34},{34,2},{3,35},{35,3},{4,36},{36... | collective-permute-start | bytes 73736 | tf_op jit(solution)/shard_map/ppermute | solution.py:195
  206.4 0.8 collective-permute-done.11
  207.1 0.6 maximum_select_fusion
  (73 shorter events, 1.5 us)
Async XLA Ops:
  0.6 1.7 copy-start
  0.6 5.6 %copy-start.1 = (bf16[768,768]{1,0:T(8,128)(2,1)S(1)}, bf16[768,768]{1,0:T(8,128)(2,1)}, u32[]{:S(2)}) copy-start(bf16[768,768]{1,0:T(8,128)(2,1)} %a_ref.8) | copy-start | bytes 3538948
  2.3 5.8 %copy-start.19 = (bf16[256,768]{1,0:T(8,128)(2,1)}, bf16[256,768]{1,0:T(8,128)(2,1)S(1)}, u32[]{:S(2)}) copy-start(bf16[256,768]{1,0:T(8,128)(2,1)S(1)} %get-tuple-element.50) | copy-start | bytes 1179652
  2.3 5.8 %copy-start.23 = (bf16[256,768]{1,0:T(8,128)(2,1)}, bf16[256,768]{1,0:T(8,128)(2,1)S(1)}, u32[]{:S(2)}) copy-start(bf16[256,768]{1,0:T(8,128)(2,1)S(1)} %get-tuple-element.49) | copy-start | bytes 1179652
  2.9 4.7 %collective-permute-start = (bf16[256,768]{1,0:T(8,128)(2,1)S(1)}, bf16[256,768]{1,0:T(8,128)(2,1)S(1)}, u32[]{:S(2)}, u32[]{:S(2)}) collective-permute-start(bf16[256,768]{1,0:T(8,128)(2,1)S(1)} %convolution_convert_fusion.2), channel_id=1, source_target_pairs={{0,32},{32,0},{1,33},{33,1},{2,34},{34,2},{3,35},{35,3},{4,36},{36... | collective-permute-start | bytes 1179656 | tf_op jit(solution)/shard_map/ppermute | solution.py:195
  6.2 20.9 %collective-permute-start.1 = (bf16[768,768]{1,0:T(8,128)(2,1)S(1)}, bf16[768,768]{1,0:T(8,128)(2,1)S(1)}, u32[]{:S(2)}, u32[]{:S(2)}) collective-permute-start(bf16[768,768]{1,0:T(8,128)(2,1)S(1)} %copy-done), channel_id=1, source_target_pairs={{0,32},{32,0},{1,33},{33,1},{2,34},{34,2},{3,35},{35,3},{4,36},{36... | collective-permute-start | bytes 3538952 | tf_op jit(solution)/shard_map/ppermute | solution.py:195
  6.3 20.8 %collective-permute-start.2 = (bf16[768,768]{1,0:T(8,128)(2,1)S(1)}, bf16[768,768]{1,0:T(8,128)(2,1)S(1)}, u32[]{:S(2)}, u32[]{:S(2)}) collective-permute-start(bf16[768,768]{1,0:T(8,128)(2,1)S(1)} %copy-done.1), channel_id=1, source_target_pairs={{0,32},{32,0},{1,33},{33,1},{2,34},{34,2},{3,35},{35,3},{4,36},{36... | collective-permute-start | bytes 3538952 | tf_op jit(solution)/shard_map/ppermute | solution.py:195
  18.2 10.6 %copy-start.17 = (bf16[64,768]{1,0:T(8,128)(2,1)}, bf16[64,768]{1,0:T(8,128)(2,1)S(1)}, u32[]{:S(2)}) copy-start(bf16[64,768]{1,0:T(8,128)(2,1)S(1)} %get-tuple-element.33.p_ref) | copy-start | bytes 294916
  27.1 1.7 copy-start.10
  27.1 1.7 copy-start.2
  28.8 26.9 %all-to-all-start.2 = ((bf16[32,8,1536]{2,1,0:T(8,128)(2,1)}), bf16[32,8,1536]{2,1,0:T(8,128)(2,1)}, u32[]{:S(2)}, u32[]{:S(2)}) async-start(bf16[32,8,1536]{2,1,0:T(8,128)(2,1)} %bitcast.60), calls=%async_computation.2 | async-start | bytes 1572864 | tf_op jit(solution)/shard_map/all_to_all | solution.py:204
  39.2 10.4 %collective-permute-start.6 = (bf16[256,768]{1,0:T(8,128)(2,1)}, bf16[256,768]{1,0:T(8,128)(2,1)}, u32[]{:S(2)}, u32[]{:S(2)}) collective-permute-start(bf16[256,768]{1,0:T(8,128)(2,1)} %copy-done.23), channel_id=1, source_target_pairs={{0,32},{32,0},{1,33},{33,1},{2,34},{34,2},{3,35},{35,3},{4,36},{36... | collective-permute-start | bytes 1179656 | tf_op jit(solution)/shard_map/ppermute | solution.py:195
  43.4 3.6 %collective-permute-start.4 = (f32[8,768]{1,0:T(8,128)S(1)}, f32[8,768]{1,0:T(8,128)S(1)}, u32[]{:S(2)}, u32[]{:S(2)}) collective-permute-start(f32[8,768]{1,0:T(8,128)S(1)} %get-tuple-element.46), channel_id=1, source_target_pairs={{0,32},{32,0},{1,33},{33,1},{2,34},{34,2},{3,35},{35,3},{4,36},{36... | collective-permute-start | bytes 73736 | tf_op jit(solution)/shard_map/ppermute | solution.py:195
  44.4 3.3 %collective-permute-start.5 = (f32[8,768]{1,0:T(8,128)S(1)}, f32[8,768]{1,0:T(8,128)S(1)}, u32[]{:S(2)}, u32[]{:S(2)}) collective-permute-start(f32[8,768]{1,0:T(8,128)S(1)} %get-tuple-element.62), channel_id=1, source_target_pairs={{0,32},{32,0},{1,33},{33,1},{2,34},{34,2},{3,35},{35,3},{4,36},{36... | collective-permute-start | bytes 73736 | tf_op jit(solution)/shard_map/ppermute | solution.py:195
  46.4 3.2 %copy-start.21 = (bf16[256,768]{1,0:T(8,128)(2,1)}, bf16[256,768]{1,0:T(8,128)(2,1)S(1)}, u32[]{:S(2)}) copy-start(bf16[256,768]{1,0:T(8,128)(2,1)S(1)} %get-tuple-element.48) | copy-start | bytes 1179652
  46.4 1.9 collective-permute-start.3
  48.3 1.3 copy-start.24
  55.7 0.8 copy-start.14
  56.5 26.3 %copy-start.3 = (bf16[768,768]{1,0:T(8,128)(2,1)S(1)}, bf16[768,768]{1,0:T(8,128)(2,1)}, u32[]{:S(2)}) copy-start(bf16[768,768]{1,0:T(8,128)(2,1)} %copy-done.2) | copy-start | bytes 3538948
  56.5 26.3 %copy-start.12 = (bf16[256,768]{1,0:T(8,128)(2,1)S(1)}, bf16[256,768]{1,0:T(8,128)(2,1)}, u32[]{:S(2)}) copy-start(bf16[256,768]{1,0:T(8,128)(2,1)} %fusion.refs_0_) | copy-start | bytes 1179652
  82.8 0.9 copy-start.6
  107.1 0.9 copy-start.8
  108.1 21.5 %copy-start.13 = (f32[8,1536]{1,0:T(8,128)S(1)}, f32[8,1536]{1,0:T(8,128)}, u32[]{:S(2)}) copy-start(f32[8,1536]{1,0:T(8,128)} %pad_maximum_fusion.7.a_ref) | copy-start | bytes 147460
  129.7 21.9 %copy-start.15 = (f32[8,1536]{1,0:T(8,128)}, f32[8,1536]{1,0:T(8,128)S(1)}, u32[]{:S(2)}) copy-start(f32[8,1536]{1,0:T(8,128)S(1)} %get-tuple-element.42.a_ref) | copy-start | bytes 147460
  151.6 0.9 copy-start.4
  151.6 9.5 %copy-start.18 = (bf16[64,768]{1,0:T(8,128)(2,1)S(1)}, bf16[64,768]{1,0:T(8,128)(2,1)}, u32[]{:S(2)}) copy-start(bf16[64,768]{1,0:T(8,128)(2,1)} %copy-done.17) | copy-start | bytes 294916
  173.3 6.4 %copy-start.7 = (bf16[32,8,1536]{2,1,0:T(8,128)(2,1)S(1)}, bf16[32,8,1536]{2,1,0:T(8,128)(2,1)}, u32[]{:S(2)}) copy-start(bf16[32,8,1536]{2,1,0:T(8,128)(2,1)} %copy-done.6) | copy-start | bytes 2359300
  173.3 6.4 %copy-start.5 = (bf16[32,8,1536]{2,1,0:T(8,128)(2,1)S(1)}, bf16[32,8,1536]{2,1,0:T(8,128)(2,1)}, u32[]{:S(2)}) copy-start(bf16[32,8,1536]{2,1,0:T(8,128)(2,1)} %copy-done.4) | copy-start | bytes 2359300
  173.4 6.4 %copy-start.9 = (bf16[4,64,1536]{2,1,0:T(8,128)(2,1)S(1)}, bf16[4,64,1536]{2,1,0:T(8,128)(2,1)}, u32[]{:S(2)}) copy-start(bf16[4,64,1536]{2,1,0:T(8,128)(2,1)} %copy-done.8) | copy-start | bytes 2359300
  173.4 26.2 %all-to-all-start.10 = ((bf16[32,8,1536]{2,1,0:T(8,128)(2,1)}), bf16[32,8,1536]{2,1,0:T(8,128)(2,1)S(1)}, u32[]{:S(2)}, u32[]{:S(2)}) async-start(bf16[32,8,1536]{2,1,0:T(8,128)(2,1)} %bitcast.61), calls=%async_computation.10 | async-start | bytes 1572864 | tf_op jit(solution)/shard_map/all_to_all | solution.py:204
  181.7 10.9 %copy-start.11 = (bf16[4,64,768]{2,1,0:T(8,128)(2,1)S(1)}, bf16[4,64,768]{2,1,0:T(8,128)(2,1)}, u32[]{:S(2)}) copy-start(bf16[4,64,768]{2,1,0:T(8,128)(2,1)} %copy-done.10) | copy-start | bytes 1179652
  181.7 10.9 %copy-start.25 = (bf16[256,768]{1,0:T(8,128)(2,1)S(1)}, bf16[256,768]{1,0:T(8,128)(2,1)}, u32[]{:S(2)}) copy-start(bf16[256,768]{1,0:T(8,128)(2,1)} %copy-done.24) | copy-start | bytes 1179652
  181.8 12.8 %collective-permute-start.7 = (bf16[384,768]{1,0:T(8,128)(2,1)S(1)}, bf16[384,768]{1,0:T(8,128)(2,1)S(1)}, u32[]{:S(2)}, u32[]{:S(2)}) collective-permute-start(bf16[384,768]{1,0:T(8,128)(2,1)S(1)} %get-tuple-element.53), channel_id=1, source_target_pairs={{0,32},{32,0},{1,33},{33,1},{2,34},{34,2},{3,35},{35,3},{4,36},{36... | collective-permute-start | bytes 1769480 | tf_op jit(solution)/shard_map/ppermute | solution.py:195
  192.6 2.5 %collective-permute-start.8 = (bf16[384,768]{1,0:T(8,128)(2,1)S(1)}, bf16[384,768]{1,0:T(8,128)(2,1)S(1)}, u32[]{:S(2)}, u32[]{:S(2)}) collective-permute-start(bf16[384,768]{1,0:T(8,128)(2,1)S(1)} %get-tuple-element.54), channel_id=1, source_target_pairs={{0,32},{32,0},{1,33},{33,1},{2,34},{34,2},{3,35},{35,3},{4,36},{36... | collective-permute-start | bytes 1769480 | tf_op jit(solution)/shard_map/ppermute | solution.py:195
  193.5 1.6 copy-start.20
  193.6 3.7 %collective-permute-start.9 = (bf16[384,768]{1,0:T(8,128)(2,1)S(1)}, bf16[384,768]{1,0:T(8,128)(2,1)S(1)}, u32[]{:S(2)}, u32[]{:S(2)}) collective-permute-start(bf16[384,768]{1,0:T(8,128)(2,1)S(1)} %get-tuple-element.51), channel_id=1, source_target_pairs={{0,32},{32,0},{1,33},{33,1},{2,34},{34,2},{3,35},{35,3},{4,36},{36... | collective-permute-start | bytes 1769480 | tf_op jit(solution)/shard_map/ppermute | solution.py:195
  194.5 2.8 %collective-permute-start.10 = (bf16[384,768]{1,0:T(8,128)(2,1)S(1)}, bf16[384,768]{1,0:T(8,128)(2,1)S(1)}, u32[]{:S(2)}, u32[]{:S(2)}) collective-permute-start(bf16[384,768]{1,0:T(8,128)(2,1)S(1)} %get-tuple-element.52), channel_id=1, source_target_pairs={{0,32},{32,0},{1,33},{33,1},{2,34},{34,2},{3,35},{35,3},{4,36},{36... | collective-permute-start | bytes 1769480 | tf_op jit(solution)/shard_map/ppermute | solution.py:195
  195.0 2.2 %copy-start.22 = (bf16[256,768]{1,0:T(8,128)(2,1)S(1)}, bf16[256,768]{1,0:T(8,128)(2,1)}, u32[]{:S(2)}) copy-start(bf16[256,768]{1,0:T(8,128)(2,1)} %copy-done.21) | copy-start | bytes 1179652
  197.3 2.2 %copy-start.16 = (f32[8,1536]{1,0:T(8,128)S(1)}, f32[8,1536]{1,0:T(8,128)}, u32[]{:S(2)}) copy-start(f32[8,1536]{1,0:T(8,128)} %copy-done.15) | copy-start | bytes 147460
  199.6 7.5 %collective-permute-start.11 = (f32[8,768]{1,0:T(8,128)S(1)}, f32[8,768]{1,0:T(8,128)S(1)}, u32[]{:S(2)}, u32[]{:S(2)}) collective-permute-start(f32[8,768]{1,0:T(8,128)S(1)} %shard_map.87), channel_id=1, source_target_pairs={{0,32},{32,0},{1,33},{33,1},{2,34},{34,2},{3,35},{35,3},{4,36},{36... | collective-permute-start | bytes 73736 | tf_op jit(solution)/shard_map/ppermute | solution.py:195
